TPU v7x, 128 devices: a whole 4x4x4 slice. The times are simulated.
128 devices in a mesh: rows: 8 (over x_hi, y), cols: 16 (over x_lo, z, core).
Axes of the slice: x: 4 (x_hi: 2, x_lo: 2; x = x_hi * 2 + x_lo), y: 4, z: 4, core: 2. Of those that a mesh axis runs over, the one named last changes fastest.
Arguments:
- features: bfloat16 [3072, 4096, 32], P('rows', 'cols'), may hold values from -6 to 6
- conv_weight: bfloat16 [3, 3, 32, 128], replicated, may hold values from -0.375 to 0.375
- conv_bias: float32 [128], replicated, may hold values from -3 to 3
- head_weight: bfloat16 [128, 33], replicated, may hold values from -0.5 to 0.5
- head_bias: float32 [33], replicated, may hold values from -4 to 4
- tissue: int32 [8, 16], P('rows', 'cols'), may hold values 0 or 1
Outputs:
- probability: float32 [2048, 2048], P('rows', 'cols')
- ray_lengths: float32 [2048, 65536], P('rows', 'cols')
- peak_gap: float32 [2048, 2048], P('rows', 'cols')
All inputs are finite; a program needn't handle non-finite values. No bound on the sum of `tissue` on one device may be relied on, other than what follows from the above.
Results may differ from a plain program's by a relative error of at most 0.0023.
Values may be sent and summed in bfloat16 or wider, within the bound.
No kernel may reach another device: no remote copies, remote signals or barrier semaphores. Data moves between devices by JAX's collectives and lax.ppermute only.
A program may use at most 192 MiB of HBM per device.

v0:
```python
import math

import jax
import jax.numpy as jnp
from jax import lax
from jax.sharding import PartitionSpec as P

MARGIN = 64


def padded_2(block, sides, width):
    for axis, dim in sides:
        count = lax.axis_size(axis)
        forward = [(i, i + 1) for i in range(count - 1)]
        backward = [(target, source) for source, target in forward]
        low = lax.ppermute(
            lax.slice_in_dim(block, block.shape[dim] - width, None, axis=dim), axis, forward
        )
        high = lax.ppermute(lax.slice_in_dim(block, 0, width, axis=dim), axis, backward)
        block = jnp.concatenate([low, block, high], axis=dim)
    return block


def local_gauss(extent):
    spread = jnp.float32(extent) / 4.0
    centred = jnp.arange(extent, dtype=jnp.int32).astype(jnp.float32) - (extent - 1) / 2.0
    return jnp.exp(-(centred * centred) / (2.0 * spread * spread))


def blend_total(positions, number, core_len, margin, extent):
    tile_ids = jnp.arange(number, dtype=jnp.int32)
    offsets = positions[None, :] - (tile_ids[:, None] * core_len - margin)
    covered = (offsets >= 0) & (offsets < extent)
    spread = jnp.float32(extent) / 4.0
    centred = offsets.astype(jnp.float32) - (extent - 1) / 2.0
    values = jnp.exp(-(centred * centred) / (2.0 * spread * spread))
    return jnp.sum(jnp.where(covered, values, jnp.float32(0.0)), axis=0)


def fold_margins(own_tile, padded, axis_dim, margin):
    extent = own_tile.shape[axis_dim]
    inner_len = extent - 2 * margin
    own_part = lax.slice_in_dim(own_tile, margin, margin + inner_len, axis=axis_dim)
    above_part = lax.slice_in_dim(padded, 0, margin, axis=axis_dim)
    below_part = lax.slice_in_dim(padded, extent + margin, extent + 2 * margin, axis=axis_dim)
    filler_shape = list(own_part.shape)
    filler_shape[axis_dim] = inner_len - margin
    filler = jnp.zeros(filler_shape, jnp.float32)
    return (
        own_part
        + jnp.concatenate([above_part, filler], axis=axis_dim)
        + jnp.concatenate([filler, below_part], axis=axis_dim)
    )


def weighted_patch(slab, row_weight, col_weight, conv_weight, conv_bias, head_weight, head_bias):
    out_rows = slab.shape[0] - 2
    out_cols = slab.shape[1] - 2
    in_count = slab.shape[2]
    block_rows = math.gcd(out_rows, 64)
    taps = conv_weight.reshape(3, 3 * in_count, conv_weight.shape[3])

    def one_block(block_id, result):
        row_start = block_id * block_rows
        piece = lax.dynamic_slice_in_dim(slab, row_start, block_rows + 2, 0)
        stacked = jnp.concatenate(
            [piece[:, 0:out_cols], piece[:, 1 : out_cols + 1], piece[:, 2 : out_cols + 2]], axis=2
        )
        summed = jnp.dot(
            stacked[0:block_rows].reshape(-1, 3 * in_count),
            taps[0],
            preferred_element_type=jnp.float32,
        )
        summed = summed + jnp.dot(
            stacked[1 : block_rows + 1].reshape(-1, 3 * in_count),
            taps[1],
            preferred_element_type=jnp.float32,
        )
        summed = summed + jnp.dot(
            stacked[2 : block_rows + 2].reshape(-1, 3 * in_count),
            taps[2],
            preferred_element_type=jnp.float32,
        )
        hidden = jnp.maximum(summed + conv_bias, 0.0).astype(jnp.bfloat16)
        logits = (
            lax.dot_general(
                head_weight, hidden, (((0,), (1,)), ((), ())), preferred_element_type=jnp.float32
            )
            + head_bias[:, None]
        )
        outputs = jnp.concatenate([jax.nn.sigmoid(logits[:1]), logits[1:]], axis=0).reshape(
            -1, block_rows, out_cols
        )
        weights = (
            lax.dynamic_slice_in_dim(row_weight, row_start, block_rows)[:, None]
            * col_weight[None, :]
        )
        return lax.dynamic_update_slice_in_dim(result, outputs * weights[None], row_start, 1)

    initial = jnp.zeros((head_weight.shape[1], out_rows, out_cols), jnp.float32)
    return lax.fori_loop(0, out_rows // block_rows, one_block, initial)


def body(features, conv_weight, conv_bias, head_weight, head_bias, tissue):
    ext_rows, ext_cols, in_count = features.shape
    core_rows = ext_rows - 2 * MARGIN
    core_cols = ext_cols - 2 * MARGIN
    out_count = head_weight.shape[1]
    row_weight = local_gauss(ext_rows)
    col_weight = local_gauss(ext_cols)

    def run_tile(window):
        padded_input = jnp.pad(window, ((1, 1), (1, 1), (0, 0)))
        return weighted_patch(
            padded_input, row_weight, col_weight, conv_weight, conv_bias, head_weight, head_bias
        )

    def skip_tile(window):
        return jnp.zeros((out_count, ext_rows, ext_cols), jnp.float32)

    weighted = lax.cond(tissue[0, 0] > 0, run_tile, skip_tile, features)
    taller = padded_2(weighted, (("rows", 1),), MARGIN)
    half_folded = fold_margins(weighted, taller, 1, MARGIN)
    wider = padded_2(half_folded, (("cols", 2),), MARGIN)
    numerator = fold_margins(half_folded, wider, 2, MARGIN)
    row_ids = lax.axis_index("rows") * core_rows + jnp.arange(core_rows, dtype=jnp.int32)
    col_ids = lax.axis_index("cols") * core_cols + jnp.arange(core_cols, dtype=jnp.int32)
    row_total = blend_total(row_ids, lax.axis_size("rows"), core_rows, MARGIN, ext_rows)
    col_total = blend_total(col_ids, lax.axis_size("cols"), core_cols, MARGIN, ext_cols)
    blended = numerator / (row_total[:, None] * col_total[None, :])[None]
    probability = blended[0]
    ray_lengths = jnp.transpose(blended[1:], (1, 2, 0)).reshape(
        core_rows, core_cols * (out_count - 1)
    )
    rimmed = padded_2(probability, (("rows", 0), ("cols", 1)), 2)
    window_max = lax.reduce_window(rimmed, -jnp.inf, lax.max, (5, 5), (1, 1), "VALID")
    return (probability, ray_lengths, window_max - probability)


def solution(mesh):
    in_specs = (P("rows", "cols", None), P(), P(), P(), P(), P("rows", "cols"))
    out_specs = (P("rows", "cols"), P("rows", "cols"), P("rows", "cols"))
    return jax.shard_map(body, mesh=mesh, in_specs=in_specs, out_specs=out_specs, check_vma=False)
```

profile of v0, /device:TPU:6, one launch (start us, length us, event | category | flops | bytes accessed | tf_op | source)
XLA Modules:
  0.0 428.0 jit_solution(16418578751772978632)
XLA Ops:
  1.3 267.1 %conditional.1 = (f32[33,384,256]{2,1,0:T(8,128)}) conditional(s32[]{:T(128)} %bitcast.8, () %tuple.28, (bf16[384,256,32]{1,2,0:T(8,128)(2,1)}, bf16[3,3,32,128]{3,2,1,0:T(8,128)(2,1)}, f32[128]{0:T(128)}, bf16[128,33]{0,1:T(8,128)(2,1)}, f32[33]{0:T(128)}, /*index=5*/f32[384]{0:T(512)S(1)}, f32[256]{0:T(256)S(1)}, f32[]{:T(128)}, f32[]{:T(128)}, ...), branch_computations={%region_0.0_spmd, %region_1.4_spmd} | conditional | flops 1368279552 | bytes 136139296 | solution.py:121
  1.3 19.3 %copy.36 = bf16[384,256,32]{2,1,0:T(8,128)(2,1)} copy(bf16[384,256,32]{1,2,0:T(8,128)(2,1)} %get-tuple-element.248) | data formatting | bytes 12582912 | tf_op jit(solution)/shard_map
  20.6 17.6 %pad.7 = bf16[386,258,32]{2,1,0:T(8,128)(2,1)} pad(bf16[384,256,32]{2,1,0:T(8,128)(2,1)} %copy.36, bf16[]{:T(256)} %constant.93.clone), padding=1_1x1_1x0_0 | pad | bytes 12665090 | tf_op jit(solution)/shard_map/cond/branch_1_fun/jit(_pad)/pad | solution.py:113
  38.4 6.2 %broadcast.114 = f32[33,384,256]{2,1,0:T(8,128)} broadcast(f32[]{:T(128)} %constant.92.clone), dimensions={} | broadcast | bytes 12976132 | tf_op jit(solution)/shard_map/broadcast.11
  44.6 223.9 %while.12 = (s32[]{:T(128)}, f32[33,384,256]{2,1,0:T(8,128)}, bf16[386,258,32]{2,1,0:T(8,128)(2,1)}, bf16[3,96,128]{2,1,0:T(8,128)(2,1)S(1)}, f32[128]{0:T(128)S...) while((s32[]{:T(128)}, f32[33,384,256]{2,1,0:T(8,128)}, ...), condition=%wide.region_3.3_spmd, body=%wide.region_2.2_spmd.sunk | while | flops 1368276992 | bytes 97561608 | solution.py:101
  44.8 11.4 %constant_dynamic-slice_fusion.4 = (bf16[66,256,32]{2,1,0:T(8,128)(2,1)}, bf16[66,256,32]{2,1,0:T(8,128)(2,1)}, bf16[66,256,32]{2,1,0:T(8,128)(2,1)}) fusion(bf16[386,258,32]{2,1,0:T(8,128)(2,1)} %get-tuple-element.395, s32[]{:T(128)S(6)} %select_n.34, s32[]{:T(128)S(6)} %add.226, s32[]{:T(128)S(6)} %add.227), kind=kLoop, calls=%fused_computation.24.clone.1 | loop fusion | bytes 6488076 | tf_op jit(solution)/shard_map/cond/branch_1_fun/while/body/eval_jaxpr/slice | solution.py:67
  56.2 6.9 %pad_maximum_fusion.8 = bf16[66,256,96]{2,1,0:T(8,128)(2,1)S(1)} fusion(bf16[66,256,32]{2,1,0:T(8,128)(2,1)} %get-tuple-element.355, bf16[66,256,32]{2,1,0:T(8,128)(2,1)} %get-tuple-element.356, bf16[66,256,32]{2,1,0:T(8,128)(2,1)} %get-tuple-element.357), kind=kLoop, calls=%fused_computation.7.clone.1 | loop fusion | flops 9732096 | bytes 6488064 | tf_op jit(solution)/shard_map/cond/branch_1_fun/while/body/eval_jaxpr/concatenate | solution.py:66
  71.8 7.1 %fusion.72 = f32[33,16384]{1,0:T(8,128)S(1)} fusion(bf16[128,33]{1,0:T(8,128)(2,1)S(1)} %get-tuple-element.398, f32[16384,128]{1,0:T(8,128)} %convolution_add_fusion.4, bf16[16384,96]{1,0:T(8,128)(2,1)} %bitcast.63, f32[128]{0:T(128)S(1)} %get-tuple-element.397, f32[33]{0:T(128)S(1)} %get-tuple-element.399, ...), kind=kOutput, calls=%fused_computation.6.clone.1 | convolution fusion | flops 549994496 | bytes 13755392 | tf_op jit(solution)/shard_map/cond/branch_1_fun/while/body/eval_jaxpr/dot_general | solution.py:86
  82.1 11.5 %constant_dynamic-slice_fusion.4 = (bf16[66,256,32]{2,1,0:T(8,128)(2,1)}, bf16[66,256,32]{2,1,0:T(8,128)(2,1)}, bf16[66,256,32]{2,1,0:T(8,128)(2,1)}) fusion(bf16[386,258,32]{2,1,0:T(8,128)(2,1)} %get-tuple-element.395, s32[]{:T(128)S(6)} %select_n.34, s32[]{:T(128)S(6)} %add.226, s32[]{:T(128)S(6)} %add.227), kind=kLoop, calls=%fused_computation.24.clone.1 | loop fusion | bytes 6488076 | tf_op jit(solution)/shard_map/cond/branch_1_fun/while/body/eval_jaxpr/slice | solution.py:67
  93.5 6.9 %pad_maximum_fusion.8 = bf16[66,256,96]{2,1,0:T(8,128)(2,1)S(1)} fusion(bf16[66,256,32]{2,1,0:T(8,128)(2,1)} %get-tuple-element.355, bf16[66,256,32]{2,1,0:T(8,128)(2,1)} %get-tuple-element.356, bf16[66,256,32]{2,1,0:T(8,128)(2,1)} %get-tuple-element.357), kind=kLoop, calls=%fused_computation.7.clone.1 | loop fusion | flops 9732096 | bytes 6488064 | tf_op jit(solution)/shard_map/cond/branch_1_fun/while/body/eval_jaxpr/concatenate | solution.py:66
  109.2 7.1 %fusion.72 = f32[33,16384]{1,0:T(8,128)S(1)} fusion(bf16[128,33]{1,0:T(8,128)(2,1)S(1)} %get-tuple-element.398, f32[16384,128]{1,0:T(8,128)} %convolution_add_fusion.4, bf16[16384,96]{1,0:T(8,128)(2,1)} %bitcast.63, f32[128]{0:T(128)S(1)} %get-tuple-element.397, f32[33]{0:T(128)S(1)} %get-tuple-element.399, ...), kind=kOutput, calls=%fused_computation.6.clone.1 | convolution fusion | flops 549994496 | bytes 13755392 | tf_op jit(solution)/shard_map/cond/branch_1_fun/while/body/eval_jaxpr/dot_general | solution.py:86
  119.4 11.4 %constant_dynamic-slice_fusion.4 = (bf16[66,256,32]{2,1,0:T(8,128)(2,1)}, bf16[66,256,32]{2,1,0:T(8,128)(2,1)}, bf16[66,256,32]{2,1,0:T(8,128)(2,1)}) fusion(bf16[386,258,32]{2,1,0:T(8,128)(2,1)} %get-tuple-element.395, s32[]{:T(128)S(6)} %select_n.34, s32[]{:T(128)S(6)} %add.226, s32[]{:T(128)S(6)} %add.227), kind=kLoop, calls=%fused_computation.24.clone.1 | loop fusion | bytes 6488076 | tf_op jit(solution)/shard_map/cond/branch_1_fun/while/body/eval_jaxpr/slice | solution.py:67
  130.8 6.9 %pad_maximum_fusion.8 = bf16[66,256,96]{2,1,0:T(8,128)(2,1)S(1)} fusion(bf16[66,256,32]{2,1,0:T(8,128)(2,1)} %get-tuple-element.355, bf16[66,256,32]{2,1,0:T(8,128)(2,1)} %get-tuple-element.356, bf16[66,256,32]{2,1,0:T(8,128)(2,1)} %get-tuple-element.357), kind=kLoop, calls=%fused_computation.7.clone.1 | loop fusion | flops 9732096 | bytes 6488064 | tf_op jit(solution)/shard_map/cond/branch_1_fun/while/body/eval_jaxpr/concatenate | solution.py:66
  146.4 7.1 %fusion.72 = f32[33,16384]{1,0:T(8,128)S(1)} fusion(bf16[128,33]{1,0:T(8,128)(2,1)S(1)} %get-tuple-element.398, f32[16384,128]{1,0:T(8,128)} %convolution_add_fusion.4, bf16[16384,96]{1,0:T(8,128)(2,1)} %bitcast.63, f32[128]{0:T(128)S(1)} %get-tuple-element.397, f32[33]{0:T(128)S(1)} %get-tuple-element.399, ...), kind=kOutput, calls=%fused_computation.6.clone.1 | convolution fusion | flops 549994496 | bytes 13755392 | tf_op jit(solution)/shard_map/cond/branch_1_fun/while/body/eval_jaxpr/dot_general | solution.py:86
  156.6 11.4 %constant_dynamic-slice_fusion.4 = (bf16[66,256,32]{2,1,0:T(8,128)(2,1)}, bf16[66,256,32]{2,1,0:T(8,128)(2,1)}, bf16[66,256,32]{2,1,0:T(8,128)(2,1)}) fusion(bf16[386,258,32]{2,1,0:T(8,128)(2,1)} %get-tuple-element.395, s32[]{:T(128)S(6)} %select_n.34, s32[]{:T(128)S(6)} %add.226, s32[]{:T(128)S(6)} %add.227), kind=kLoop, calls=%fused_computation.24.clone.1 | loop fusion | bytes 6488076 | tf_op jit(solution)/shard_map/cond/branch_1_fun/while/body/eval_jaxpr/slice | solution.py:67
  168.1 6.9 %pad_maximum_fusion.8 = bf16[66,256,96]{2,1,0:T(8,128)(2,1)S(1)} fusion(bf16[66,256,32]{2,1,0:T(8,128)(2,1)} %get-tuple-element.355, bf16[66,256,32]{2,1,0:T(8,128)(2,1)} %get-tuple-element.356, bf16[66,256,32]{2,1,0:T(8,128)(2,1)} %get-tuple-element.357), kind=kLoop, calls=%fused_computation.7.clone.1 | loop fusion | flops 9732096 | bytes 6488064 | tf_op jit(solution)/shard_map/cond/branch_1_fun/while/body/eval_jaxpr/concatenate | solution.py:66
  183.7 7.1 %fusion.72 = f32[33,16384]{1,0:T(8,128)S(1)} fusion(bf16[128,33]{1,0:T(8,128)(2,1)S(1)} %get-tuple-element.398, f32[16384,128]{1,0:T(8,128)} %convolution_add_fusion.4, bf16[16384,96]{1,0:T(8,128)(2,1)} %bitcast.63, f32[128]{0:T(128)S(1)} %get-tuple-element.397, f32[33]{0:T(128)S(1)} %get-tuple-element.399, ...), kind=kOutput, calls=%fused_computation.6.clone.1 | convolution fusion | flops 549994496 | bytes 13755392 | tf_op jit(solution)/shard_map/cond/branch_1_fun/while/body/eval_jaxpr/dot_general | solution.py:86
  193.9 11.4 %constant_dynamic-slice_fusion.4 = (bf16[66,256,32]{2,1,0:T(8,128)(2,1)}, bf16[66,256,32]{2,1,0:T(8,128)(2,1)}, bf16[66,256,32]{2,1,0:T(8,128)(2,1)}) fusion(bf16[386,258,32]{2,1,0:T(8,128)(2,1)} %get-tuple-element.395, s32[]{:T(128)S(6)} %select_n.34, s32[]{:T(128)S(6)} %add.226, s32[]{:T(128)S(6)} %add.227), kind=kLoop, calls=%fused_computation.24.clone.1 | loop fusion | bytes 6488076 | tf_op jit(solution)/shard_map/cond/branch_1_fun/while/body/eval_jaxpr/slice | solution.py:67
  205.3 6.9 %pad_maximum_fusion.8 = bf16[66,256,96]{2,1,0:T(8,128)(2,1)S(1)} fusion(bf16[66,256,32]{2,1,0:T(8,128)(2,1)} %get-tuple-element.355, bf16[66,256,32]{2,1,0:T(8,128)(2,1)} %get-tuple-element.356, bf16[66,256,32]{2,1,0:T(8,128)(2,1)} %get-tuple-element.357), kind=kLoop, calls=%fused_computation.7.clone.1 | loop fusion | flops 9732096 | bytes 6488064 | tf_op jit(solution)/shard_map/cond/branch_1_fun/while/body/eval_jaxpr/concatenate | solution.py:66
  220.9 7.1 %fusion.72 = f32[33,16384]{1,0:T(8,128)S(1)} fusion(bf16[128,33]{1,0:T(8,128)(2,1)S(1)} %get-tuple-element.398, f32[16384,128]{1,0:T(8,128)} %convolution_add_fusion.4, bf16[16384,96]{1,0:T(8,128)(2,1)} %bitcast.63, f32[128]{0:T(128)S(1)} %get-tuple-element.397, f32[33]{0:T(128)S(1)} %get-tuple-element.399, ...), kind=kOutput, calls=%fused_computation.6.clone.1 | convolution fusion | flops 549994496 | bytes 13755392 | tf_op jit(solution)/shard_map/cond/branch_1_fun/while/body/eval_jaxpr/dot_general | solution.py:86
  231.1 11.5 %constant_dynamic-slice_fusion.4 = (bf16[66,256,32]{2,1,0:T(8,128)(2,1)}, bf16[66,256,32]{2,1,0:T(8,128)(2,1)}, bf16[66,256,32]{2,1,0:T(8,128)(2,1)}) fusion(bf16[386,258,32]{2,1,0:T(8,128)(2,1)} %get-tuple-element.395, s32[]{:T(128)S(6)} %select_n.34, s32[]{:T(128)S(6)} %add.226, s32[]{:T(128)S(6)} %add.227), kind=kLoop, calls=%fused_computation.24.clone.1 | loop fusion | bytes 6488076 | tf_op jit(solution)/shard_map/cond/branch_1_fun/while/body/eval_jaxpr/slice | solution.py:67
  242.6 6.9 %pad_maximum_fusion.8 = bf16[66,256,96]{2,1,0:T(8,128)(2,1)S(1)} fusion(bf16[66,256,32]{2,1,0:T(8,128)(2,1)} %get-tuple-element.355, bf16[66,256,32]{2,1,0:T(8,128)(2,1)} %get-tuple-element.356, bf16[66,256,32]{2,1,0:T(8,128)(2,1)} %get-tuple-element.357), kind=kLoop, calls=%fused_computation.7.clone.1 | loop fusion | flops 9732096 | bytes 6488064 | tf_op jit(solution)/shard_map/cond/branch_1_fun/while/body/eval_jaxpr/concatenate | solution.py:66
  258.2 7.1 %fusion.72 = f32[33,16384]{1,0:T(8,128)S(1)} fusion(bf16[128,33]{1,0:T(8,128)(2,1)S(1)} %get-tuple-element.398, f32[16384,128]{1,0:T(8,128)} %convolution_add_fusion.4, bf16[16384,96]{1,0:T(8,128)(2,1)} %bitcast.63, f32[128]{0:T(128)S(1)} %get-tuple-element.397, f32[33]{0:T(128)S(1)} %get-tuple-element.399, ...), kind=kOutput, calls=%fused_computation.6.clone.1 | convolution fusion | flops 549994496 | bytes 13755392 | tf_op jit(solution)/shard_map/cond/branch_1_fun/while/body/eval_jaxpr/dot_general | solution.py:86
  276.8 6.0 %collective-permute-start.1 = (f32[33,64,256]{2,1,0:T(8,128)}, f32[33,64,256]{2,1,0:T(8,128)S(1)}, u32[]{:S(2)}, u32[]{:S(2)}) collective-permute-start(f32[33,64,256]{2,1,0:T(8,128)} %get-tuple-element.287), channel_id=1, source_target_pairs={{16,0},{32,16},{48,32},{64,48},{80,64},{96,80},{112,96},{17,1},{33... | collective-permute-start | bytes 6488072 | tf_op jit(solution)/shard_map/ppermute | solution.py:19
  282.7 7.8 %slice.140 = f32[33,256,256]{2,1,0:T(8,128)} slice(f32[33,384,256]{2,1,0:T(8,128)} %get-tuple-element.409), slice={[0:33], [64:320], [0:256]} | slice | bytes 17301504 | tf_op jit(solution)/shard_map/slice | solution.py:43
  290.5 10.4 %copy.49 = f32[33,256,256]{1,0,2:T(8,128)} copy(f32[33,256,256]{2,1,0:T(8,128)} %slice.140) | data formatting | bytes 17301504
  300.9 26.9 %collective-permute-done = f32[33,64,256]{2,1,0:T(8,128)} collective-permute-done((f32[33,64,256]{2,1,0:T(8,128)}, f32[33,64,256]{2,1,0:T(8,128)}, u32[]{:S(2)}, u32[]{:S(2)}) %collective-permute-start) | collective-permute-done | bytes 2162720 | tf_op jit(solution)/shard_map/ppermute | solution.py:16
  327.9 5.9 %copy.39 = f32[33,64,256]{1,0,2:T(8,128)} copy(f32[33,64,256]{2,1,0:T(8,128)} %collective-permute-done) | data formatting | bytes 4325376 | tf_op jit(solution)/shard_map/ppermute | solution.py:16
  338.7 12.8 %pad_add_fusion = f32[33,256,256]{1,0,2:T(8,128)} fusion(f32[33,64,256]{1,0,2:T(8,128)} %copy.40, f32[33,256,256]{1,0,2:T(8,128)} %copy.49, f32[33,64,256]{1,0,2:T(8,128)} %copy.39), kind=kLoop, calls=%fused_computation.35 | loop fusion | flops 4325376 | bytes 21626880 | tf_op jit(solution)/shard_map/add | solution.py:50
  365.1 20.2 %collective-permute-done.2 = f32[33,256,64]{1,2,0:T(8,128)} collective-permute-done((f32[33,256,64]{1,2,0:T(8,128)S(1)}, f32[33,256,64]{1,2,0:T(8,128)}, u32[]{:S(2)}, u32[]{:S(2)}) %collective-permute-start.2) | collective-permute-done | bytes 2162720 | tf_op jit(solution)/shard_map/ppermute | solution.py:16
  397.4 7.5 %collective-permute-start.5 = (f32[2,128]{0,1:T(8,128)S(1)}, f32[2,128]{0,1:T(8,128)S(1)}, u32[]{:S(2)}, u32[]{:S(2)}) collective-permute-start(f32[2,128]{0,1:T(8,128)S(1)} %bitcast.71), channel_id=1, source_target_pairs={{16,0},{32,16},{48,32},{64,48},{80,64},{96,80},{112,96},{17,1},{33... | collective-permute-start | bytes 3080 | tf_op jit(solution)/shard_map/ppermute | solution.py:19
  408.8 5.8 %collective-permute-start.7 = (f32[260,2]{0,1:T(2,128)S(1)}, f32[260,2]{0,1:T(2,128)S(1)}, u32[]{:S(2)}, u32[]{:S(2)}) collective-permute-start(f32[260,2]{0,1:T(2,128)S(1)} %get-tuple-element.293), channel_id=1, source_target_pairs={{1,0},{2,1},{3,2},{4,3},{5,4},{6,5},{7,6},{8,7},{9,8},{10,9},{11,1... | collective-permute-start | bytes 6248 | tf_op jit(solution)/shard_map/ppermute | solution.py:19
  (112 shorter events, 126.9 us)
Async XLA Ops:
  20.6 17.6 %copy-start.4 = (bf16[128,33]{0,1:T(8,128)(2,1)S(1)}, bf16[128,33]{0,1:T(8,128)(2,1)}, u32[]{:S(2)}) copy-start(bf16[128,33]{0,1:T(8,128)(2,1)} %get-tuple-element.251) | copy-start | bytes 25348 | tf_op jit(solution)/shard_map/cond
  38.3 6.2 %copy-start.1 = (bf16[3,3,32,128]{3,2,1,0:T(8,128)(2,1)S(1)}, bf16[3,3,32,128]{3,2,1,0:T(8,128)(2,1)}, u32[]{:S(2)}) copy-start(bf16[3,3,32,128]{3,2,1,0:T(8,128)(2,1)} %get-tuple-element.189) | copy-start | bytes 221188 | tf_op jit(solution)/shard_map/cond
  38.4 6.2 %copy-start.2 = (f32[128]{0:T(128)S(1)}, f32[128]{0:T(128)}, u32[]{:S(2)}) copy-start(f32[128]{0:T(128)} %get-tuple-element.365) | copy-start | bytes 1540 | tf_op jit(solution)/shard_map/cond
  38.4 6.2 %copy-start.3 = (f32[33]{0:T(128)S(1)}, f32[33]{0:T(128)}, u32[]{:S(2)}) copy-start(f32[33]{0:T(128)} %get-tuple-element.367) | copy-start | bytes 400 | tf_op jit(solution)/shard_map/cond
  273.3 54.6 %collective-permute-start = (f32[33,64,256]{2,1,0:T(8,128)}, f32[33,64,256]{2,1,0:T(8,128)}, u32[]{:S(2)}, u32[]{:S(2)}) collective-permute-start(f32[33,64,256]{2,1,0:T(8,128)} %get-tuple-element.286), channel_id=1, source_target_pairs={{0,16},{16,32},{32,48},{48,64},{64,80},{80,96},{96,112},{1,17},{17... | collective-permute-start | bytes 6488072 | tf_op jit(solution)/shard_map/ppermute | solution.py:16
  276.8 57.0 %collective-permute-start.1 = (f32[33,64,256]{2,1,0:T(8,128)}, f32[33,64,256]{2,1,0:T(8,128)S(1)}, u32[]{:S(2)}, u32[]{:S(2)}) collective-permute-start(f32[33,64,256]{2,1,0:T(8,128)} %get-tuple-element.287), channel_id=1, source_target_pairs={{16,0},{32,16},{48,32},{64,48},{80,64},{96,80},{112,96},{17,1},{33... | collective-permute-start | bytes 6488072 | tf_op jit(solution)/shard_map/ppermute | solution.py:19
  355.1 30.3 %collective-permute-start.2 = (f32[33,256,64]{1,2,0:T(8,128)S(1)}, f32[33,256,64]{1,2,0:T(8,128)}, u32[]{:S(2)}, u32[]{:S(2)}) collective-permute-start(f32[33,256,64]{1,2,0:T(8,128)S(1)} %copy.41), channel_id=1, source_target_pairs={{0,1},{1,2},{2,3},{3,4},{4,5},{5,6},{6,7},{7,8},{8,9},{9,10},{10,1... | collective-permute-start | bytes 6488072 | tf_op jit(solution)/shard_map/ppermute | solution.py:16
  359.0 30.3 %collective-permute-start.3 = (f32[33,256,64]{1,2,0:T(8,128)}, f32[33,256,64]{1,2,0:T(8,128)}, u32[]{:S(2)}, u32[]{:S(2)}) collective-permute-start(f32[33,256,64]{1,2,0:T(8,128)} %copy.43), channel_id=1, source_target_pairs={{1,0},{2,1},{3,2},{4,3},{5,4},{6,5},{7,6},{8,7},{9,8},{10,9},{11,1... | collective-permute-start | bytes 6488072 | tf_op jit(solution)/shard_map/ppermute | solution.py:19
  395.3 9.7 %copy-start = (f32[33,256,128]{1,0,2:T(8,128)}, f32[33,256,128]{1,0,2:T(8,128)S(1)}, u32[]{:S(2)}) copy-start(f32[33,256,128]{1,0,2:T(8,128)S(1)} %fusion.25) | copy-start | bytes 12976132
  395.5 9.8 %collective-permute-start.4 = (f32[2,128]{0,1:T(8,128)S(1)}, f32[2,128]{0,1:T(8,128)S(1)}, u32[]{:S(2)}, u32[]{:S(2)}) collective-permute-start(f32[2,128]{0,1:T(8,128)S(1)} %bitcast.72), channel_id=1, source_target_pairs={{0,16},{16,32},{32,48},{48,64},{64,80},{80,96},{96,112},{1,17},{17... | collective-permute-start | bytes 3080 | tf_op jit(solution)/shard_map/ppermute | solution.py:16
  397.4 9.4 %collective-permute-start.5 = (f32[2,128]{0,1:T(8,128)S(1)}, f32[2,128]{0,1:T(8,128)S(1)}, u32[]{:S(2)}, u32[]{:S(2)}) collective-permute-start(f32[2,128]{0,1:T(8,128)S(1)} %bitcast.71), channel_id=1, source_target_pairs={{16,0},{32,16},{48,32},{64,48},{80,64},{96,80},{112,96},{17,1},{33... | collective-permute-start | bytes 3080 | tf_op jit(solution)/shard_map/ppermute | solution.py:19
  406.9 19.3 %collective-permute-start.6 = (f32[260,2]{0,1:T(2,128)S(1)}, f32[260,2]{0,1:T(2,128)S(1)}, u32[]{:S(2)}, u32[]{:S(2)}) collective-permute-start(f32[260,2]{0,1:T(2,128)S(1)} %get-tuple-element.292), channel_id=1, source_target_pairs={{0,1},{1,2},{2,3},{3,4},{4,5},{5,6},{6,7},{7,8},{8,9},{9,10},{10,1... | collective-permute-start | bytes 6248 | tf_op jit(solution)/shard_map/ppermute | solution.py:16
  408.8 17.4 %collective-permute-start.7 = (f32[260,2]{0,1:T(2,128)S(1)}, f32[260,2]{0,1:T(2,128)S(1)}, u32[]{:S(2)}, u32[]{:S(2)}) collective-permute-start(f32[260,2]{0,1:T(2,128)S(1)} %get-tuple-element.293), channel_id=1, source_target_pairs={{1,0},{2,1},{3,2},{4,3},{5,4},{6,5},{7,6},{8,7},{9,8},{10,9},{11,1... | collective-permute-start | bytes 6248 | tf_op jit(solution)/shard_map/ppermute | solution.py:19
where the time goes:
time: 431 us; the launch traced here: 428 us
  local copies, waits for them, and re-layouts  194 us (45%)
  matrix products  77.4 us (18%)
  other arithmetic  70.5 us (16%)
  waiting for transfers between devices  50 us (12%)
  starting transfers between devices  34.2 us (8%)
    slice x6, local copies, waits for them, and re-layouts, one_block(): piece[:, 0:out_cols]  68.6 us
    ppermute x4, waiting for transfers between devices, padded_2(): lax.ppermute(lax.slice_in_dim(block, block.shape[dim] - width, None, axis...  47.3 us
    dot_general x6, matrix products, one_block(): lax.dot_general(head_weight, hidden, (((0,), (1,)), ((), ())), preferred_...  42.7 us
    concatenate x6, other arithmetic, one_block(): jnp.concatenate([piece[:, 0:out_cols], piece[:, 1:out_cols + 1], piece[:,...  41.2 us
    dot_general x6, matrix products, one_block(): jnp.dot(stacked[1:block_rows + 1].reshape(-1, 3 * in_count), taps[1], pre...  27.4 us
    another operation x3, local copies, waits for them, and re-layouts  25.6 us
    ppermute x4, starting transfers between devices, padded_2(): lax.ppermute(lax.slice_in_dim(block, 0, width, axis=dim), axis, backward)  25 us
    slice x6, local copies, waits for them, and re-layouts, one_block(): stacked[2:block_rows + 2].reshape(-1, 3 * in_count)  17.7 us
  transfers between devices with their start and end apart: 8, of which 5 were waited for; matrix products, arithmetic and copies ran while one was open for 10% of the time, Pallas kernels for 0%

commit v1 on v0

v1 whole, which is shorter than its diff:
```python
import functools

import jax
import jax.numpy as jnp
from jax import lax
from jax.experimental import pallas as pl
from jax.experimental.pallas import tpu as pltpu
from jax.sharding import PartitionSpec as P

MARGIN = 64
EXT_H, EXT_W = 384, 256
CORE_H, CORE_W = 256, 128
N_ROWS, N_COLS = 8, 16
CIN, COUT, RAYS = 32, 128, 32
M_PAIRS = 73
C_PAIRS = 128
M_OUT = 72
TAPS = 3 * CIN
F32, BF16 = jnp.float32, jnp.bfloat16


def lanes_of(shape):
    return lax.broadcasted_iota(jnp.int32, shape, len(shape) - 1)


def gauss(position, extent):
    spread = extent / 4.0
    centred = position.astype(F32) - (extent - 1) / 2.0
    return jnp.exp(-(centred * centred) / (2.0 * spread * spread))


def pack_pair(lo, hi, t, right_ref, left_ref, slot, extras):
    low_half = lanes_of((CIN, 128)) < 64
    spot = lanes_of((CIN, 128)) == t
    west_lo, east_lo = lo[:, :128], lo[:, 128:]
    west_hi, east_hi = hi[:, :128], hi[:, 128:]
    right_ref[slot] = jnp.where(low_half, pltpu.roll(east_lo, 64, 1), east_hi)
    left_ref[slot] = jnp.where(low_half, west_hi, pltpu.roll(west_lo, 64, 1))
    to_t_east = lax.rem(t + 128 - 63, 128)
    to_t_west = lax.rem(t + 128 - 64, 128)
    return (
        jnp.where(spot, pltpu.roll(east_lo, to_t_east, 1), extras[0]),
        jnp.where(spot, pltpu.roll(east_hi, to_t_east, 1), extras[1]),
        jnp.where(spot, pltpu.roll(west_lo, to_t_west, 1), extras[2]),
        jnp.where(spot, pltpu.roll(west_hi, to_t_west, 1), extras[3]),
    )


def pack_margin_kernel(tissue_ref, top_ref, bottom_ref, right_ref, left_ref):
    zero = jnp.zeros((CIN, 128), BF16)

    def step(t, extras):
        return pack_pair(top_ref[t], bottom_ref[95 - t], t, right_ref, left_ref, t, extras)

    extras = lax.fori_loop(0, M_PAIRS, step, (zero, zero, zero, zero))
    flag = jnp.where(tissue_ref[0, 0] > 0, 1.0, 0.0)
    flags = jnp.full((CIN, 128), flag, F32).astype(BF16)
    right_ref[M_PAIRS] = extras[0]
    right_ref[M_PAIRS + 1] = extras[1]
    right_ref[M_PAIRS + 2] = flags
    left_ref[M_PAIRS] = extras[2]
    left_ref[M_PAIRS + 1] = extras[3]
    left_ref[M_PAIRS + 2] = flags


def pack_margin(tissue, features):
    shape = jax.ShapeDtypeStruct((M_PAIRS + 3, CIN, 128), BF16)
    return pl.pallas_call(
        pack_margin_kernel,
        grid=(1,),
        in_specs=[
            pl.BlockSpec(memory_space=pltpu.SMEM),
            pl.BlockSpec((96, CIN, EXT_W), lambda s: (0, 0, 0)),
            pl.BlockSpec((96, CIN, EXT_W), lambda s: (3, 0, 0)),
        ],
        out_specs=[pl.BlockSpec(shape.shape, lambda s: (0, 0, 0))] * 2,
        out_shape=[shape, shape],
        compiler_params=pltpu.CompilerParams(vmem_limit_bytes=32 << 20),
        cost_estimate=pl.CostEstimate(flops=0, bytes_accessed=5 << 20, transcendentals=0),
    )(tissue, features, features)


def pack_core_kernel(low_ref, high_ref, right_ref, left_ref):
    zero = jnp.zeros((CIN, 128), BF16)

    def step(t, extras):
        q = lax.div(t, 64)
        s = lax.rem(t, 64)
        return pack_pair(
            low_ref[t], high_ref[127 - t], t, right_ref, left_ref, t, extras
        )

    extras = lax.fori_loop(0, C_PAIRS, step, (zero, zero, zero, zero))
    right_ref[C_PAIRS] = extras[0]
    right_ref[C_PAIRS + 1] = extras[1]
    left_ref[C_PAIRS] = extras[2]
    left_ref[C_PAIRS + 1] = extras[3]


def pack_core(features):
    shape = jax.ShapeDtypeStruct((C_PAIRS + 2, CIN, 128), BF16)
    core = features[MARGIN : EXT_H - MARGIN]
    return pl.pallas_call(
        pack_core_kernel,
        grid=(1,),
        in_specs=[
            pl.BlockSpec((128, CIN, EXT_W), lambda s: (0, 0, 0)),
            pl.BlockSpec((128, CIN, EXT_W), lambda s: (1, 0, 0)),
        ],
        out_specs=[pl.BlockSpec(shape.shape, lambda s: (0, 0, 0))] * 2,
        out_shape=[shape, shape],
        compiler_params=pltpu.CompilerParams(vmem_limit_bytes=32 << 20),
        cost_estimate=pl.CostEstimate(flops=0, bytes_accessed=6 << 20, transcendentals=0),
    )(core, core)


def column_taps(own, strip, from_west, from_east):
    lane = lanes_of((CIN, 128))
    west, east = own[:, :128], own[:, 128:]
    zero = jnp.zeros((CIN, 128), BF16)

    def own_tap(shift):
        amount = 64 - shift
        return jnp.where(lane < amount, pltpu.roll(west, amount, 1), pltpu.roll(east, amount, 1))

    strip_minus = jnp.where(
        lane == 0, from_west, jnp.where(lane == 64, zero, pltpu.roll(strip, 1, 1))
    )
    strip_plus = jnp.where(
        lane == 127, from_east, jnp.where(lane == 63, zero, pltpu.roll(strip, 127, 1))
    )
    return (
        jnp.concatenate([own_tap(-1), strip_minus], axis=1),
        jnp.concatenate([own_tap(0), strip], axis=1),
        jnp.concatenate([own_tap(1), strip_plus], axis=1),
    )


def build_pair(own_lo, own_hi, left, right, extras, t, taps_ref, lo_index, hi_index):
    low_half = lanes_of((CIN, 128)) < 64
    strip_lo = jnp.where(low_half, left, right)
    strip_hi = pltpu.roll(jnp.where(low_half, right, left), 64, 1)
    to_first = lax.rem(128 - t, 128)
    to_last = 127 - t
    for own, strip, west, east, index in (
        (own_lo, strip_lo, extras[0], extras[2], lo_index),
        (own_hi, strip_hi, extras[1], extras[3], hi_index),
    ):
        parts = column_taps(own, strip, pltpu.roll(west, to_first, 1), pltpu.roll(east, to_last, 1))
        start = pl.multiple_of(index * TAPS, 32)
        for k, part in enumerate(parts):
            taps_ref[pl.ds(start + k * CIN, CIN), :] = part


def prepare_weights(conv_ref, head_ref, bias_ref, conv_scr, head_scr):
    zero = jnp.zeros((TAPS, COUT), BF16)
    conv_scr[0 : 3 * TAPS, 0:COUT] = conv_ref[...]
    conv_scr[3 * TAPS : 4 * TAPS, 0:COUT] = zero
    conv_scr[0:TAPS, COUT:] = zero
    conv_scr[TAPS : 4 * TAPS, COUT:] = conv_ref[...]
    head = head_ref[...].astype(F32)
    head = jnp.concatenate([head, jnp.zeros((COUT - head.shape[0], COUT), F32)], axis=0).T
    lane = lanes_of((COUT, 128))
    for r in range(4):
        rays = pltpu.roll(head, (r * RAYS - 1) % 128, 1)
        rays = jnp.where((lane >= r * RAYS) & (lane < (r + 1) * RAYS), rays, 0.0)
        prob = jnp.where(lane == r, pltpu.roll(head, r, 1), 0.0)
        head_scr[r * COUT : (r + 1) * COUT, 0:128] = rays.astype(BF16)
        head_scr[r * COUT : (r + 1) * COUT, 128:256] = prob.astype(BF16)


def spread_bias(head_bias):
    lane = lanes_of((8, 128))
    rays = jnp.zeros((8, 128), F32)
    for r in range(4):
        moved = pltpu.roll(head_bias, (r * RAYS - 1) % 128, 1)
        rays = jnp.where((lane >= r * RAYS) & (lane < (r + 1) * RAYS), moved, rays)
    return rays[0:1]


def column_weights(tile_col, tissue, left_flags, right_flags):
    q = lax.broadcasted_iota(jnp.int32, (CORE_W, 128), 0)
    own = gauss(q + MARGIN, EXT_W)
    west = gauss(q + CORE_W + MARGIN, EXT_W)
    east = gauss(q - MARGIN, EXT_W)
    west_side = q < MARGIN
    has_west = jnp.where(tile_col > 0, 1.0, 0.0)
    has_east = jnp.where(tile_col < N_COLS - 1, 1.0, 0.0)
    side = jnp.where(west_side, west, east)
    total = own + side * jnp.where(west_side, has_west, has_east)
    flags = jnp.concatenate([left_flags, left_flags, right_flags, right_flags], axis=0)
    return own / total * jnp.where(tissue > 0, 1.0, 0.0), side / total * flags


def row_weights(row, tile_row):
    own = gauss(row, EXT_H)
    above = gauss(row + CORE_H, EXT_H) * jnp.where(tile_row > 0, 1.0, 0.0)
    below = gauss(row - CORE_H, EXT_H) * jnp.where(tile_row < N_ROWS - 1, 1.0, 0.0)
    total = own + jnp.where(row < 2 * MARGIN, above, 0.0) + jnp.where(row >= CORE_H, below, 0.0)
    return own / total


def group_logits(taps_ref, base, conv_scr, head_scr, bias):
    hidden = []
    for pair in range(2):
        start = pl.multiple_of((base + 2 * pair) * TAPS, 64)
        summed = lax.dot_general(
            taps_ref[pl.ds(start, 4 * TAPS), :],
            conv_scr[...],
            (((0,), (0,)), ((), ())),
            preferred_element_type=F32,
        )
        hidden.append(jnp.maximum(summed + bias, 0.0).astype(BF16))
    return jnp.dot(
        jnp.concatenate(hidden, axis=1), head_scr[...], preferred_element_type=F32
    )


def probability_block(logits, bias, first_row, tile_row, own_weight, side_weight):
    rows = lanes_of((CORE_W, 128)) + first_row
    values = 1.0 / (1.0 + jnp.exp(-(logits + bias)))
    return (values[:CORE_W] * own_weight + values[CORE_W:] * side_weight) * row_weights(
        rows, tile_row
    )


def margin_kernel(
    where_ref, tissue_ref, top_ref, bottom_ref, left_ref, right_ref,
    conv_ref, bias_ref, head_ref, hbias_ref,
    up_ref, down_ref, edge_ref,
    taps_ref, logit_ref, conv_scr, head_scr,
):
    tile_row, tile_col = where_ref[0], where_ref[1]
    prepare_weights(conv_ref, head_ref, bias_ref, conv_scr, head_scr)
    second = M_PAIRS + 1
    taps_ref[0:TAPS, :] = jnp.zeros((TAPS, 256), BF16)
    taps_ref[(2 * M_PAIRS + 1) * TAPS : (2 * M_PAIRS + 2) * TAPS, :] = jnp.zeros((TAPS, 256), BF16)
    extras = (left_ref[M_PAIRS], left_ref[M_PAIRS + 1], right_ref[M_PAIRS], right_ref[M_PAIRS + 1])

    def build(t, carry):
        build_pair(
            top_ref[t], bottom_ref[95 - t], left_ref[t], right_ref[t], extras, t,
            taps_ref, t + 1, second + 72 - t,
        )
        return carry

    lax.fori_loop(0, M_PAIRS, build, 0)
    own_weight, side_weight = column_weights(
        tile_col, tissue_ref[0, 0],
        left_ref[M_PAIRS + 2].astype(F32), right_ref[M_PAIRS + 2].astype(F32),
    )
    bias = jnp.concatenate([bias_ref[...], bias_ref[...]], axis=1)
    ray_bias = spread_bias(hbias_ref[...])
    logit_ref[...] = jnp.zeros(logit_ref.shape, F32)
    quarter = lax.div(lanes_of((1, 128)), RAYS)

    def compute(g, carry):
        for block, first_row, base in ((0, 0, 0), (1, 312, second)):
            logits = group_logits(taps_ref, base + 4 * g, conv_scr, head_scr, bias)
            factor = row_weights(first_row + 4 * g + quarter, tile_row)
            rays = (
                (logits[:CORE_W, :128] + ray_bias) * own_weight
                + (logits[CORE_W:, :128] + ray_bias) * side_weight
            ) * factor
            logit_ref[block] += pltpu.roll(logits[:, 128:], 4 * g, 1)
            if block == 0:
                @pl.when(g < 16)
                def _():
                    up_ref[pl.ds(pl.multiple_of(g * 128, 128), 128), :] = rays.astype(BF16)
            else:
                @pl.when(g >= 2)
                def _():
                    down_ref[pl.ds(pl.multiple_of((g - 2) * 128, 128), 128), :] = rays.astype(BF16)
        return carry

    lax.fori_loop(0, M_OUT // 4, compute, 0)
    for block, first_row, ref in ((0, 0, up_ref), (1, 312, down_ref)):
        prob = probability_block(
            logit_ref[block], hbias_ref[0, 0], first_row, tile_row, own_weight, side_weight
        )
        prob = jnp.where(lanes_of((CORE_W, 128)) < M_OUT, prob, 0.0)
        edge_ref[block] = prob
        high = prob.astype(BF16)
        ref[2048:2176, :] = high
        ref[2176:2304, :] = (prob - high.astype(F32)).astype(BF16)


def margin_outputs(where, tissue, features, left, right, weights):
    shape = jax.ShapeDtypeStruct((2304, 128), BF16)
    edge = jax.ShapeDtypeStruct((2, CORE_W, 128), F32)
    smem = pl.BlockSpec(memory_space=pltpu.SMEM)
    vmem = pl.BlockSpec(memory_space=pltpu.VMEM)
    return pl.pallas_call(
        margin_kernel,
        grid=(1,),
        in_specs=[
            smem, smem,
            pl.BlockSpec((96, CIN, EXT_W), lambda s: (0, 0, 0)),
            pl.BlockSpec((96, CIN, EXT_W), lambda s: (3, 0, 0)),
            vmem, vmem, vmem, vmem, vmem, vmem,
        ],
        out_specs=[vmem, vmem, vmem],
        out_shape=[shape, shape, edge],
        scratch_shapes=[
            pltpu.VMEM(((2 * M_PAIRS + 2) * TAPS, 256), BF16),
            pltpu.VMEM((2, 256, 128), F32),
            pltpu.VMEM((4 * TAPS, 256), BF16),
            pltpu.VMEM((4 * COUT, 256), BF16),
        ],
        compiler_params=pltpu.CompilerParams(vmem_limit_bytes=48 << 20),
        cost_estimate=pl.CostEstimate(flops=8 << 30, bytes_accessed=8 << 20, transcendentals=0),
    )(where, tissue, features, features, left, right, *weights)


def core_kernel(
    where_ref, tissue_ref, before_ref, low_ref, high_ref, after_ref, mleft_ref, mright_ref,
    left_ref, right_ref, conv_ref, bias_ref, head_ref, hbias_ref,
    rays_ref, prob_ref,
    taps_ref, logit_ref, conv_scr, head_scr,
):
    tile_row, tile_col = where_ref[0], where_ref[1]
    prepare_weights(conv_ref, head_ref, bias_ref, conv_scr, head_scr)
    extras = (mleft_ref[M_PAIRS], mleft_ref[M_PAIRS + 1], mright_ref[M_PAIRS], mright_ref[M_PAIRS + 1])
    build_pair(
        before_ref[0], after_ref[0], mleft_ref[63], mright_ref[63], extras, 63,
        taps_ref, 0, 257,
    )
    extras = (left_ref[C_PAIRS], left_ref[C_PAIRS + 1], right_ref[C_PAIRS], right_ref[C_PAIRS + 1])

    def build(t, carry):
        build_pair(
            low_ref[t], high_ref[127 - t], left_ref[t], right_ref[t], extras, t,
            taps_ref, 1 + t, 256 - t,
        )
        return carry

    lax.fori_loop(0, C_PAIRS, build, 0)
    own_weight, side_weight = column_weights(
        tile_col, tissue_ref[0, 0],
        mleft_ref[M_PAIRS + 2].astype(F32), mright_ref[M_PAIRS + 2].astype(F32),
    )
    bias = jnp.concatenate([bias_ref[...], bias_ref[...]], axis=1)
    ray_bias = spread_bias(hbias_ref[...])
    logit_ref[...] = jnp.zeros(logit_ref.shape, F32)
    quarter = lax.div(lanes_of((1, 128)), RAYS)

    def compute(h, carry):
        for block in range(2):
            g = block * 32 + h
            logits = group_logits(taps_ref, 4 * g, conv_scr, head_scr, bias)
            factor = row_weights(MARGIN + 4 * g + quarter, tile_row)
            rays = (
                (logits[:CORE_W, :128] + ray_bias) * own_weight
                + (logits[CORE_W:, :128] + ray_bias) * side_weight
            ) * factor
            rays_ref[g] = rays
            logit_ref[block] += pltpu.roll(logits[:, 128:], 4 * h, 1)
        return carry

    lax.fori_loop(0, 32, compute, 0)
    for block in range(2):
        prob_ref[block] = probability_block(
            logit_ref[block], hbias_ref[0, 0], MARGIN + 128 * block, tile_row,
            own_weight, side_weight,
        )


def core_outputs(where, tissue, features, mleft, mright, left, right, weights):
    smem = pl.BlockSpec(memory_space=pltpu.SMEM)
    vmem = pl.BlockSpec(memory_space=pltpu.VMEM)
    core = features[MARGIN : EXT_H - MARGIN]
    return pl.pallas_call(
        core_kernel,
        grid=(1,),
        in_specs=[
            smem, smem,
            pl.BlockSpec((1, CIN, EXT_W), lambda s: (63, 0, 0)),
            pl.BlockSpec((128, CIN, EXT_W), lambda s: (0, 0, 0)),
            pl.BlockSpec((128, CIN, EXT_W), lambda s: (1, 0, 0)),
            pl.BlockSpec((1, CIN, EXT_W), lambda s: (320, 0, 0)),
            vmem, vmem, vmem, vmem, vmem, vmem, vmem, vmem,
        ],
        out_specs=[vmem, vmem],
        out_shape=[
            jax.ShapeDtypeStruct((64, CORE_W, 128), F32),
            jax.ShapeDtypeStruct((2, CORE_W, 128), F32),
        ],
        scratch_shapes=[
            pltpu.VMEM((258 * TAPS, 256), BF16),
            pltpu.VMEM((2, 256, 128), F32),
            pltpu.VMEM((4 * TAPS, 256), BF16),
            pltpu.VMEM((4 * COUT, 256), BF16),
        ],
        compiler_params=pltpu.CompilerParams(vmem_limit_bytes=56 << 20),
        cost_estimate=pl.CostEstimate(flops=16 << 30, bytes_accessed=12 << 20, transcendentals=0),
    )(where, tissue, features, core, core, features, mleft, mright, left, right, *weights)


def finish_kernel(
    where_ref, rays_ref, prob_ref, edge_ref, above_ref, below_ref,
    out_ref, probability_ref, wide_ref, west_ref, east_ref, group_ref,
):
    tile_row = where_ref[0]
    quarter = lax.div(lanes_of((32, 128)), RAYS)

    def group(g, carry):
        rays = rays_ref[g]
        group_ref[...] = rays

        @pl.when(g < 16)
        def _():
            start = pl.multiple_of(g * 128, 128)
            group_ref[...] += above_ref[pl.ds(start, 128), :].astype(F32)

        @pl.when(g >= 48)
        def _():
            start = pl.multiple_of((g - 48) * 128, 128)
            group_ref[...] += below_ref[pl.ds(start, 128), :].astype(F32)

        phases = [group_ref[pl.ds(b, 32, stride=4), :] for b in range(4)]
        for p in range(4):
            row = phases[0] if p == 0 else pltpu.roll(phases[0], (-p * RAYS) % 128, 1)
            for b in range(1, 4):
                moved = phases[b] if b == p else pltpu.roll(phases[b], ((b - p) * RAYS) % 128, 1)
                row = jnp.where(quarter == b, moved, row)
            start = lax.div(g, 2) * 256 + lax.rem(g, 2) * 4 + p
            out_ref[pl.ds(start, 32, stride=8), :] = row
        return carry

    lax.fori_loop(0, 64, group, 0)
    lane = lanes_of((CORE_W, 128))
    above = above_ref[2048:2176, :].astype(F32) + above_ref[2176:2304, :].astype(F32)
    below = below_ref[2048:2176, :].astype(F32) + below_ref[2176:2304, :].astype(F32)
    first = prob_ref[0] + jnp.where(lane < 64, pltpu.roll(above, 120, 1), 0.0)
    last = prob_ref[1] + jnp.where(lane >= 64, pltpu.roll(below, 64, 1), 0.0)
    probability_ref[0:128, :] = first.T
    probability_ref[128:256, :] = last.T
    head = pltpu.roll(above, 122, 1) + pltpu.roll(edge_ref[0], 66, 1)
    head = jnp.where(tile_row > 0, head, 0.0)
    tail = pltpu.roll(edge_ref[1], 122, 1) + pltpu.roll(below, 66, 1)
    tail = jnp.where(tile_row < N_ROWS - 1, tail, 0.0)
    first_moved, last_moved = pltpu.roll(first, 2, 1), pltpu.roll(last, 2, 1)
    parts = [
        jnp.where(lane < 2, head, first_moved),
        jnp.where(lane < 2, first_moved, last_moved),
        jnp.where(lane < 2, last_moved, jnp.where(lane < 4, tail, 0.0)),
    ]
    for k, part in enumerate(parts):
        wide_ref[:, 128 * k : 128 * (k + 1)] = part
        west_ref[:, 128 * k : 128 * (k + 1)] = part[0:8]
        east_ref[:, 128 * k : 128 * (k + 1)] = part[120:128]


def finish(where, rays, prob, edge, above, below):
    smem = pl.BlockSpec(memory_space=pltpu.SMEM)
    vmem = pl.BlockSpec(memory_space=pltpu.VMEM)
    return pl.pallas_call(
        finish_kernel,
        in_specs=[smem, vmem, vmem, vmem, vmem, vmem],
        out_specs=[vmem] * 5,
        out_shape=[
            jax.ShapeDtypeStruct((8192, 128), F32),
            jax.ShapeDtypeStruct((CORE_H, CORE_W), F32),
            jax.ShapeDtypeStruct((CORE_W, 384), F32),
            jax.ShapeDtypeStruct((8, 384), F32),
            jax.ShapeDtypeStruct((8, 384), F32),
        ],
        scratch_shapes=[pltpu.VMEM((CORE_W, 128), F32)],
        compiler_params=pltpu.CompilerParams(vmem_limit_bytes=40 << 20),
        cost_estimate=pl.CostEstimate(flops=0, bytes_accessed=10 << 20, transcendentals=0),
    )(where, rays, prob, edge, above, below)


def peak_kernel(wide_ref, west_ref, east_ref, gap_ref, tall_ref):
    tall_ref[0:8, :] = west_ref[...]
    tall_ref[8:136, :] = wide_ref[...]
    tall_ref[136:144, :] = east_ref[...]
    best = tall_ref[6:134, :]
    for k in range(1, 5):
        best = jnp.maximum(best, tall_ref[6 + k : 134 + k, :])
    along = best
    for k in range(1, 5):
        along = jnp.maximum(along, pltpu.roll(best, 384 - k, 1))
    gap = along - pltpu.roll(wide_ref[...], 382, 1)
    gap_ref[0:128, :] = gap[:, 0:128].T
    gap_ref[128:256, :] = gap[:, 128:256].T


def peak(wide, west, east):
    vmem = pl.BlockSpec(memory_space=pltpu.VMEM)
    return pl.pallas_call(
        peak_kernel,
        in_specs=[vmem] * 3,
        out_specs=vmem,
        out_shape=jax.ShapeDtypeStruct((CORE_H, CORE_W), F32),
        scratch_shapes=[pltpu.VMEM((144, 384), F32)],
    )(wide, west, east)


def shift(array, axis, step):
    count = lax.axis_size(axis)
    pairs = [(i, i + step) for i in range(count) if 0 <= i + step < count]
    return lax.ppermute(array, axis, pairs)


def body(features, conv_weight, conv_bias, head_weight, head_bias, tissue):
    features = jnp.transpose(features, (0, 2, 1))
    where = jnp.stack([lax.axis_index("rows"), lax.axis_index("cols")]).astype(jnp.int32)
    hbias = jnp.pad(head_bias[None, :], ((0, 7), (0, 128 - head_bias.shape[0])))
    weights = (
        conv_weight.reshape(9 * CIN, COUT), conv_bias[None, :], jnp.transpose(head_weight), hbias,
    )
    to_right, to_left = pack_margin(tissue, features)
    mleft = shift(to_right, "cols", 1)
    mright = shift(to_left, "cols", -1)
    to_right, to_left = pack_core(features)
    cleft = shift(to_right, "cols", 1)
    cright = shift(to_left, "cols", -1)
    up, down, edge = margin_outputs(where, tissue, features, mleft, mright, weights)
    above = shift(down, "rows", 1)
    below = shift(up, "rows", -1)
    rays, prob = core_outputs(where, tissue, features, mleft, mright, cleft, cright, weights)
    out, probability, wide, west, east = finish(where, rays, prob, edge, above, below)
    from_west = shift(east, "cols", 1)
    from_east = shift(west, "cols", -1)
    gap = peak(wide, from_west, from_east)
    lengths = out.reshape(32, 32, 8, 128).transpose(0, 2, 1, 3).reshape(CORE_H, CORE_W * RAYS)
    return (probability, lengths, gap)


def solution(mesh):
    in_specs = (P("rows", "cols", None), P(), P(), P(), P(), P("rows", "cols"))
    out_specs = (P("rows", "cols"), P("rows", "cols"), P("rows", "cols"))
    return jax.shard_map(body, mesh=mesh, in_specs=in_specs, out_specs=out_specs, check_vma=False)
```

time: 431 us -> 159 us (0.37)
  local copies, waits for them, and re-layouts: 194 us -> 7.66 us
  Pallas kernels: 0 us -> 116 us
  matrix products: 77.4 us -> 0 us
  other arithmetic: 70.5 us -> 0.08 us
  waiting for transfers between devices: 50 us -> 1.38 us
    pallas_call x0 -> x6, Pallas kernels: none -> 116 us  [the longest x1 51.4 us: core_outputs(): pl.pallas_call(core_kernel, grid=(1,), in_specs=[smem, smem, pl.BlockSpec...]
    slice x26 -> x1, local copies, waits for them, and re-layouts: 111 us -> 0.44 us  [core_outputs(): core = features[MARGIN:EXT_H - MARGIN]]
    dot_general x18 -> x0, matrix products: 77.4 us -> none  [the longest x6 42.7 us: one_block(): lax.dot_general(head_weight, hidden, (((0,), (1,)), ((), ())), preferred_...]
    ppermute x8, waiting for transfers between devices: 50 us -> 1.38 us  [shift(): return lax.ppermute(array, axis, pairs)]
    concatenate x13 -> x0, other arithmetic: 42.7 us -> none  [the longest x6 41.2 us: one_block(): jnp.concatenate([piece[:, 0:out_cols], piece[:, 1:out_cols + 1], piece[:,...]
    another operation x3 -> x0, local copies, waits for them, and re-layouts: 25.6 us -> none
    pad x1, local copies, waits for them, and re-layouts: 17.6 us -> 0.01 us  [body(): hbias = jnp.pad(head_bias[None, :], ((0, 7), (0, 128 - head_bias.shape[0])))]
    ppermute x4 -> x0, local copies, waits for them, and re-layouts: 16.6 us -> none  [the longest x2 8.78 us: padded_2(): lax.ppermute(lax.slice_in_dim(block, block.shape[dim] - width, None, axis...]
  transfers between devices with their start and end apart: 8 -> 8, of which waited for: 5 -> 1; matrix products, arithmetic and copies ran while one was open for 10% -> 0% of each run, Pallas kernels for 0% -> 60%
where the time goes in v1:
time: 159 us
  Pallas kernels  116 us (73%)
  starting transfers between devices  32.4 us (20%)
  local copies, waits for them, and re-layouts  7.66 us (5%)
  between operations  1.59 us (1%)
    pallas_call x1, Pallas kernels, core_outputs(): pl.pallas_call(core_kernel, grid=(1,), in_specs=[smem, smem, pl.BlockSpec...  51.4 us
    pallas_call x1, Pallas kernels, margin_outputs(): pl.pallas_call(margin_kernel, grid=(1,), in_specs=[smem, smem, pl.BlockSp...  33.8 us
    ppermute x8, starting transfers between devices, shift(): return lax.ppermute(array, axis, pairs)  32.4 us
    pallas_call x1, Pallas kernels, finish(): pl.pallas_call(finish_kernel, in_specs=[smem, vmem, vmem, vmem, vmem, vme...  11.3 us
    pallas_call x1, Pallas kernels, pack_core(): pl.pallas_call(pack_core_kernel, grid=(1,), in_specs=[pl.BlockSpec((128,...  10.3 us
    unnamed x34, local copies, waits for them, and re-layouts  7.21 us
    pallas_call x1, Pallas kernels, pack_margin(): pl.pallas_call(pack_margin_kernel, grid=(1,), in_specs=[pl.BlockSpec(memo...  6.92 us
  transfers between devices with their start and end apart: 8, of which 1 were waited for; matrix products, arithmetic and copies ran while one was open for 0% of the time, Pallas kernels for 60%

profile of v1, /device:TPU:6, one launch (start us, length us, event | category | flops | bytes accessed | tf_op | source)
XLA Modules:
  0.0 158.9 jit_solution(10514828442954265365)
XLA Ops:
  1.3 0.0 copy-start
  1.3 2.8 %copy-done = bf16[384,256,32]{1,2,0:T(8,128)(2,1)S(1)} copy-done((bf16[384,256,32]{1,2,0:T(8,128)(2,1)S(1)}, bf16[384,256,32]{1,2,0:T(8,128)(2,1)}, u32[]{:S(2)}) %copy-start) | copy-done | bytes 6291480
  4.1 6.9 %shard_map.85 = (bf16[76,32,128]{2,1,0:T(8,128)(2,1)}, bf16[76,32,128]{2,1,0:T(8,128)(2,1)}) custom-call(s32[1,1]{1,0:T(1,128)S(6)} %copy.9.tissue_ref, bf16[384,32,256]{2,1,0:T(8,128)(2,1)S(1)} %bitcast.16, bf16[384,32,256]{2,1,0:T(8,128)(2,1)S(1)} %bitcast.17), custom_call_target="tpu_custom_call" | custom-call | bytes 5242880 | tf_op jit(solution)/shard_map/pallas_call | solution.py:68
  11.0 1.9 %collective-permute-start = (bf16[76,32,128]{2,1,0:T(8,128)(2,1)}, bf16[76,32,128]{2,1,0:T(8,128)(2,1)S(1)}, u32[]{:S(2)}, u32[]{:S(2)}) collective-permute-start(bf16[76,32,128]{2,1,0:T(8,128)(2,1)} %get-tuple-element.17), channel_id=1, source_target_pairs={{0,1},{1,2},{2,3},{3,4},{4,5},{5,6},{6,7},{7,8},{8,9},{9,10},{10,1... | collective-permute-start | bytes 1867784 | tf_op jit(solution)/shard_map/ppermute | solution.py:503
  12.9 5.8 %collective-permute-start.1 = (bf16[76,32,128]{2,1,0:T(8,128)(2,1)}, bf16[76,32,128]{2,1,0:T(8,128)(2,1)S(1)}, u32[]{:S(2)}, u32[]{:S(2)}) collective-permute-start(bf16[76,32,128]{2,1,0:T(8,128)(2,1)} %get-tuple-element.18), channel_id=1, source_target_pairs={{1,0},{2,1},{3,2},{4,3},{5,4},{6,5},{7,6},{8,7},{9,8},{10,9},{11,1... | collective-permute-start | bytes 1867784 | tf_op jit(solution)/shard_map/ppermute | solution.py:503
  18.7 0.4 slice.5.low_ref.high_ref
  19.1 0.0 copy-start.2
  19.1 0.0 copy-start.16
  19.1 0.0 copy-start.11
  19.2 0.0 copy-start.12
  19.2 0.0 copy-start.13
  19.2 10.3 %shard_map.86 = (bf16[130,32,128]{2,1,0:T(8,128)(2,1)S(1)}, bf16[130,32,128]{2,1,0:T(8,128)(2,1)S(1)}) custom-call(bf16[256,32,256]{2,1,0:T(8,128)(2,1)S(1)} %slice.5.low_ref.high_ref, bf16[256,32,256]{2,1,0:T(8,128)(2,1)S(1)} %slice.5.low_ref.high_ref), custom_call_target="tpu_custom_call" | custom-call | bytes 6291456 | tf_op jit(solution)/shard_map/pallas_call | solution.py:103
  29.5 1.9 %collective-permute-start.2 = (bf16[130,32,128]{2,1,0:T(8,128)(2,1)S(1)}, bf16[130,32,128]{2,1,0:T(8,128)(2,1)}, u32[]{:S(2)}, u32[]{:S(2)}) collective-permute-start(bf16[130,32,128]{2,1,0:T(8,128)(2,1)S(1)} %get-tuple-element.19), channel_id=1, source_target_pairs={{0,1},{1,2},{2,3},{3,4},{4,5},{5,6},{6,7},{7,8},{8,9},{9,10},{10,1... | collective-permute-start | bytes 3194888 | tf_op jit(solution)/shard_map/ppermute | solution.py:503
  31.4 5.8 %collective-permute-start.3 = (bf16[130,32,128]{2,1,0:T(8,128)(2,1)S(1)}, bf16[130,32,128]{2,1,0:T(8,128)(2,1)}, u32[]{:S(2)}, u32[]{:S(2)}) collective-permute-start(bf16[130,32,128]{2,1,0:T(8,128)(2,1)S(1)} %get-tuple-element.20), channel_id=1, source_target_pairs={{1,0},{2,1},{3,2},{4,3},{5,4},{6,5},{7,6},{8,7},{9,8},{10,9},{11,1... | collective-permute-start | bytes 3194888 | tf_op jit(solution)/shard_map/ppermute | solution.py:503
  37.2 0.0 copy-start.6
  37.2 0.1 pad_add_fusion.where_ref
  37.3 0.0 collective-permute-done.mleft_ref.left_ref
  37.3 0.0 collective-permute-done.1.mright_ref.right_ref
  37.4 33.8 %shard_map.88 = (bf16[2304,128]{1,0:T(8,128)(2,1)S(1)}, bf16[2304,128]{1,0:T(8,128)(2,1)S(1)}, f32[2,128,128]{2,1,0:T(8,128)S(1)}) custom-call(s32[2]{0:T(128)S(1)} %pad_add_fusion.where_ref, s32[1,1]{1,0:T(1,128)S(6)} %copy.9.tissue_ref, bf16[384,32,256]{2,1,0:T(8,128)(2,1)} %bitcast.12, bf16[384,32,256]{2,1,0:T(8,128)(2,1)} %bitcast.13, ...), custom_call_target="tpu_custom_call" | custom-call | flops 8589934592 | bytes 8388608 | tf_op jit(solution)/shard_map/pallas_call | solution.py:293
  71.2 3.5 %collective-permute-start.4 = (bf16[2304,128]{1,0:T(8,128)(2,1)S(1)}, bf16[2304,128]{1,0:T(8,128)(2,1)S(1)}, u32[]{:S(2)}, u32[]{:S(2)}) collective-permute-start(bf16[2304,128]{1,0:T(8,128)(2,1)S(1)} %get-tuple-element.24), channel_id=1, source_target_pairs={{0,16},{16,32},{32,48},{48,64},{64,80},{80,96},{96,112},{1,17},{17... | collective-permute-start | bytes 1769480 | tf_op jit(solution)/shard_map/ppermute | solution.py:503
  74.7 6.0 %collective-permute-start.5 = (bf16[2304,128]{1,0:T(8,128)(2,1)S(1)}, bf16[2304,128]{1,0:T(8,128)(2,1)S(1)}, u32[]{:S(2)}, u32[]{:S(2)}) collective-permute-start(bf16[2304,128]{1,0:T(8,128)(2,1)S(1)} %get-tuple-element.25), channel_id=1, source_target_pairs={{16,0},{32,16},{48,32},{64,48},{80,64},{96,80},{112,96},{17,1},{33... | collective-permute-start | bytes 1769480 | tf_op jit(solution)/shard_map/ppermute | solution.py:503
  80.7 0.0 collective-permute-done.2.left_ref
  80.7 51.4 %shard_map.87 = (f32[64,128,128]{2,1,0:T(8,128)}, f32[2,128,128]{2,1,0:T(8,128)}) custom-call(s32[2]{0:T(128)} %copy-done.7, s32[1,1]{1,0:T(1,128)S(6)} %copy.9.tissue_ref, bf16[384,32,256]{2,1,0:T(8,128)(2,1)} %bitcast.14, bf16[256,32,256]{2,1,0:T(8,128)(2,1)} %copy-done.2, bf16[256,32,256]{2,1,0:T(8,128)(2,1)} %copy-done.2, ...), custom_call_target="tpu_custom_call" | custom-call | flops 17179869184 | bytes 12582912 | tf_op jit(solution)/shard_map/pallas_call | solution.py:372
  132.1 2.2 %copy-done.3 = f32[64,128,128]{2,1,0:T(8,128)S(1)} copy-done((f32[64,128,128]{2,1,0:T(8,128)S(1)}, f32[64,128,128]{2,1,0:T(8,128)}, u32[]{:S(2)}) %copy-start.3) | copy-done | bytes 4194328
  134.3 0.9 copy-done.5
  135.2 11.3 %shard_map.89 = (f32[8192,128]{1,0:T(8,128)}, f32[256,128]{1,0:T(8,128)}, f32[128,384]{1,0:T(8,128)S(1)}, f32[8,384]{1,0:T(8,128)S(1)}, f32[8,384]{1,0:T(8,128)S(1)}) custom-call(s32[2]{0:T(128)S(1)} %copy-done.8, f32[64,128,128]{2,1,0:T(8,128)S(1)} %copy-done.3, f32[2,128,128]{2,1,0:T(8,128)S(1)} %copy-done.5, ...), custom_call_target="tpu_custom_call" | custom-call | bytes 10485760 | tf_op jit(solution)/shard_map/pallas_call | solution.py:457
  146.5 0.7 copy-done.4
  147.2 1.9 %collective-permute-start.6 = (f32[8,384]{1,0:T(8,128)S(1)}, f32[8,384]{1,0:T(8,128)S(1)}, u32[]{:S(2)}, u32[]{:S(2)}) collective-permute-start(f32[8,384]{1,0:T(8,128)S(1)} %get-tuple-element.29), channel_id=1, source_target_pairs={{0,1},{1,2},{2,3},{3,4},{4,5},{5,6},{6,7},{7,8},{8,9},{9,10},{10,1... | collective-permute-start | bytes 36872 | tf_op jit(solution)/shard_map/ppermute | solution.py:503
  149.1 5.8 %collective-permute-start.7 = (f32[8,384]{1,0:T(8,128)S(1)}, f32[8,384]{1,0:T(8,128)S(1)}, u32[]{:S(2)}, u32[]{:S(2)}) collective-permute-start(f32[8,384]{1,0:T(8,128)S(1)} %get-tuple-element.30), channel_id=1, source_target_pairs={{1,0},{2,1},{3,2},{4,3},{5,4},{6,5},{7,6},{8,7},{9,8},{10,9},{11,1... | collective-permute-start | bytes 36872 | tf_op jit(solution)/shard_map/ppermute | solution.py:503
  154.9 1.4 collective-permute-done.7.east_ref
  156.3 0.6 copy-done.15
  156.9 2.0 %shard_map.90 = f32[256,128]{1,0:T(8,128)} custom-call(f32[128,384]{1,0:T(8,128)} %copy-done.4, f32[8,384]{1,0:T(8,128)} %copy-done.14, f32[8,384]{1,0:T(8,128)} %copy-done.15), custom_call_target="tpu_custom_call" | custom-call | tf_op jit(solution)/shard_map/pallas_call | solution.py:491
  (27 shorter events, 0.1 us)
Async XLA Ops:
  1.3 2.8 %copy-start = (bf16[384,256,32]{1,2,0:T(8,128)(2,1)S(1)}, bf16[384,256,32]{1,2,0:T(8,128)(2,1)}, u32[]{:S(2)}) copy-start(bf16[384,256,32]{1,2,0:T(8,128)(2,1)} %param.6) | copy-start | bytes 18874372
  4.1 14.6 %copy-start.1 = (bf16[384,256,32]{1,2,0:T(8,128)(2,1)S(1)}, bf16[384,256,32]{1,2,0:T(8,128)(2,1)}, u32[]{:S(2)}) copy-start(bf16[384,256,32]{1,2,0:T(8,128)(2,1)} %param.6) | copy-start | bytes 18874372
  11.0 26.3 %collective-permute-start = (bf16[76,32,128]{2,1,0:T(8,128)(2,1)}, bf16[76,32,128]{2,1,0:T(8,128)(2,1)S(1)}, u32[]{:S(2)}, u32[]{:S(2)}) collective-permute-start(bf16[76,32,128]{2,1,0:T(8,128)(2,1)} %get-tuple-element.17), channel_id=1, source_target_pairs={{0,1},{1,2},{2,3},{3,4},{4,5},{5,6},{6,7},{7,8},{8,9},{9,10},{10,1... | collective-permute-start | bytes 1867784 | tf_op jit(solution)/shard_map/ppermute | solution.py:503
  12.9 24.4 %collective-permute-start.1 = (bf16[76,32,128]{2,1,0:T(8,128)(2,1)}, bf16[76,32,128]{2,1,0:T(8,128)(2,1)S(1)}, u32[]{:S(2)}, u32[]{:S(2)}) collective-permute-start(bf16[76,32,128]{2,1,0:T(8,128)(2,1)} %get-tuple-element.18), channel_id=1, source_target_pairs={{1,0},{2,1},{3,2},{4,3},{5,4},{6,5},{7,6},{8,7},{9,8},{10,9},{11,1... | collective-permute-start | bytes 1867784 | tf_op jit(solution)/shard_map/ppermute | solution.py:503
  19.1 10.4 %copy-start.2 = (bf16[256,32,256]{2,1,0:T(8,128)(2,1)}, bf16[256,32,256]{2,1,0:T(8,128)(2,1)S(1)}, u32[]{:S(2)}) copy-start(bf16[256,32,256]{2,1,0:T(8,128)(2,1)S(1)} %slice.5.low_ref.high_ref) | copy-start | bytes 12582916
  19.1 18.1 %copy-start.16 = (f32[33]{0:T(128)S(1)}, f32[33]{0:T(128)}, u32[]{:S(2)}) copy-start(f32[33]{0:T(128)} %param.10) | copy-start | bytes 400
  19.1 18.2 %copy-start.11 = (bf16[3,3,32,128]{3,2,1,0:T(8,128)(2,1)S(1)}, bf16[3,3,32,128]{3,2,1,0:T(8,128)(2,1)}, u32[]{:S(2)}) copy-start(bf16[3,3,32,128]{3,2,1,0:T(8,128)(2,1)} %param.7) | copy-start | bytes 221188
  19.2 18.2 %copy-start.12 = (bf16[128,33]{0,1:T(8,128)(2,1)S(1)}, bf16[128,33]{0,1:T(8,128)(2,1)}, u32[]{:S(2)}) copy-start(bf16[128,33]{0,1:T(8,128)(2,1)} %param.9) | copy-start | bytes 25348
  19.2 18.2 %copy-start.13 = (f32[128]{0:T(128)S(1)}, f32[128]{0:T(128)}, u32[]{:S(2)}) copy-start(f32[128]{0:T(128)} %param.8) | copy-start | bytes 1540
  29.5 51.2 %collective-permute-start.2 = (bf16[130,32,128]{2,1,0:T(8,128)(2,1)S(1)}, bf16[130,32,128]{2,1,0:T(8,128)(2,1)}, u32[]{:S(2)}, u32[]{:S(2)}) collective-permute-start(bf16[130,32,128]{2,1,0:T(8,128)(2,1)S(1)} %get-tuple-element.19), channel_id=1, source_target_pairs={{0,1},{1,2},{2,3},{3,4},{4,5},{5,6},{6,7},{7,8},{8,9},{9,10},{10,1... | collective-permute-start | bytes 3194888 | tf_op jit(solution)/shard_map/ppermute | solution.py:503
  31.4 49.3 %collective-permute-start.3 = (bf16[130,32,128]{2,1,0:T(8,128)(2,1)S(1)}, bf16[130,32,128]{2,1,0:T(8,128)(2,1)}, u32[]{:S(2)}, u32[]{:S(2)}) collective-permute-start(bf16[130,32,128]{2,1,0:T(8,128)(2,1)S(1)} %get-tuple-element.20), channel_id=1, source_target_pairs={{1,0},{2,1},{3,2},{4,3},{5,4},{6,5},{7,6},{8,7},{9,8},{10,9},{11,1... | collective-permute-start | bytes 3194888 | tf_op jit(solution)/shard_map/ppermute | solution.py:503
  37.2 34.0 %copy-start.6 = (f32[8,128]{1,0:T(8,128)}, f32[8,128]{1,0:T(8,128)S(1)}, u32[]{:S(2)}) copy-start(f32[8,128]{1,0:T(8,128)S(1)} %pad.4.hbias_ref) | copy-start | bytes 12292
  37.3 33.9 %copy-start.7 = (s32[2]{0:T(128)}, s32[2]{0:T(128)S(1)}, u32[]{:S(2)}) copy-start(s32[2]{0:T(128)S(1)} %pad_add_fusion.where_ref) | copy-start | bytes 28
  37.3 33.9 %copy-start.9 = (bf16[76,32,128]{2,1,0:T(8,128)(2,1)}, bf16[76,32,128]{2,1,0:T(8,128)(2,1)S(1)}, u32[]{:S(2)}) copy-start(bf16[76,32,128]{2,1,0:T(8,128)(2,1)S(1)} %collective-permute-done.mleft_ref.left_ref) | copy-start | bytes 1867780
  37.3 33.9 %copy-start.10 = (bf16[76,32,128]{2,1,0:T(8,128)(2,1)}, bf16[76,32,128]{2,1,0:T(8,128)(2,1)S(1)}, u32[]{:S(2)}) copy-start(bf16[76,32,128]{2,1,0:T(8,128)(2,1)S(1)} %collective-permute-done.1.mright_ref.right_ref) | copy-start | bytes 1867780
  71.2 60.9 %collective-permute-start.4 = (bf16[2304,128]{1,0:T(8,128)(2,1)S(1)}, bf16[2304,128]{1,0:T(8,128)(2,1)S(1)}, u32[]{:S(2)}, u32[]{:S(2)}) collective-permute-start(bf16[2304,128]{1,0:T(8,128)(2,1)S(1)} %get-tuple-element.24), channel_id=1, source_target_pairs={{0,16},{16,32},{32,48},{48,64},{64,80},{80,96},{96,112},{1,17},{17... | collective-permute-start | bytes 1769480 | tf_op jit(solution)/shard_map/ppermute | solution.py:503
  74.7 57.4 %copy-start.8 = (s32[2]{0:T(128)S(1)}, s32[2]{0:T(128)}, u32[]{:S(2)}) copy-start(s32[2]{0:T(128)} %copy-done.7) | copy-start | bytes 28
  74.7 57.4 %collective-permute-start.5 = (bf16[2304,128]{1,0:T(8,128)(2,1)S(1)}, bf16[2304,128]{1,0:T(8,128)(2,1)S(1)}, u32[]{:S(2)}, u32[]{:S(2)}) collective-permute-start(bf16[2304,128]{1,0:T(8,128)(2,1)S(1)} %get-tuple-element.25), channel_id=1, source_target_pairs={{16,0},{32,16},{48,32},{64,48},{80,64},{96,80},{112,96},{17,1},{33... | collective-permute-start | bytes 1769480 | tf_op jit(solution)/shard_map/ppermute | solution.py:503
  132.1 2.2 %copy-start.3 = (f32[64,128,128]{2,1,0:T(8,128)S(1)}, f32[64,128,128]{2,1,0:T(8,128)}, u32[]{:S(2)}) copy-start(f32[64,128,128]{2,1,0:T(8,128)} %get-tuple-element.21.rays_ref) | copy-start | bytes 12582916
  134.3 0.9 copy-start.5
  146.5 0.7 copy-start.4
  147.2 7.7 %collective-permute-start.6 = (f32[8,384]{1,0:T(8,128)S(1)}, f32[8,384]{1,0:T(8,128)S(1)}, u32[]{:S(2)}, u32[]{:S(2)}) collective-permute-start(f32[8,384]{1,0:T(8,128)S(1)} %get-tuple-element.29), channel_id=1, source_target_pairs={{0,1},{1,2},{2,3},{3,4},{4,5},{5,6},{6,7},{7,8},{8,9},{9,10},{10,1... | collective-permute-start | bytes 36872 | tf_op jit(solution)/shard_map/ppermute | solution.py:503
  149.1 7.1 %collective-permute-start.7 = (f32[8,384]{1,0:T(8,128)S(1)}, f32[8,384]{1,0:T(8,128)S(1)}, u32[]{:S(2)}, u32[]{:S(2)}) collective-permute-start(f32[8,384]{1,0:T(8,128)S(1)} %get-tuple-element.30), channel_id=1, source_target_pairs={{1,0},{2,1},{3,2},{4,3},{5,4},{6,5},{7,6},{8,7},{9,8},{10,9},{11,1... | collective-permute-start | bytes 36872 | tf_op jit(solution)/shard_map/ppermute | solution.py:503
  154.9 1.4 copy-start.14
  156.3 0.6 copy-start.15

commit v2 on v1

--- a/solution.py
+++ b/solution.py
@@ -12,9 +12,13 @@
 CORE_H, CORE_W = 256, 128
 N_ROWS, N_COLS = 8, 16
 CIN, COUT, RAYS = 32, 128, 32
-M_PAIRS = 73
-C_PAIRS = 128
-M_OUT = 72
+M_PAIRS = 74
+C_PAIRS = 130
+CHUNK = 8
+SPAN = CHUNK + 2
+M_CHUNKS = 9
+C_CHUNKS = 16
+M_OUT = M_CHUNKS * CHUNK
 TAPS = 3 * CIN
 F32, BF16 = jnp.float32, jnp.bfloat16
 
@@ -29,38 +33,40 @@
     return jnp.exp(-(centred * centred) / (2.0 * spread * spread))
 
 
-def pack_pair(lo, hi, t, right_ref, left_ref, slot, extras):
+def pack_pair(lo, hi, slot, right_ref, left_ref, extras):
     low_half = lanes_of((CIN, 128)) < 64
-    spot = lanes_of((CIN, 128)) == t
+    place = lax.rem(slot, 128)
+    spot = lanes_of((CIN, 128)) == place
     west_lo, east_lo = lo[:, :128], lo[:, 128:]
     west_hi, east_hi = hi[:, :128], hi[:, 128:]
     right_ref[slot] = jnp.where(low_half, pltpu.roll(east_lo, 64, 1), east_hi)
     left_ref[slot] = jnp.where(low_half, west_hi, pltpu.roll(west_lo, 64, 1))
-    to_t_east = lax.rem(t + 128 - 63, 128)
-    to_t_west = lax.rem(t + 128 - 64, 128)
+    to_east = lax.rem(place + 128 - 63, 128)
+    to_west = lax.rem(place + 128 - 64, 128)
     return (
-        jnp.where(spot, pltpu.roll(east_lo, to_t_east, 1), extras[0]),
-        jnp.where(spot, pltpu.roll(east_hi, to_t_east, 1), extras[1]),
-        jnp.where(spot, pltpu.roll(west_lo, to_t_west, 1), extras[2]),
-        jnp.where(spot, pltpu.roll(west_hi, to_t_west, 1), extras[3]),
+        jnp.where(spot, pltpu.roll(east_lo, to_east, 1), extras[0]),
+        jnp.where(spot, pltpu.roll(east_hi, to_east, 1), extras[1]),
+        jnp.where(spot, pltpu.roll(west_lo, to_west, 1), extras[2]),
+        jnp.where(spot, pltpu.roll(west_hi, to_west, 1), extras[3]),
     )
 
 
 def pack_margin_kernel(tissue_ref, top_ref, bottom_ref, right_ref, left_ref):
     zero = jnp.zeros((CIN, 128), BF16)
+    right_ref[0] = zero
+    left_ref[0] = zero
 
     def step(t, extras):
-        return pack_pair(top_ref[t], bottom_ref[95 - t], t, right_ref, left_ref, t, extras)
-
-    extras = lax.fori_loop(0, M_PAIRS, step, (zero, zero, zero, zero))
+        return pack_pair(top_ref[t], bottom_ref[95 - t], t + 1, right_ref, left_ref, extras)
+
+    extras = lax.fori_loop(0, M_PAIRS - 2, step, (zero,) * 4, unroll=8)
+    extras = step(M_PAIRS - 2, extras)
     flag = jnp.where(tissue_ref[0, 0] > 0, 1.0, 0.0)
     flags = jnp.full((CIN, 128), flag, F32).astype(BF16)
-    right_ref[M_PAIRS] = extras[0]
-    right_ref[M_PAIRS + 1] = extras[1]
-    right_ref[M_PAIRS + 2] = flags
-    left_ref[M_PAIRS] = extras[2]
-    left_ref[M_PAIRS + 1] = extras[3]
-    left_ref[M_PAIRS + 2] = flags
+    for ref, lo, hi in ((right_ref, extras[0], extras[1]), (left_ref, extras[2], extras[3])):
+        ref[M_PAIRS] = lo
+        ref[M_PAIRS + 1] = hi
+        ref[M_PAIRS + 2] = flags
 
 
 def pack_margin(tissue, features):
@@ -75,43 +81,40 @@
         ],
         out_specs=[pl.BlockSpec(shape.shape, lambda s: (0, 0, 0))] * 2,
         out_shape=[shape, shape],
-        compiler_params=pltpu.CompilerParams(vmem_limit_bytes=32 << 20),
+        compiler_params=pltpu.CompilerParams(vmem_limit_bytes=60 << 20),
         cost_estimate=pl.CostEstimate(flops=0, bytes_accessed=5 << 20, transcendentals=0),
     )(tissue, features, features)
 
 
-def pack_core_kernel(low_ref, high_ref, right_ref, left_ref):
+def pack_core_kernel(features_ref, right_ref, left_ref):
     zero = jnp.zeros((CIN, 128), BF16)
 
-    def step(t, extras):
-        q = lax.div(t, 64)
-        s = lax.rem(t, 64)
+    def step(slot, extras):
         return pack_pair(
-            low_ref[t], high_ref[127 - t], t, right_ref, left_ref, t, extras
+            features_ref[MARGIN - 1 + slot], features_ref[EXT_H - MARGIN - slot], slot,
+            right_ref, left_ref, extras,
         )
 
-    extras = lax.fori_loop(0, C_PAIRS, step, (zero, zero, zero, zero))
-    right_ref[C_PAIRS] = extras[0]
-    right_ref[C_PAIRS + 1] = extras[1]
-    left_ref[C_PAIRS] = extras[2]
-    left_ref[C_PAIRS + 1] = extras[3]
+    extras = lax.fori_loop(0, 128, step, (zero,) * 4, unroll=8)
+    more = lax.fori_loop(128, C_PAIRS, step, (zero,) * 4, unroll=2)
+    for ref, k in ((right_ref, 0), (left_ref, 2)):
+        ref[C_PAIRS] = extras[k]
+        ref[C_PAIRS + 1] = more[k]
+        ref[C_PAIRS + 2] = extras[k + 1]
+        ref[C_PAIRS + 3] = more[k + 1]
 
 
 def pack_core(features):
-    shape = jax.ShapeDtypeStruct((C_PAIRS + 2, CIN, 128), BF16)
-    core = features[MARGIN : EXT_H - MARGIN]
+    shape = jax.ShapeDtypeStruct((C_PAIRS + 4, CIN, 128), BF16)
+    vmem = pl.BlockSpec(memory_space=pltpu.VMEM)
     return pl.pallas_call(
         pack_core_kernel,
-        grid=(1,),
-        in_specs=[
-            pl.BlockSpec((128, CIN, EXT_W), lambda s: (0, 0, 0)),
-            pl.BlockSpec((128, CIN, EXT_W), lambda s: (1, 0, 0)),
-        ],
-        out_specs=[pl.BlockSpec(shape.shape, lambda s: (0, 0, 0))] * 2,
+        in_specs=[vmem],
+        out_specs=[vmem, vmem],
         out_shape=[shape, shape],
         compiler_params=pltpu.CompilerParams(vmem_limit_bytes=32 << 20),
         cost_estimate=pl.CostEstimate(flops=0, bytes_accessed=6 << 20, transcendentals=0),
-    )(core, core)
+    )(features)
 
 
 def column_taps(own, strip, from_west, from_east):
@@ -136,20 +139,61 @@
     )
 
 
-def build_pair(own_lo, own_hi, left, right, extras, t, taps_ref, lo_index, hi_index):
+def build_pair(own_lo, own_hi, left, right, extras, slot, lo_ref, hi_ref, place):
     low_half = lanes_of((CIN, 128)) < 64
     strip_lo = jnp.where(low_half, left, right)
     strip_hi = pltpu.roll(jnp.where(low_half, right, left), 64, 1)
-    to_first = lax.rem(128 - t, 128)
-    to_last = 127 - t
-    for own, strip, west, east, index in (
-        (own_lo, strip_lo, extras[0], extras[2], lo_index),
-        (own_hi, strip_hi, extras[1], extras[3], hi_index),
+    lane = lax.rem(slot, 128)
+    to_first = lax.rem(128 - lane, 128)
+    to_last = 127 - lane
+    for own, strip, west, east, ref, row in (
+        (own_lo, strip_lo, extras[0], extras[2], lo_ref, place),
+        (own_hi, strip_hi, extras[1], extras[3], hi_ref, SPAN - 1 - place),
     ):
         parts = column_taps(own, strip, pltpu.roll(west, to_first, 1), pltpu.roll(east, to_last, 1))
-        start = pl.multiple_of(index * TAPS, 32)
         for k, part in enumerate(parts):
-            taps_ref[pl.ds(start + k * CIN, CIN), :] = part
+            ref[row * TAPS + k * CIN : row * TAPS + (k + 1) * CIN, :] = part
+
+
+def build_chunk(chunk, first, pair, lo_ref, hi_ref):
+    for place in range(first, SPAN):
+        slot = chunk * CHUNK + place
+        own_lo, own_hi, left, right, extras = pair(slot)
+        build_pair(own_lo, own_hi, left, right, extras, slot, lo_ref, hi_ref, place)
+
+
+def next_chunk(chunk, pair, lo_ref, hi_ref, next_lo_ref, next_hi_ref):
+    next_lo_ref[0 : 2 * TAPS, :] = lo_ref[CHUNK * TAPS :, :]
+    next_hi_ref[CHUNK * TAPS :, :] = hi_ref[0 : 2 * TAPS, :]
+    build_chunk(chunk + 1, 2, pair, next_lo_ref, next_hi_ref)
+
+
+def chunk_logits(lo_ref, hi_ref, conv_scr, head_scr, bias):
+    return [
+        [group_logits(ref, 4 * u, conv_scr, head_scr, bias) for u in range(2)]
+        for ref in (lo_ref, hi_ref)
+    ]
+
+
+def walk(chunks, pair, refs, use):
+    even, odd = refs[0:2], refs[2:4]
+
+    def two(i, carry):
+        use(2 * i, *even)
+        next_chunk(2 * i, pair, *even, *odd)
+        use(2 * i + 1, *odd)
+        next_chunk(2 * i + 1, pair, *odd, *even)
+        return carry
+
+    if chunks > 2:
+        lax.fori_loop(0, (chunks - 1) // 2, two, 0)
+    last = chunks - 1
+    if chunks % 2:
+        use(last, *even)
+    else:
+        use(last - 1, *even)
+        next_chunk(last - 1, pair, *even, *odd)
+        use(last, *odd)
 
 
 def prepare_weights(conv_ref, head_ref, bias_ref, conv_scr, head_scr):
@@ -203,9 +247,9 @@
 def group_logits(taps_ref, base, conv_scr, head_scr, bias):
     hidden = []
     for pair in range(2):
-        start = pl.multiple_of((base + 2 * pair) * TAPS, 64)
+        start = (base + 2 * pair) * TAPS
         summed = lax.dot_general(
-            taps_ref[pl.ds(start, 4 * TAPS), :],
+            taps_ref[start : start + 4 * TAPS, :],
             conv_scr[...],
             (((0,), (0,)), ((), ())),
             preferred_element_type=F32,
@@ -224,27 +268,37 @@
     )
 
 
+def weighted_rays(logits, ray_bias, own_weight, side_weight, first_row, tile_row):
+    quarter = lax.div(lanes_of((1, 128)), RAYS)
+    factor = row_weights(first_row + quarter, tile_row)
+    return (
+        (logits[:CORE_W, :128] + ray_bias) * own_weight
+        + (logits[CORE_W:, :128] + ray_bias) * side_weight
+    ) * factor
+
+
+def add_probability(logit_ref, block, logits, first_lane):
+    both = logits[0][:, 128:] + pltpu.roll(logits[1][:, 128:], 4, 1)
+    logit_ref[block] += pltpu.roll(both, first_lane, 1)
+
+
 def margin_kernel(
     where_ref, tissue_ref, top_ref, bottom_ref, left_ref, right_ref,
     conv_ref, bias_ref, head_ref, hbias_ref,
     up_ref, down_ref, edge_ref,
-    taps_ref, logit_ref, conv_scr, head_scr,
+    lo0_ref, hi0_ref, lo1_ref, hi1_ref, logit_ref, conv_scr, head_scr,
 ):
     tile_row, tile_col = where_ref[0], where_ref[1]
     prepare_weights(conv_ref, head_ref, bias_ref, conv_scr, head_scr)
-    second = M_PAIRS + 1
-    taps_ref[0:TAPS, :] = jnp.zeros((TAPS, 256), BF16)
-    taps_ref[(2 * M_PAIRS + 1) * TAPS : (2 * M_PAIRS + 2) * TAPS, :] = jnp.zeros((TAPS, 256), BF16)
     extras = (left_ref[M_PAIRS], left_ref[M_PAIRS + 1], right_ref[M_PAIRS], right_ref[M_PAIRS + 1])
 
-    def build(t, carry):
-        build_pair(
-            top_ref[t], bottom_ref[95 - t], left_ref[t], right_ref[t], extras, t,
-            taps_ref, t + 1, second + 72 - t,
-        )
-        return carry
-
-    lax.fori_loop(0, M_PAIRS, build, 0)
+    def pair(slot):
+        row = slot - 1 if isinstance(slot, jax.Array) else max(slot - 1, 0)
+        return top_ref[row], bottom_ref[95 - row], left_ref[slot], right_ref[slot], extras
+
+    build_chunk(0, 0, pair, lo0_ref, hi0_ref)
+    lo0_ref[0:TAPS, :] = jnp.zeros((TAPS, 256), BF16)
+    hi0_ref[(SPAN - 1) * TAPS :, :] = jnp.zeros((TAPS, 256), BF16)
     own_weight, side_weight = column_weights(
         tile_col, tissue_ref[0, 0],
         left_ref[M_PAIRS + 2].astype(F32), right_ref[M_PAIRS + 2].astype(F32),
@@ -252,29 +306,26 @@
     bias = jnp.concatenate([bias_ref[...], bias_ref[...]], axis=1)
     ray_bias = spread_bias(hbias_ref[...])
     logit_ref[...] = jnp.zeros(logit_ref.shape, F32)
-    quarter = lax.div(lanes_of((1, 128)), RAYS)
-
-    def compute(g, carry):
-        for block, first_row, base in ((0, 0, 0), (1, 312, second)):
-            logits = group_logits(taps_ref, base + 4 * g, conv_scr, head_scr, bias)
-            factor = row_weights(first_row + 4 * g + quarter, tile_row)
-            rays = (
-                (logits[:CORE_W, :128] + ray_bias) * own_weight
-                + (logits[CORE_W:, :128] + ray_bias) * side_weight
-            ) * factor
-            logit_ref[block] += pltpu.roll(logits[:, 128:], 4 * g, 1)
-            if block == 0:
-                @pl.when(g < 16)
-                def _():
-                    up_ref[pl.ds(pl.multiple_of(g * 128, 128), 128), :] = rays.astype(BF16)
-            else:
-                @pl.when(g >= 2)
-                def _():
-                    down_ref[pl.ds(pl.multiple_of((g - 2) * 128, 128), 128), :] = rays.astype(BF16)
-        return carry
-
-    lax.fori_loop(0, M_OUT // 4, compute, 0)
-    for block, first_row, ref in ((0, 0, up_ref), (1, 312, down_ref)):
+
+    def use(chunk, lo_ref, hi_ref):
+        lo, hi = chunk_logits(lo_ref, hi_ref, conv_scr, head_scr, bias)
+        for u in range(2):
+            start = pl.multiple_of((2 * chunk + u) * 128, 128)
+            first_row = CHUNK * chunk + 4 * u
+            up_ref[pl.ds(start, 128), :] = weighted_rays(
+                lo[u], ray_bias, own_weight, side_weight, first_row, tile_row
+            ).astype(BF16)
+            first_row = EXT_H - CHUNK * (chunk + 1) + 4 * u
+            group = 14 - 2 * chunk + u
+            start = pl.multiple_of(jnp.where(group < 0, group + 18, group) * 128, 128)
+            down_ref[pl.ds(start, 128), :] = weighted_rays(
+                hi[u], ray_bias, own_weight, side_weight, first_row, tile_row
+            ).astype(BF16)
+        add_probability(logit_ref, 0, lo, CHUNK * chunk)
+        add_probability(logit_ref, 1, hi, M_OUT - CHUNK * (chunk + 1))
+
+    walk(M_CHUNKS, pair, (lo0_ref, hi0_ref, lo1_ref, hi1_ref), use)
+    for block, first_row, ref in ((0, 0, up_ref), (1, EXT_H - M_OUT, down_ref)):
         prob = probability_block(
             logit_ref[block], hbias_ref[0, 0], first_row, tile_row, own_weight, side_weight
         )
@@ -283,6 +334,14 @@
         high = prob.astype(BF16)
         ref[2048:2176, :] = high
         ref[2176:2304, :] = (prob - high.astype(F32)).astype(BF16)
+
+
+def conv_scratch():
+    return [pltpu.VMEM((SPAN * TAPS, 256), BF16)] * 4 + [
+        pltpu.VMEM((2, 256, 128), F32),
+        pltpu.VMEM((4 * TAPS, 256), BF16),
+        pltpu.VMEM((4 * COUT, 256), BF16),
+    ]
 
 
 def margin_outputs(where, tissue, features, left, right, weights):
@@ -301,63 +360,52 @@
         ],
         out_specs=[vmem, vmem, vmem],
         out_shape=[shape, shape, edge],
-        scratch_shapes=[
-            pltpu.VMEM(((2 * M_PAIRS + 2) * TAPS, 256), BF16),
-            pltpu.VMEM((2, 256, 128), F32),
-            pltpu.VMEM((4 * TAPS, 256), BF16),
-            pltpu.VMEM((4 * COUT, 256), BF16),
-        ],
-        compiler_params=pltpu.CompilerParams(vmem_limit_bytes=48 << 20),
+        scratch_shapes=conv_scratch(),
+        compiler_params=pltpu.CompilerParams(vmem_limit_bytes=32 << 20),
         cost_estimate=pl.CostEstimate(flops=8 << 30, bytes_accessed=8 << 20, transcendentals=0),
     )(where, tissue, features, features, left, right, *weights)
 
 
 def core_kernel(
-    where_ref, tissue_ref, before_ref, low_ref, high_ref, after_ref, mleft_ref, mright_ref,
-    left_ref, right_ref, conv_ref, bias_ref, head_ref, hbias_ref,
+    where_ref, tissue_ref, features_ref, mleft_ref, mright_ref, left_ref, right_ref,
+    conv_ref, bias_ref, head_ref, hbias_ref,
     rays_ref, prob_ref,
-    taps_ref, logit_ref, conv_scr, head_scr,
+    lo0_ref, hi0_ref, lo1_ref, hi1_ref, logit_ref, conv_scr, head_scr,
 ):
     tile_row, tile_col = where_ref[0], where_ref[1]
     prepare_weights(conv_ref, head_ref, bias_ref, conv_scr, head_scr)
-    extras = (mleft_ref[M_PAIRS], mleft_ref[M_PAIRS + 1], mright_ref[M_PAIRS], mright_ref[M_PAIRS + 1])
-    build_pair(
-        before_ref[0], after_ref[0], mleft_ref[63], mright_ref[63], extras, 63,
-        taps_ref, 0, 257,
-    )
-    extras = (left_ref[C_PAIRS], left_ref[C_PAIRS + 1], right_ref[C_PAIRS], right_ref[C_PAIRS + 1])
-
-    def build(t, carry):
-        build_pair(
-            low_ref[t], high_ref[127 - t], left_ref[t], right_ref[t], extras, t,
-            taps_ref, 1 + t, 256 - t,
+
+    def pair(slot):
+        block = C_PAIRS + slot // 128
+        extras = (left_ref[block], left_ref[block + 2], right_ref[block], right_ref[block + 2])
+        return (
+            features_ref[MARGIN - 1 + slot], features_ref[EXT_H - MARGIN - slot],
+            left_ref[slot], right_ref[slot], extras,
         )
-        return carry
-
-    lax.fori_loop(0, C_PAIRS, build, 0)
+
+    build_chunk(0, 0, pair, lo0_ref, hi0_ref)
     own_weight, side_weight = column_weights(
-        tile_col, tissue_ref[0, 0],
-        mleft_ref[M_PAIRS + 2].astype(F32), mright_ref[M_PAIRS + 2].astype(F32),
+        tile_col, tissue_ref[0, 0], mleft_ref[0].astype(F32), mright_ref[0].astype(F32)
     )
     bias = jnp.concatenate([bias_ref[...], bias_ref[...]], axis=1)
     ray_bias = spread_bias(hbias_ref[...])
     logit_ref[...] = jnp.zeros(logit_ref.shape, F32)
-    quarter = lax.div(lanes_of((1, 128)), RAYS)
-
-    def compute(h, carry):
-        for block in range(2):
-            g = block * 32 + h
-            logits = group_logits(taps_ref, 4 * g, conv_scr, head_scr, bias)
-            factor = row_weights(MARGIN + 4 * g + quarter, tile_row)
-            rays = (
-                (logits[:CORE_W, :128] + ray_bias) * own_weight
-                + (logits[CORE_W:, :128] + ray_bias) * side_weight
-            ) * factor
-            rays_ref[g] = rays
-            logit_ref[block] += pltpu.roll(logits[:, 128:], 4 * h, 1)
-        return carry
-
-    lax.fori_loop(0, 32, compute, 0)
+
+    def use(chunk, lo_ref, hi_ref):
+        lo, hi = chunk_logits(lo_ref, hi_ref, conv_scr, head_scr, bias)
+        for u in range(2):
+            group = 2 * chunk + u
+            rays_ref[group] = weighted_rays(
+                lo[u], ray_bias, own_weight, side_weight, MARGIN + 4 * group, tile_row
+            )
+            group = 62 - 2 * chunk + u
+            rays_ref[group] = weighted_rays(
+                hi[u], ray_bias, own_weight, side_weight, MARGIN + 4 * group, tile_row
+            )
+        add_probability(logit_ref, 0, lo, CHUNK * chunk)
+        add_probability(logit_ref, 1, hi, 128 - CHUNK * (chunk + 1))
+
+    walk(C_CHUNKS, pair, (lo0_ref, hi0_ref, lo1_ref, hi1_ref), use)
     for block in range(2):
         prob_ref[block] = probability_block(
             logit_ref[block], hbias_ref[0, 0], MARGIN + 128 * block, tile_row,
@@ -368,32 +416,20 @@
 def core_outputs(where, tissue, features, mleft, mright, left, right, weights):
     smem = pl.BlockSpec(memory_space=pltpu.SMEM)
     vmem = pl.BlockSpec(memory_space=pltpu.VMEM)
-    core = features[MARGIN : EXT_H - MARGIN]
+    flag = pl.BlockSpec((1, CIN, 128), lambda s: (M_PAIRS + 2, 0, 0))
     return pl.pallas_call(
         core_kernel,
         grid=(1,),
-        in_specs=[
-            smem, smem,
-            pl.BlockSpec((1, CIN, EXT_W), lambda s: (63, 0, 0)),
-            pl.BlockSpec((128, CIN, EXT_W), lambda s: (0, 0, 0)),
-            pl.BlockSpec((128, CIN, EXT_W), lambda s: (1, 0, 0)),
-            pl.BlockSpec((1, CIN, EXT_W), lambda s: (320, 0, 0)),
-            vmem, vmem, vmem, vmem, vmem, vmem, vmem, vmem,
-        ],
+        in_specs=[smem, smem, vmem, flag, flag, vmem, vmem, vmem, vmem, vmem, vmem],
         out_specs=[vmem, vmem],
         out_shape=[
             jax.ShapeDtypeStruct((64, CORE_W, 128), F32),
             jax.ShapeDtypeStruct((2, CORE_W, 128), F32),
         ],
-        scratch_shapes=[
-            pltpu.VMEM((258 * TAPS, 256), BF16),
-            pltpu.VMEM((2, 256, 128), F32),
-            pltpu.VMEM((4 * TAPS, 256), BF16),
-            pltpu.VMEM((4 * COUT, 256), BF16),
-        ],
-        compiler_params=pltpu.CompilerParams(vmem_limit_bytes=56 << 20),
+        scratch_shapes=conv_scratch(),
+        compiler_params=pltpu.CompilerParams(vmem_limit_bytes=40 << 20),
         cost_estimate=pl.CostEstimate(flops=16 << 30, bytes_accessed=12 << 20, transcendentals=0),
-    )(where, tissue, features, core, core, features, mleft, mright, left, right, *weights)
+    )(where, tissue, features, mleft, mright, left, right, *weights)
 
 
 def finish_kernel(

time: 159 us -> 106 us (0.67)
  Pallas kernels: 116 us -> 63 us
    pallas_call x2, Pallas kernels: 61.7 us -> 29.5 us  [the longest x1 25.4 us: core_outputs(): pl.pallas_call(core_kernel, grid=(1,), in_specs=[smem, smem, vmem, flag,...]
    pallas_call x1, Pallas kernels: 33.8 us -> 15.6 us  [margin_outputs(): pl.pallas_call(margin_kernel, grid=(1,), in_specs=[smem, smem, pl.BlockSp...]
    pallas_call x1, Pallas kernels: 6.92 us -> 4.56 us  [pack_margin(): pl.pallas_call(pack_margin_kernel, grid=(1,), in_specs=[pl.BlockSpec(memo...]
    unnamed x34 -> x22, local copies, waits for them, and re-layouts: 7.21 us -> 6.85 us
  transfers between devices with their start and end apart: 8 -> 8, of which waited for: 1 -> 1; matrix products, arithmetic and copies ran while one was open for 0% -> 0% of each run, Pallas kernels for 60% -> 43%
where the time goes in v2:
time: 106 us; the launch traced here: 105 us
  Pallas kernels  63 us (59%)
  starting transfers between devices  32.4 us (31%)
  local copies, waits for them, and re-layouts  6.86 us (6%)
  between operations  1.5 us (1%)
  waiting for transfers between devices  1.38 us (1%)
    ppermute x8, starting transfers between devices, shift(): return lax.ppermute(array, axis, pairs)  32.4 us
    pallas_call x1, Pallas kernels, core_outputs(): pl.pallas_call(core_kernel, grid=(1,), in_specs=[smem, smem, vmem, flag,...  25.4 us
    pallas_call x1, Pallas kernels, margin_outputs(): pl.pallas_call(margin_kernel, grid=(1,), in_specs=[smem, smem, pl.BlockSp...  15.6 us
    pallas_call x1, Pallas kernels, finish(): pl.pallas_call(finish_kernel, in_specs=[smem, vmem, vmem, vmem, vmem, vme...  11.3 us
    unnamed x22, local copies, waits for them, and re-layouts  6.85 us
    pallas_call x1, Pallas kernels, pack_margin(): pl.pallas_call(pack_margin_kernel, grid=(1,), in_specs=[pl.BlockSpec(memo...  4.56 us
    pallas_call x1, Pallas kernels, pack_core(): pl.pallas_call(pack_core_kernel, in_specs=[vmem], out_specs=[vmem, vmem],...  4.15 us
  transfers between devices with their start and end apart: 8, of which 1 were waited for; matrix products, arithmetic and copies ran while one was open for 0% of the time, Pallas kernels for 43%

profile of v2, /device:TPU:6, one launch (start us, length us, event | category | flops | bytes accessed | tf_op | source)
XLA Modules:
  0.0 105.3 jit_solution(2235425579199842770)
XLA Ops:
  1.3 4.6 %shard_map.85 = (bf16[77,32,128]{2,1,0:T(8,128)(2,1)}, bf16[77,32,128]{2,1,0:T(8,128)(2,1)}) custom-call(s32[1,1]{1,0:T(1,128)S(6)} %copy.9.tissue_ref, bf16[384,32,256]{2,1,0:T(8,128)(2,1)} %bitcast.12, bf16[384,32,256]{2,1,0:T(8,128)(2,1)} %bitcast.13), custom_call_target="tpu_custom_call" | custom-call | bytes 5242880 | tf_op jit(solution)/shard_map/pallas_call | solution.py:74
  5.8 1.9 %collective-permute-start = (bf16[77,32,128]{2,1,0:T(8,128)(2,1)}, bf16[77,32,128]{2,1,0:T(8,128)(2,1)}, u32[]{:S(2)}, u32[]{:S(2)}) collective-permute-start(bf16[77,32,128]{2,1,0:T(8,128)(2,1)} %get-tuple-element.17), channel_id=1, source_target_pairs={{0,1},{1,2},{2,3},{3,4},{4,5},{5,6},{6,7},{7,8},{8,9},{9,10},{10,1... | collective-permute-start | bytes 1892360 | tf_op jit(solution)/shard_map/ppermute | solution.py:539
  7.8 5.8 %collective-permute-start.1 = (bf16[77,32,128]{2,1,0:T(8,128)(2,1)}, bf16[77,32,128]{2,1,0:T(8,128)(2,1)}, u32[]{:S(2)}, u32[]{:S(2)}) collective-permute-start(bf16[77,32,128]{2,1,0:T(8,128)(2,1)} %get-tuple-element.18), channel_id=1, source_target_pairs={{1,0},{2,1},{3,2},{4,3},{5,4},{6,5},{7,6},{8,7},{9,8},{10,9},{11,1... | collective-permute-start | bytes 1892360 | tf_op jit(solution)/shard_map/ppermute | solution.py:539
  13.5 0.0 copy-start
  13.5 2.8 %copy-done = bf16[384,256,32]{1,2,0:T(8,128)(2,1)S(1)} copy-done((bf16[384,256,32]{1,2,0:T(8,128)(2,1)S(1)}, bf16[384,256,32]{1,2,0:T(8,128)(2,1)}, u32[]{:S(2)}) %copy-start) | copy-done | bytes 6291480
  16.3 0.0 slice-start
  16.3 4.2 %shard_map.86 = (bf16[134,32,128]{2,1,0:T(8,128)(2,1)}, bf16[134,32,128]{2,1,0:T(8,128)(2,1)}) custom-call(bf16[384,32,256]{2,1,0:T(8,128)(2,1)S(1)} %bitcast.14), custom_call_target="tpu_custom_call" | custom-call | bytes 6291456 | tf_op jit(solution)/shard_map/pallas_call | solution.py:110
  20.5 1.9 %collective-permute-start.2 = (bf16[134,32,128]{2,1,0:T(8,128)(2,1)}, bf16[134,32,128]{2,1,0:T(8,128)(2,1)S(1)}, u32[]{:S(2)}, u32[]{:S(2)}) collective-permute-start(bf16[134,32,128]{2,1,0:T(8,128)(2,1)} %get-tuple-element.19), channel_id=1, source_target_pairs={{0,1},{1,2},{2,3},{3,4},{4,5},{5,6},{6,7},{7,8},{8,9},{9,10},{10,1... | collective-permute-start | bytes 3293192 | tf_op jit(solution)/shard_map/ppermute | solution.py:539
  22.4 5.8 %collective-permute-start.3 = (bf16[134,32,128]{2,1,0:T(8,128)(2,1)}, bf16[134,32,128]{2,1,0:T(8,128)(2,1)}, u32[]{:S(2)}, u32[]{:S(2)}) collective-permute-start(bf16[134,32,128]{2,1,0:T(8,128)(2,1)} %get-tuple-element.20), channel_id=1, source_target_pairs={{1,0},{2,1},{3,2},{4,3},{5,4},{6,5},{7,6},{8,7},{9,8},{10,9},{11,1... | collective-permute-start | bytes 3293192 | tf_op jit(solution)/shard_map/ppermute | solution.py:539
  28.2 0.1 pad_add_fusion.where_ref
  28.3 0.0 collective-permute-done.mleft_ref.left_ref
  28.3 0.0 collective-permute-done.1.mright_ref.right_ref
  28.3 0.0 copy-start.1
  28.3 2.8 %copy-done.1 = bf16[384,256,32]{1,2,0:T(8,128)(2,1)S(1)} copy-done((bf16[384,256,32]{1,2,0:T(8,128)(2,1)S(1)}, bf16[384,256,32]{1,2,0:T(8,128)(2,1)}, u32[]{:S(2)}) %copy-start.1) | copy-done | bytes 6291480
  31.1 15.6 %shard_map.88 = (bf16[2304,128]{1,0:T(8,128)(2,1)S(1)}, bf16[2304,128]{1,0:T(8,128)(2,1)S(1)}, f32[2,128,128]{2,1,0:T(8,128)S(1)}) custom-call(s32[2]{0:T(128)S(1)} %pad_add_fusion.where_ref, s32[1,1]{1,0:T(1,128)S(6)} %copy.9.tissue_ref, bf16[384,32,256]{2,1,0:T(8,128)(2,1)S(1)} %bitcast.15, bf16[384,32,256]{2,1,0:T(8,128)(2,1)S(1)} %bitcast.16, ...), custom_call_target="tpu_custom_call" | custom-call | flops 8589934592 | bytes 8388608 | tf_op jit(solution)/shard_map/pallas_call | solution.py:352
  46.7 3.5 %collective-permute-start.4 = (bf16[2304,128]{1,0:T(8,128)(2,1)S(1)}, bf16[2304,128]{1,0:T(8,128)(2,1)S(1)}, u32[]{:S(2)}, u32[]{:S(2)}) collective-permute-start(bf16[2304,128]{1,0:T(8,128)(2,1)S(1)} %get-tuple-element.24), channel_id=1, source_target_pairs={{0,16},{16,32},{32,48},{48,64},{64,80},{80,96},{96,112},{1,17},{17... | collective-permute-start | bytes 1769480 | tf_op jit(solution)/shard_map/ppermute | solution.py:539
  50.2 6.0 %collective-permute-start.5 = (bf16[2304,128]{1,0:T(8,128)(2,1)S(1)}, bf16[2304,128]{1,0:T(8,128)(2,1)S(1)}, u32[]{:S(2)}, u32[]{:S(2)}) collective-permute-start(bf16[2304,128]{1,0:T(8,128)(2,1)S(1)} %get-tuple-element.25), channel_id=1, source_target_pairs={{16,0},{32,16},{48,32},{64,48},{80,64},{96,80},{112,96},{17,1},{33... | collective-permute-start | bytes 1769480 | tf_op jit(solution)/shard_map/ppermute | solution.py:539
  56.2 0.0 collective-permute-done.2.left_ref
  56.2 0.0 collective-permute-done.3.right_ref
  56.2 0.0 slice-done
  56.2 0.0 slice-done.1
  56.2 25.4 %shard_map.87 = (f32[64,128,128]{2,1,0:T(8,128)S(1)}, f32[2,128,128]{2,1,0:T(8,128)S(1)}) custom-call(s32[2]{0:T(128)S(1)} %pad_add_fusion.where_ref, s32[1,1]{1,0:T(1,128)S(6)} %copy.9.tissue_ref, bf16[384,32,256]{2,1,0:T(8,128)(2,1)S(1)} %bitcast.19, bf16[77,32,128]{2,1,0:T(8,128)(2,1)} %collective-permute-done.mleft_ref.left_ref, ...), custom_call_target="tpu_custom_call" | custom-call | flops 17179869184 | bytes 12582912 | tf_op jit(solution)/shard_map/pallas_call | solution.py:420
  81.6 0.0 collective-permute-done.4.above_ref
  81.6 0.0 collective-permute-done.5.below_ref
  81.6 11.3 %shard_map.89 = (f32[8192,128]{1,0:T(8,128)}, f32[256,128]{1,0:T(8,128)}, f32[128,384]{1,0:T(8,128)S(1)}, f32[8,384]{1,0:T(8,128)S(1)}, f32[8,384]{1,0:T(8,128)S(1)}) custom-call(s32[2]{0:T(128)S(1)} %pad_add_fusion.where_ref, f32[64,128,128]{2,1,0:T(8,128)S(1)} %get-tuple-element.21.rays_ref, f32[2,128,128]{2,1,0:T(8,128)S(1)} %get-tuple-element.22.prob_ref, ...), custom_call_target="tpu_custom_call" | custom-call | bytes 10485760 | tf_op jit(solution)/shard_map/pallas_call | solution.py:493
  92.9 0.7 copy-done.2
  93.6 1.9 %collective-permute-start.6 = (f32[8,384]{1,0:T(8,128)S(1)}, f32[8,384]{1,0:T(8,128)S(1)}, u32[]{:S(2)}, u32[]{:S(2)}) collective-permute-start(f32[8,384]{1,0:T(8,128)S(1)} %get-tuple-element.29), channel_id=1, source_target_pairs={{0,1},{1,2},{2,3},{3,4},{4,5},{5,6},{6,7},{7,8},{8,9},{9,10},{10,1... | collective-permute-start | bytes 36872 | tf_op jit(solution)/shard_map/ppermute | solution.py:539
  95.5 5.8 %collective-permute-start.7 = (f32[8,384]{1,0:T(8,128)S(1)}, f32[8,384]{1,0:T(8,128)S(1)}, u32[]{:S(2)}, u32[]{:S(2)}) collective-permute-start(f32[8,384]{1,0:T(8,128)S(1)} %get-tuple-element.30), channel_id=1, source_target_pairs={{1,0},{2,1},{3,2},{4,3},{5,4},{6,5},{7,6},{8,7},{9,8},{10,9},{11,1... | collective-permute-start | bytes 36872 | tf_op jit(solution)/shard_map/ppermute | solution.py:539
  101.3 0.0 collective-permute-done.6.west_ref
  101.3 1.4 %collective-permute-done.7.east_ref = f32[8,384]{1,0:T(8,128)S(1)} collective-permute-done((f32[8,384]{1,0:T(8,128)S(1)}, f32[8,384]{1,0:T(8,128)S(1)}, u32[]{:S(2)}, u32[]{:S(2)}) %collective-permute-start.7) | collective-permute-done | bytes 12320 | tf_op jit(solution)/shard_map/ppermute | solution.py:539
  102.7 0.6 copy-done.7
  103.2 2.0 %shard_map.90 = f32[256,128]{1,0:T(8,128)} custom-call(f32[128,384]{1,0:T(8,128)} %copy-done.2, f32[8,384]{1,0:T(8,128)} %copy-done.6, f32[8,384]{1,0:T(8,128)} %copy-done.7), custom_call_target="tpu_custom_call" | custom-call | tf_op jit(solution)/shard_map/pallas_call | solution.py:527
  (15 shorter events, 0.0 us)
Async XLA Ops:
  5.8 22.4 %collective-permute-start = (bf16[77,32,128]{2,1,0:T(8,128)(2,1)}, bf16[77,32,128]{2,1,0:T(8,128)(2,1)}, u32[]{:S(2)}, u32[]{:S(2)}) collective-permute-start(bf16[77,32,128]{2,1,0:T(8,128)(2,1)} %get-tuple-element.17), channel_id=1, source_target_pairs={{0,1},{1,2},{2,3},{3,4},{4,5},{5,6},{6,7},{7,8},{8,9},{9,10},{10,1... | collective-permute-start | bytes 1892360 | tf_op jit(solution)/shard_map/ppermute | solution.py:539
  7.8 20.5 %collective-permute-start.1 = (bf16[77,32,128]{2,1,0:T(8,128)(2,1)}, bf16[77,32,128]{2,1,0:T(8,128)(2,1)}, u32[]{:S(2)}, u32[]{:S(2)}) collective-permute-start(bf16[77,32,128]{2,1,0:T(8,128)(2,1)} %get-tuple-element.18), channel_id=1, source_target_pairs={{1,0},{2,1},{3,2},{4,3},{5,4},{6,5},{7,6},{8,7},{9,8},{10,9},{11,1... | collective-permute-start | bytes 1892360 | tf_op jit(solution)/shard_map/ppermute | solution.py:539
  13.5 2.8 %copy-start = (bf16[384,256,32]{1,2,0:T(8,128)(2,1)S(1)}, bf16[384,256,32]{1,2,0:T(8,128)(2,1)}, u32[]{:S(2)}) copy-start(bf16[384,256,32]{1,2,0:T(8,128)(2,1)} %param.6) | copy-start | bytes 18874372
  16.3 11.9 %copy-start.8 = (f32[33]{0:T(128)S(1)}, f32[33]{0:T(128)}, u32[]{:S(2)}) copy-start(f32[33]{0:T(128)} %param.10) | copy-start | bytes 400
  16.3 12.0 %copy-start.3 = (bf16[3,3,32,128]{3,2,1,0:T(8,128)(2,1)S(1)}, bf16[3,3,32,128]{3,2,1,0:T(8,128)(2,1)}, u32[]{:S(2)}) copy-start(bf16[3,3,32,128]{3,2,1,0:T(8,128)(2,1)} %param.7) | copy-start | bytes 221188
  16.3 12.0 %copy-start.4 = (bf16[128,33]{0,1:T(8,128)(2,1)S(1)}, bf16[128,33]{0,1:T(8,128)(2,1)}, u32[]{:S(2)}) copy-start(bf16[128,33]{0,1:T(8,128)(2,1)} %param.9) | copy-start | bytes 25348
  16.3 12.0 %copy-start.5 = (f32[128]{0:T(128)S(1)}, f32[128]{0:T(128)}, u32[]{:S(2)}) copy-start(f32[128]{0:T(128)} %param.8) | copy-start | bytes 1540
  16.3 39.9 %slice-start = ((s8[6291456]{0:T(1024)(128)(4,1)}), s8[2097152]{0:T(1024)(128)(4,1)S(1)}, s32[]{:S(2)}) async-start(s8[6291456]{0:T(1024)(128)(4,1)} %bitcast.17), calls=%async_computation | async-start | bytes 4194304
  20.5 35.7 %collective-permute-start.2 = (bf16[134,32,128]{2,1,0:T(8,128)(2,1)}, bf16[134,32,128]{2,1,0:T(8,128)(2,1)S(1)}, u32[]{:S(2)}, u32[]{:S(2)}) collective-permute-start(bf16[134,32,128]{2,1,0:T(8,128)(2,1)} %get-tuple-element.19), channel_id=1, source_target_pairs={{0,1},{1,2},{2,3},{3,4},{4,5},{5,6},{6,7},{7,8},{8,9},{9,10},{10,1... | collective-permute-start | bytes 3293192 | tf_op jit(solution)/shard_map/ppermute | solution.py:539
  22.4 33.8 %collective-permute-start.3 = (bf16[134,32,128]{2,1,0:T(8,128)(2,1)}, bf16[134,32,128]{2,1,0:T(8,128)(2,1)}, u32[]{:S(2)}, u32[]{:S(2)}) collective-permute-start(bf16[134,32,128]{2,1,0:T(8,128)(2,1)} %get-tuple-element.20), channel_id=1, source_target_pairs={{1,0},{2,1},{3,2},{4,3},{5,4},{6,5},{7,6},{8,7},{9,8},{10,9},{11,1... | collective-permute-start | bytes 3293192 | tf_op jit(solution)/shard_map/ppermute | solution.py:539
  28.3 2.8 %copy-start.1 = (bf16[384,256,32]{1,2,0:T(8,128)(2,1)S(1)}, bf16[384,256,32]{1,2,0:T(8,128)(2,1)}, u32[]{:S(2)}) copy-start(bf16[384,256,32]{1,2,0:T(8,128)(2,1)} %param.6) | copy-start | bytes 18874372
  31.1 25.1 %slice-start.1 = ((s8[6291456]{0:T(1024)(128)(4,1)}), s8[4194304]{0:T(1024)(128)(4,1)S(1)}, s32[]{:S(2)}) async-start(s8[6291456]{0:T(1024)(128)(4,1)} %bitcast.17), calls=%async_computation.1 | async-start | bytes 8388608
  46.7 34.9 %collective-permute-start.4 = (bf16[2304,128]{1,0:T(8,128)(2,1)S(1)}, bf16[2304,128]{1,0:T(8,128)(2,1)S(1)}, u32[]{:S(2)}, u32[]{:S(2)}) collective-permute-start(bf16[2304,128]{1,0:T(8,128)(2,1)S(1)} %get-tuple-element.24), channel_id=1, source_target_pairs={{0,16},{16,32},{32,48},{48,64},{64,80},{80,96},{96,112},{1,17},{17... | collective-permute-start | bytes 1769480 | tf_op jit(solution)/shard_map/ppermute | solution.py:539
  50.2 31.4 %collective-permute-start.5 = (bf16[2304,128]{1,0:T(8,128)(2,1)S(1)}, bf16[2304,128]{1,0:T(8,128)(2,1)S(1)}, u32[]{:S(2)}, u32[]{:S(2)}) collective-permute-start(bf16[2304,128]{1,0:T(8,128)(2,1)S(1)} %get-tuple-element.25), channel_id=1, source_target_pairs={{16,0},{32,16},{48,32},{64,48},{80,64},{96,80},{112,96},{17,1},{33... | collective-permute-start | bytes 1769480 | tf_op jit(solution)/shard_map/ppermute | solution.py:539
  92.9 0.7 copy-start.2
  93.6 7.7 %collective-permute-start.6 = (f32[8,384]{1,0:T(8,128)S(1)}, f32[8,384]{1,0:T(8,128)S(1)}, u32[]{:S(2)}, u32[]{:S(2)}) collective-permute-start(f32[8,384]{1,0:T(8,128)S(1)} %get-tuple-element.29), channel_id=1, source_target_pairs={{0,1},{1,2},{2,3},{3,4},{4,5},{5,6},{6,7},{7,8},{8,9},{9,10},{10,1... | collective-permute-start | bytes 36872 | tf_op jit(solution)/shard_map/ppermute | solution.py:539
  95.5 7.1 %collective-permute-start.7 = (f32[8,384]{1,0:T(8,128)S(1)}, f32[8,384]{1,0:T(8,128)S(1)}, u32[]{:S(2)}, u32[]{:S(2)}) collective-permute-start(f32[8,384]{1,0:T(8,128)S(1)} %get-tuple-element.30), channel_id=1, source_target_pairs={{1,0},{2,1},{3,2},{4,3},{5,4},{6,5},{7,6},{8,7},{9,8},{10,9},{11,1... | collective-permute-start | bytes 36872 | tf_op jit(solution)/shard_map/ppermute | solution.py:539
  101.3 1.4 %copy-start.6 = (f32[8,384]{1,0:T(8,128)}, f32[8,384]{1,0:T(8,128)S(1)}, u32[]{:S(2)}) copy-start(f32[8,384]{1,0:T(8,128)S(1)} %collective-permute-done.6.west_ref) | copy-start | bytes 36868
  102.7 0.6 copy-start.7

commit v3 on v0

v3 whole, which is shorter than its diff:
```python
import jax
import jax.numpy as jnp
from jax import lax
from jax.experimental import pallas as pl
from jax.experimental.pallas import tpu as pltpu
from jax.sharding import PartitionSpec as P

MARGIN = 64
EXT_H, EXT_W = 384, 256
CORE_H, CORE_W = 256, 128
N_ROWS, N_COLS = 8, 16
CIN, COUT, RAYS = 32, 128, 32
SIDE = 80
M_HALF = 19
M_BLOCKS = 2 * M_HALF
C_FIRST = 16
C_BLOCKS = 65
M_GROUPS = 18
M_OUT = 4 * M_GROUPS
GAP = 88
F32, BF16 = jnp.float32, jnp.bfloat16
SMEM = pl.BlockSpec(memory_space=pltpu.SMEM)
VMEM = pl.BlockSpec(memory_space=pltpu.VMEM)


def lanes_of(shape):
    return lax.broadcasted_iota(jnp.int32, shape, len(shape) - 1)


def gauss(position, extent):
    spread = extent / 4.0
    centred = position.astype(F32) - (extent - 1) / 2.0
    return jnp.exp(-(centred * centred) / (2.0 * spread * spread))


def turn(rows, index, right_ref, left_ref):
    block = jnp.concatenate(rows, axis=0).T
    right_ref[index] = block[EXT_W - SIDE :]
    left_ref[index] = block[:SIDE]


def turn_margin_kernel(tissue_ref, top_ref, bottom_ref, right_ref, left_ref):
    zero = jnp.zeros((CIN, EXT_W), BF16)
    turn([zero] + [top_ref[k] for k in range(3)], 0, right_ref, left_ref)
    turn([bottom_ref[95], zero, zero, zero], M_BLOCKS - 1, right_ref, left_ref)

    def step(m, carry):
        rows = [top_ref[4 * m - 1 + k] for k in range(4)]
        turn(rows, m, right_ref, left_ref)
        rows = [bottom_ref[19 + 4 * m + k] for k in range(4)]
        turn(rows, M_HALF - 1 + m, right_ref, left_ref)
        return carry

    lax.fori_loop(1, M_HALF, step, 0, unroll=6)
    flag = jnp.where(tissue_ref[0, 0] > 0, 1.0, 0.0)
    flags = jnp.full((SIDE, 128), flag, F32).astype(BF16)
    right_ref[M_BLOCKS] = flags
    left_ref[M_BLOCKS] = flags


def turn_margin(tissue, features):
    side = jax.ShapeDtypeStruct((M_BLOCKS + 1, SIDE, 128), BF16)
    return pl.pallas_call(
        turn_margin_kernel,
        grid=(1,),
        in_specs=[
            SMEM,
            pl.BlockSpec((96, CIN, EXT_W), lambda s: (0, 0, 0)),
            pl.BlockSpec((96, CIN, EXT_W), lambda s: (3, 0, 0)),
        ],
        out_specs=[VMEM, VMEM],
        out_shape=[side, side],
        compiler_params=pltpu.CompilerParams(vmem_limit_bytes=60 << 20),
        cost_estimate=pl.CostEstimate(flops=0, bytes_accessed=8 << 20, transcendentals=0),
    )(tissue, features, features)


def turn_core_kernel(features_ref, right_ref, left_ref):
    def step(m, carry):
        rows = [features_ref[4 * (C_FIRST + m) - 1 + k] for k in range(4)]
        turn(rows, m, right_ref, left_ref)
        return carry

    lax.fori_loop(0, C_BLOCKS, step, 0, unroll=13)


def turn_core(features):
    side = jax.ShapeDtypeStruct((C_BLOCKS, SIDE, 128), BF16)
    return pl.pallas_call(
        turn_core_kernel,
        in_specs=[VMEM],
        out_specs=[VMEM, VMEM],
        out_shape=[side, side],
        compiler_params=pltpu.CompilerParams(vmem_limit_bytes=60 << 20),
        cost_estimate=pl.CostEstimate(flops=0, bytes_accessed=12 << 20, transcendentals=0),
    )(features)


def prepare_weights(conv_ref, head_ref, conv_scr, head_scr):
    zero = jnp.zeros((CIN, COUT), BF16)
    for o in range(2):
        for i in range(4):
            for dc in range(3):
                dr = i - o
                piece = zero
                if 0 <= dr < 3:
                    piece = conv_ref[(3 * dr + dc) * CIN : (3 * dr + dc + 1) * CIN, :]
                row = dc * 128 + i * CIN
                conv_scr[row : row + CIN, o * COUT : (o + 1) * COUT] = piece
    head = head_ref[...].astype(F32)
    head = jnp.concatenate([head, jnp.zeros((COUT - head.shape[0], COUT), F32)], axis=0).T
    part = lax.div(lanes_of((COUT, 128)), RAYS)
    first = jnp.broadcast_to(head[:, 0:1], (COUT, 128))
    for b in range(4):
        rays = jnp.where(part == b, pltpu.roll(head, (b * RAYS - 1) % 128, 1), 0.0)
        prob = jnp.where(part == b, first, 0.0)
        head_scr[b * COUT : (b + 1) * COUT, 0:128] = rays.astype(BF16)
        head_scr[b * COUT : (b + 1) * COUT, 128:256] = prob.astype(BF16)


def spread_bias(head_bias):
    part = lax.div(lanes_of((8, 128)), RAYS)
    rays = jnp.zeros((8, 128), F32)
    for b in range(4):
        rays = jnp.where(part == b, pltpu.roll(head_bias, (b * RAYS - 1) % 128, 1), rays)
    return rays[0:1]


def column_weights(tile_col, tissue, left_flags, right_flags):
    q = lax.broadcasted_iota(jnp.int32, (32, 128), 0) * 4 + lax.div(lanes_of((32, 128)), RAYS)
    own = gauss(q + MARGIN, EXT_W)
    west_side = q < MARGIN
    side = jnp.where(west_side, gauss(q + CORE_W + MARGIN, EXT_W), gauss(q - MARGIN, EXT_W))
    has_west = jnp.where(tile_col > 0, 1.0, 0.0)
    has_east = jnp.where(tile_col < N_COLS - 1, 1.0, 0.0)
    total = own + side * jnp.where(west_side, has_west, has_east)
    flags = jnp.concatenate([left_flags[:16], right_flags[:16]], axis=0)
    return own / total * jnp.where(tissue > 0, 1.0, 0.0), side / total * flags


def row_weights(row, tile_row):
    own = gauss(row, EXT_H)
    above = gauss(row + CORE_H, EXT_H) * jnp.where(tile_row > 0, 1.0, 0.0)
    below = gauss(row - CORE_H, EXT_H) * jnp.where(tile_row < N_ROWS - 1, 1.0, 0.0)
    total = own + jnp.where(row < 2 * MARGIN, above, 0.0) + jnp.where(row >= CORE_H, below, 0.0)
    return own / total


def slid(now, later):
    low_half = lanes_of(now.shape) < 64
    return pltpu.roll(jnp.where(low_half, later, now), 64, 1)


def window_taps(own, left, right, own_f, side_f, taps_ref, w):
    own_f[...] = own.astype(F32)
    side_f[0:SIDE, :] = left.astype(F32)
    side_f[GAP : GAP + SIDE, :] = right.astype(F32)
    for d in range(3):
        lanes = slice(128 * d, 128 * (d + 1))
        for b in range(4):
            row = 256 * w + 32 * b
            taps_ref[row : row + 32, lanes] = own_f[pl.ds(15 + b + d, 32, stride=4), :].astype(BF16)
            west = side_f[pl.ds(15 + b + d, 16, stride=4), :]
            east = side_f[pl.ds(GAP - 1 + b + d, 16, stride=4), :]
            taps_ref[row + 128 : row + 144, lanes] = west.astype(BF16)
            taps_ref[row + 144 : row + 160, lanes] = east.astype(BF16)


def turned(rows):
    return jnp.concatenate(rows, axis=0).T[48:208]


def groups_taps(sources, buffers, taps_ref):
    for k, (now, later) in enumerate(sources):
        windows = now, tuple(slid(x, y) for x, y in zip(now, later))
        for w, window in enumerate(windows):
            at = 2 * k + w
            window_taps(*window, buffers[2 * at], buffers[2 * at + 1], taps_ref, at)


def groups_hidden(taps_ref, hidden_ref, conv_scr, bias):
    for first in range(0, taps_ref.shape[0], CONV_CHUNK):
        summed = jnp.dot(
            taps_ref[first : first + CONV_CHUNK, :], conv_scr[...], preferred_element_type=F32
        )
        hidden = jnp.maximum(summed + bias, 0.0).astype(BF16)
        for w in range(CONV_CHUNK // 256):
            for o in range(2):
                for s in range(2):
                    row = first // 2 + 32 * (4 * w + 2 * o + s)
                    for b in range(4):
                        start = 256 * w + 128 * s + 32 * b
                        hidden_ref[row : row + 32, b * COUT : (b + 1) * COUT] = hidden[
                            start : start + 32, o * COUT : (o + 1) * COUT
                        ]


def head_logits(hidden_ref, head_scr):
    every = []
    for first in range(0, hidden_ref.shape[0], HEAD_CHUNK):
        logits = jnp.dot(
            hidden_ref[first : first + HEAD_CHUNK, :], head_scr[...], preferred_element_type=F32
        )
        every += [logits[k : k + 256] for k in range(0, HEAD_CHUNK, 256)]
    return every


def walk(count, taps_stage, hidden_stage, head_stage, taps, hidden):
    taps_stage(0, taps[0])
    taps_stage(1, taps[1])
    hidden_stage(taps[0], hidden[0])

    def two(n, carry):
        for odd in (1, 0):
            i = 2 * n + 2 - odd
            taps_stage(i + 1, taps[1 - odd])
            hidden_stage(taps[odd], hidden[odd])
            head_stage(i - 1, hidden[1 - odd])
        return carry

    lax.fori_loop(0, (count - 2) // 2, two, 0)
    head_stage(count - 2, hidden[0])
    hidden_stage(taps[1], hidden[1])
    head_stage(count - 1, hidden[1])


def split_logits(logits, r):
    return logits[64 * r : 64 * r + 32], logits[64 * r + 32 : 64 * r + 64]


def weighted_rays(logits, r, ray_bias, own_weight, side_weight, row, factor_ref):
    own, side = split_logits(logits, r)
    factor = factor_ref[pl.ds(row, 1), :]
    return (
        (own[:, :128] + ray_bias) * own_weight + (side[:, :128] + ray_bias) * side_weight
    ) * factor


def keep_probability(logit_ref, logits, r, position):
    spot = lax.rem(lanes_of((32, 128)), RAYS) == lax.rem(position, RAYS)
    block = lax.div(position, RAYS)
    for k, part in enumerate(split_logits(logits, r)):
        logit_ref[k, block] = jnp.where(spot, part[:, 128:], logit_ref[k, block])


def probability_by_row(logit_ref, first_block, blocks, first_row, bias, tile_row, own_weight, side_weight, out_ref):
    lane = lanes_of((32, 128))
    values = []
    for j in range(blocks):
        own = 1.0 / (1.0 + jnp.exp(-(logit_ref[0, first_block + j] + bias)))
        side = 1.0 / (1.0 + jnp.exp(-(logit_ref[1, first_block + j] + bias)))
        factor = row_weights(first_row + 32 * j + lax.rem(lane, RAYS), tile_row)
        values.append((own * own_weight + side * side_weight) * factor)
    for b in range(4):
        rows = jnp.zeros((32, 128), F32)
        for j in range(blocks):
            moved = values[j] if j == b else pltpu.roll(values[j], ((j - b) * 32) % 128, 1)
            rows = jnp.where(lax.div(lane, 32) == j, moved, rows)
        out_ref[pl.ds(b, 32, stride=4), :] = rows


def margin_kernel(
    where_ref, tissue_ref, features_ref, left_ref, right_ref, conv_ref, bias_ref, head_ref, hbias_ref,
    up_ref, down_ref, edge_ref,
    logit_ref, turn_ref, factor_ref, conv_scr, head_scr, taps0, taps1, hidden0, hidden1, *buffers,
):
    tile_row, tile_col = where_ref[0], where_ref[1]
    prepare_weights(conv_ref, head_ref, conv_scr, head_scr)
    for k in range(len(buffers) // 2):
        buffers[2 * k + 1][SIDE:GAP, :] = jnp.zeros((GAP - SIDE, 128), F32)
    own_weight, side_weight = column_weights(
        tile_col, tissue_ref[0, 0], left_ref[M_BLOCKS].astype(F32), right_ref[M_BLOCKS].astype(F32)
    )
    bias = jnp.concatenate([bias_ref[...], bias_ref[...]], axis=1)
    ray_bias = spread_bias(hbias_ref[...])
    logit_ref[...] = jnp.zeros(logit_ref.shape, F32)
    table = lax.broadcasted_iota(jnp.int32, (EXT_H, 128), 0)
    factor_ref[...] = row_weights(table, tile_row)

    def taps_stage(g, taps_ref):
        def source(first_block, first_row, block):
            rows = []
            for k in range(4):
                row = first_row + 4 * block - 1 + k
                inside = (row >= 0) & (row < EXT_H)
                values = features_ref[jnp.where(inside, row, 0)]
                rows.append(jnp.where(inside, values, jnp.zeros_like(values)))
            at = first_block + block
            return turned(rows), left_ref[at], right_ref[at]

        groups_taps(
            [
                (source(*half, g), source(*half, g + 1))
                for half in ((0, 0), (M_HALF, EXT_H - M_OUT))
            ],
            buffers, taps_ref,
        )

    def hidden_stage(taps_ref, hidden_ref):
        groups_hidden(taps_ref, hidden_ref, conv_scr, bias)

    def head_stage(g, hidden_ref):
        every = head_logits(hidden_ref, head_scr)
        for half, (ref, first_row) in enumerate(((up_ref, 0), (down_ref, EXT_H - M_OUT))):
            logits = every[half]
            for r in range(4):
                position = 4 * g + r
                rays = weighted_rays(
                    logits, r, ray_bias, own_weight, side_weight, first_row + position, factor_ref
                )
                slot = position
                if half == 1:
                    slot = jnp.where(position < 8, position + 64, position - 8)
                ref[pl.ds(pl.multiple_of(slot * 32, 32), 32), :] = rays.astype(BF16)
                keep_probability(logit_ref, logits, r, position + 96 * half)

    walk(M_GROUPS, taps_stage, hidden_stage, head_stage, (taps0, taps1), (hidden0, hidden1))
    for half, (ref, first_row) in enumerate(((up_ref, 0), (down_ref, EXT_H - M_OUT))):
        probability_by_row(
            logit_ref, 3 * half, 3, first_row, hbias_ref[0, 0], tile_row,
            own_weight, side_weight, turn_ref,
        )
        prob = jnp.where(lanes_of((CORE_W, 128)) < M_OUT, turn_ref[...], 0.0)
        edge_ref[half] = prob
        high = prob.astype(BF16)
        ref[2048:2176, :] = high
        ref[2176:2304, :] = (prob - high.astype(F32)).astype(BF16)


C_GROUPS = 4
CONV_CHUNK, HEAD_CHUNK = 256, 256


def conv_scratch(groups, logit_blocks):
    return [
        pltpu.VMEM((2, logit_blocks, 32, 128), F32),
        pltpu.VMEM((CORE_W, 128), F32),
        pltpu.VMEM((EXT_H, 128), F32),
        pltpu.VMEM((384, 256), BF16),
        pltpu.VMEM((4 * COUT, 256), BF16),
        pltpu.VMEM((512 * groups, 384), BF16),
        pltpu.VMEM((512 * groups, 384), BF16),
        pltpu.VMEM((256 * groups, 512), BF16),
        pltpu.VMEM((256 * groups, 512), BF16),
    ] + [pltpu.VMEM((160, 128), F32), pltpu.VMEM((GAP + SIDE, 128), F32)] * (2 * groups)


def margin_outputs(where, tissue, features, left, right, weights):
    shape = jax.ShapeDtypeStruct((2304, 128), BF16)
    edge = jax.ShapeDtypeStruct((2, CORE_W, 128), F32)
    return pl.pallas_call(
        margin_kernel,
        in_specs=[SMEM, SMEM] + [VMEM] * 7,
        out_specs=[VMEM, VMEM, VMEM],
        out_shape=[shape, shape, edge],
        scratch_shapes=conv_scratch(2, 6),
        compiler_params=pltpu.CompilerParams(vmem_limit_bytes=24 << 20),
        cost_estimate=pl.CostEstimate(flops=8 << 30, bytes_accessed=8 << 20, transcendentals=0),
    )(where, tissue, features, left, right, *weights)


def core_kernel(
    where_ref, tissue_ref, features_ref, mleft_ref, mright_ref, left_ref, right_ref,
    conv_ref, bias_ref, head_ref, hbias_ref,
    out_ref, prob_ref,
    logit_ref, turn_ref, factor_ref, conv_scr, head_scr, taps0, taps1, hidden0, hidden1, *buffers,
):
    tile_row, tile_col = where_ref[0], where_ref[1]
    prepare_weights(conv_ref, head_ref, conv_scr, head_scr)
    for k in range(len(buffers) // 2):
        buffers[2 * k + 1][SIDE:GAP, :] = jnp.zeros((GAP - SIDE, 128), F32)
    own_weight, side_weight = column_weights(
        tile_col, tissue_ref[0, 0], mleft_ref[0].astype(F32), mright_ref[0].astype(F32)
    )
    bias = jnp.concatenate([bias_ref[...], bias_ref[...]], axis=1)
    ray_bias = spread_bias(hbias_ref[...])
    logit_ref[...] = jnp.zeros(logit_ref.shape, F32)
    table = lax.broadcasted_iota(jnp.int32, (EXT_H, 128), 0)
    factor_ref[...] = row_weights(table, tile_row)

    def taps_stage(h, taps_ref):
        blocks = []
        for k in range(C_GROUPS + 1):
            at = C_GROUPS * h + k
            rows = [features_ref[4 * (C_FIRST + at) - 1 + r] for r in range(4)]
            blocks.append((turned(rows), left_ref[at], right_ref[at]))
        groups_taps(list(zip(blocks[:-1], blocks[1:])), buffers, taps_ref)

    def hidden_stage(taps_ref, hidden_ref):
        groups_hidden(taps_ref, hidden_ref, conv_scr, bias)

    def head_stage(h, hidden_ref):
        every = head_logits(hidden_ref, head_scr)
        for k in range(C_GROUPS):
            logits = every[k]
            for r in range(4):
                row = 4 * (C_GROUPS * h + k) + r
                rays = weighted_rays(
                    logits, r, ray_bias, own_weight, side_weight, MARGIN + row, factor_ref
                )
                start = 128 * C_GROUPS * h + 256 * (k // 2) + 4 * (k % 2) + r
                out_ref[pl.ds(start, 32, stride=8), :] = rays
                keep_probability(logit_ref, logits, r, row)

    walk(
        64 // C_GROUPS, taps_stage, hidden_stage, head_stage, (taps0, taps1), (hidden0, hidden1)
    )
    for block in range(2):
        probability_by_row(
            logit_ref, 4 * block, 4, MARGIN + 128 * block, hbias_ref[0, 0], tile_row,
            own_weight, side_weight, turn_ref,
        )
        prob_ref[block] = turn_ref[...]


def core_outputs(where, tissue, features, mleft, mright, left, right, weights):
    flag = pl.BlockSpec((1, SIDE, 128), lambda s: (M_BLOCKS, 0, 0))
    return pl.pallas_call(
        core_kernel,
        grid=(1,),
        in_specs=[SMEM, SMEM, VMEM, flag, flag] + [VMEM] * 6,
        out_specs=[VMEM, VMEM],
        out_shape=[
            jax.ShapeDtypeStruct((CORE_H * 32, 128), F32),
            jax.ShapeDtypeStruct((2, CORE_W, 128), F32),
        ],
        scratch_shapes=conv_scratch(C_GROUPS, 8),
        compiler_params=pltpu.CompilerParams(vmem_limit_bytes=32 << 20),
        cost_estimate=pl.CostEstimate(flops=16 << 30, bytes_accessed=12 << 20, transcendentals=0),
    )(where, tissue, features, mleft, mright, left, right, *weights)


def probability_kernel(
    where_ref, prob_ref, edge_ref, above_ref, below_ref,
    probability_ref, wide_ref, west_ref, east_ref,
):
    tile_row = where_ref[0]
    lane = lanes_of((CORE_W, 128))
    above = above_ref[0:128, :].astype(F32) + above_ref[128:256, :].astype(F32)
    below = below_ref[0:128, :].astype(F32) + below_ref[128:256, :].astype(F32)
    first = prob_ref[0] + jnp.where(lane < 64, pltpu.roll(above, 120, 1), 0.0)
    last = prob_ref[1] + jnp.where(lane >= 64, pltpu.roll(below, 64, 1), 0.0)
    probability_ref[0:128, :] = first.T
    probability_ref[128:256, :] = last.T
    head = pltpu.roll(above, 122, 1) + pltpu.roll(edge_ref[0], 66, 1)
    head = jnp.where(tile_row > 0, head, 0.0)
    tail = pltpu.roll(edge_ref[1], 122, 1) + pltpu.roll(below, 66, 1)
    tail = jnp.where(tile_row < N_ROWS - 1, tail, 0.0)
    first_moved, last_moved = pltpu.roll(first, 2, 1), pltpu.roll(last, 2, 1)
    parts = [
        jnp.where(lane < 2, head, first_moved),
        jnp.where(lane < 2, first_moved, last_moved),
        jnp.where(lane < 2, last_moved, jnp.where(lane < 4, tail, 0.0)),
    ]
    for k, part in enumerate(parts):
        wide_ref[:, 128 * k : 128 * (k + 1)] = part
        west_ref[:, 128 * k : 128 * (k + 1)] = part[0:8]
        east_ref[:, 128 * k : 128 * (k + 1)] = part[120:128]


def final_probability(where, prob, edge, above, below):
    last = pl.BlockSpec((256, 128), lambda s: (8, 0))
    return pl.pallas_call(
        probability_kernel,
        grid=(1,),
        in_specs=[SMEM, VMEM, VMEM, last, last],
        out_specs=[VMEM] * 4,
        out_shape=[
            jax.ShapeDtypeStruct((CORE_H, CORE_W), F32),
            jax.ShapeDtypeStruct((CORE_W, 384), F32),
            jax.ShapeDtypeStruct((8, 384), F32),
            jax.ShapeDtypeStruct((8, 384), F32),
        ],
        cost_estimate=pl.CostEstimate(flops=0, bytes_accessed=1 << 20, transcendentals=0),
    )(where, prob, edge, above, below)


def add_margins_kernel(rays_ref, above_ref, below_ref, out_ref, edge_ref, sems):
    ends = (0, 6144)
    loads = [
        pltpu.make_async_copy(rays_ref.at[pl.ds(start, 2048)], edge_ref.at[k], sems.at[k])
        for k, start in enumerate(ends)
    ]
    for load in loads:
        load.start()
    stores = []
    for k, (start, ref) in enumerate(zip(ends, (above_ref, below_ref))):
        loads[k].wait()

        def step(t, carry, k=k, ref=ref):
            for r in range(8):
                margin = ref[pl.ds(pl.multiple_of((8 * t + r) * 32, 32), 32), :].astype(F32)
                edge_ref[k, pl.ds(256 * t + r, 32, stride=8), :] += margin
            return carry

        lax.fori_loop(0, 8, step, 0, unroll=4)
        store = pltpu.make_async_copy(edge_ref.at[k], out_ref.at[pl.ds(start, 2048)], sems.at[2 + k])
        store.start()
        stores.append(store)
    for store in stores:
        store.wait()


def add_margins(rays, above, below):
    some = pl.BlockSpec(memory_space=pl.ANY)
    return pl.pallas_call(
        add_margins_kernel,
        in_specs=[some, VMEM, VMEM],
        out_specs=some,
        out_shape=jax.ShapeDtypeStruct((CORE_H * 32, 128), F32),
        scratch_shapes=[pltpu.VMEM((2, 2048, 128), F32), pltpu.SemaphoreType.DMA((4,))],
        input_output_aliases={0: 0},
        cost_estimate=pl.CostEstimate(flops=0, bytes_accessed=6 << 20, transcendentals=0),
    )(rays, above, below)


def peak_kernel(wide_ref, west_ref, east_ref, gap_ref, tall_ref):
    tall_ref[0:8, :] = west_ref[...]
    tall_ref[8:136, :] = wide_ref[...]
    tall_ref[136:144, :] = east_ref[...]
    best = tall_ref[6:134, :]
    for k in range(1, 5):
        best = jnp.maximum(best, tall_ref[6 + k : 134 + k, :])
    along = best
    for k in range(1, 5):
        along = jnp.maximum(along, pltpu.roll(best, 384 - k, 1))
    gap = along - pltpu.roll(wide_ref[...], 382, 1)
    gap_ref[0:128, :] = gap[:, 0:128].T
    gap_ref[128:256, :] = gap[:, 128:256].T


def peak(wide, west, east):
    return pl.pallas_call(
        peak_kernel,
        in_specs=[VMEM] * 3,
        out_specs=VMEM,
        out_shape=jax.ShapeDtypeStruct((CORE_H, CORE_W), F32),
        scratch_shapes=[pltpu.VMEM((144, 384), F32)],
    )(wide, west, east)


def shift(array, axis, step):
    count = lax.axis_size(axis)
    pairs = [(i, i + step) for i in range(count) if 0 <= i + step < count]
    return lax.ppermute(array, axis, pairs)


def body(features, conv_weight, conv_bias, head_weight, head_bias, tissue):
    features = jnp.transpose(features, (0, 2, 1))
    where = jnp.stack([lax.axis_index("rows"), lax.axis_index("cols")]).astype(jnp.int32)
    hbias = jnp.pad(head_bias[None, :], ((0, 7), (0, 128 - head_bias.shape[0])))
    weights = (
        conv_weight.reshape(9 * CIN, COUT), conv_bias[None, :], jnp.transpose(head_weight), hbias,
    )
    to_right, to_left = turn_margin(tissue, features)
    mleft = shift(to_right, "cols", 1)
    mright = shift(to_left, "cols", -1)
    to_right, to_left = turn_core(features)
    cleft = shift(to_right, "cols", 1)
    cright = shift(to_left, "cols", -1)
    up, down, edge = margin_outputs(where, tissue, features, mleft, mright, weights)
    above = shift(down, "rows", 1)
    below = shift(up, "rows", -1)
    rays, prob = core_outputs(where, tissue, features, mleft, mright, cleft, cright, weights)
    probability, wide, west, east = final_probability(where, prob, edge, above, below)
    from_west = shift(east, "cols", 1)
    from_east = shift(west, "cols", -1)
    out = add_margins(rays, above, below)
    gap = peak(wide, from_west, from_east)
    lengths = out.reshape(32, 32, 8, 128).transpose(0, 2, 1, 3).reshape(CORE_H, CORE_W * RAYS)
    return (probability, lengths, gap)


def solution(mesh):
    in_specs = (P("rows", "cols", None), P(), P(), P(), P(), P("rows", "cols"))
    out_specs = (P("rows", "cols"), P("rows", "cols"), P("rows", "cols"))
    return jax.shard_map(body, mesh=mesh, in_specs=in_specs, out_specs=out_specs, check_vma=False)
```

time: 431 us -> 92.4 us (0.21)
  local copies, waits for them, and re-layouts: 194 us -> 5.75 us
  matrix products: 77.4 us -> 0 us
  other arithmetic: 70.5 us -> 0.08 us
  Pallas kernels: 0 us -> 51.9 us
  waiting for transfers between devices: 50 us -> 0.02 us
    slice x26 -> x0, local copies, waits for them, and re-layouts: 111 us -> none  [the longest x6 68.6 us: one_block(): piece[:, 0:out_cols]]
    dot_general x18 -> x0, matrix products: 77.4 us -> none  [the longest x6 42.7 us: one_block(): lax.dot_general(head_weight, hidden, (((0,), (1,)), ((), ())), preferred_...]
    pallas_call x0 -> x7, Pallas kernels: none -> 51.9 us  [the longest x1 21.4 us: core_outputs(): pl.pallas_call(core_kernel, grid=(1,), in_specs=[SMEM, SMEM, VMEM, flag,...]
    ppermute x8, waiting for transfers between devices: 50 us -> 0.02 us  [shift(): return lax.ppermute(array, axis, pairs)]
    concatenate x13 -> x0, other arithmetic: 42.7 us -> none  [the longest x6 41.2 us: one_block(): jnp.concatenate([piece[:, 0:out_cols], piece[:, 1:out_cols + 1], piece[:,...]
    another operation x3 -> x0, local copies, waits for them, and re-layouts: 25.6 us -> none
    pad x1, local copies, waits for them, and re-layouts: 17.6 us -> 0.01 us  [body(): hbias = jnp.pad(head_bias[None, :], ((0, 7), (0, 128 - head_bias.shape[0])))]
    ppermute x4 -> x0, local copies, waits for them, and re-layouts: 16.6 us -> none  [the longest x2 8.78 us: padded_2(): lax.ppermute(lax.slice_in_dim(block, block.shape[dim] - width, None, axis...]
  transfers between devices with their start and end apart: 8 -> 8, of which waited for: 5 -> 0; matrix products, arithmetic and copies ran while one was open for 10% -> 0% of each run, Pallas kernels for 0% -> 48%
where the time goes in v3:
time: 92.4 us; the launch traced here: 91.9 us
  Pallas kernels  51.9 us (56%)
  starting transfers between devices  32.6 us (35%)
  local copies, waits for them, and re-layouts  5.75 us (6%)
  between operations  1.55 us (2%)
    ppermute x8, starting transfers between devices, shift(): return lax.ppermute(array, axis, pairs)  32.6 us
    pallas_call x1, Pallas kernels, core_outputs(): pl.pallas_call(core_kernel, grid=(1,), in_specs=[SMEM, SMEM, VMEM, flag,...  21.4 us
    pallas_call x1, Pallas kernels, margin_outputs(): pl.pallas_call(margin_kernel, in_specs=[SMEM, SMEM] + [VMEM] * 7, out_spe...  12.6 us
    pallas_call x1, Pallas kernels, turn_core(): pl.pallas_call(turn_core_kernel, in_specs=[VMEM], out_specs=[VMEM, VMEM],...  5.8 us
    unnamed x28, local copies, waits for them, and re-layouts  5.74 us
    pallas_call x1, Pallas kernels, add_margins(): pl.pallas_call(add_margins_kernel, in_specs=[some, VMEM, VMEM], out_specs...  4.13 us
    pallas_call x1, Pallas kernels, turn_margin(): pl.pallas_call(turn_margin_kernel, grid=(1,), in_specs=[SMEM, pl.BlockSpe...  3.9 us
    pallas_call x1, Pallas kernels, peak(): pl.pallas_call(peak_kernel, in_specs=[VMEM] * 3, out_specs=VMEM, out_shap...  2.05 us
  transfers between devices with their start and end apart: 8, of which 0 were waited for; matrix products, arithmetic and copies ran while one was open for 0% of the time, Pallas kernels for 48%

profile of v3, /device:TPU:6, one launch (start us, length us, event | category | flops | bytes accessed | tf_op | source)
XLA Modules:
  0.0 91.9 jit_solution(5968520232124588601)
XLA Ops:
  1.3 3.9 %shard_map.85 = (bf16[39,80,128]{2,1,0:T(8,128)(2,1)}, bf16[39,80,128]{2,1,0:T(8,128)(2,1)}) custom-call(s32[1,1]{1,0:T(1,128)S(6)} %copy.11.tissue_ref, bf16[384,32,256]{2,1,0:T(8,128)(2,1)} %bitcast.12, bf16[384,32,256]{2,1,0:T(8,128)(2,1)} %bitcast.13), custom_call_target="tpu_custom_call" | custom-call | bytes 8388608 | tf_op jit(solution)/shard_map/pallas_call | solution.py:63
  5.2 1.9 %collective-permute-start = (bf16[39,80,128]{2,1,0:T(8,128)(2,1)}, bf16[39,80,128]{2,1,0:T(8,128)(2,1)}, u32[]{:S(2)}, u32[]{:S(2)}) collective-permute-start(bf16[39,80,128]{2,1,0:T(8,128)(2,1)} %get-tuple-element.16), channel_id=1, source_target_pairs={{0,1},{1,2},{2,3},{3,4},{4,5},{5,6},{6,7},{7,8},{8,9},{9,10},{10,1... | collective-permute-start | bytes 2396168 | tf_op jit(solution)/shard_map/ppermute | solution.py:545
  7.1 0.0 copy-start.11
  7.1 0.0 copy-start.4
  7.1 0.0 copy-start.5
  7.1 0.0 copy-start.6
  7.1 5.9 %collective-permute-start.1 = (bf16[39,80,128]{2,1,0:T(8,128)(2,1)}, bf16[39,80,128]{2,1,0:T(8,128)(2,1)}, u32[]{:S(2)}, u32[]{:S(2)}) collective-permute-start(bf16[39,80,128]{2,1,0:T(8,128)(2,1)} %get-tuple-element.17), channel_id=1, source_target_pairs={{1,0},{2,1},{3,2},{4,3},{5,4},{6,5},{7,6},{8,7},{9,8},{10,9},{11,1... | collective-permute-start | bytes 2396168 | tf_op jit(solution)/shard_map/ppermute | solution.py:545
  13.0 0.0 slice-start
  13.1 5.8 %shard_map.86 = (bf16[65,80,128]{2,1,0:T(8,128)(2,1)}, bf16[65,80,128]{2,1,0:T(8,128)(2,1)}) custom-call(bf16[384,32,256]{2,1,0:T(8,128)(2,1)} %bitcast.14), custom_call_target="tpu_custom_call" | custom-call | bytes 12582912 | tf_op jit(solution)/shard_map/pallas_call | solution.py:89
  18.9 1.9 %collective-permute-start.2 = (bf16[65,80,128]{2,1,0:T(8,128)(2,1)}, bf16[65,80,128]{2,1,0:T(8,128)(2,1)S(1)}, u32[]{:S(2)}, u32[]{:S(2)}) collective-permute-start(bf16[65,80,128]{2,1,0:T(8,128)(2,1)} %get-tuple-element.18), channel_id=1, source_target_pairs={{0,1},{1,2},{2,3},{3,4},{4,5},{5,6},{6,7},{7,8},{8,9},{9,10},{10,1... | collective-permute-start | bytes 3993608 | tf_op jit(solution)/shard_map/ppermute | solution.py:545
  20.8 5.8 %collective-permute-start.3 = (bf16[65,80,128]{2,1,0:T(8,128)(2,1)}, bf16[65,80,128]{2,1,0:T(8,128)(2,1)}, u32[]{:S(2)}, u32[]{:S(2)}) collective-permute-start(bf16[65,80,128]{2,1,0:T(8,128)(2,1)} %get-tuple-element.19), channel_id=1, source_target_pairs={{1,0},{2,1},{3,2},{4,3},{5,4},{6,5},{7,6},{8,7},{9,8},{10,9},{11,1... | collective-permute-start | bytes 3993608 | tf_op jit(solution)/shard_map/ppermute | solution.py:545
  26.6 0.1 pad_add_fusion.where_ref
  26.7 0.0 copy-start
  26.7 2.8 %copy-done = bf16[384,256,32]{1,2,0:T(8,128)(2,1)S(1)} copy-done((bf16[384,256,32]{1,2,0:T(8,128)(2,1)S(1)}, bf16[384,256,32]{1,2,0:T(8,128)(2,1)}, u32[]{:S(2)}) %copy-start) | copy-done | bytes 6291480
  29.5 12.6 %shard_map.88 = (bf16[2304,128]{1,0:T(8,128)(2,1)S(1)}, bf16[2304,128]{1,0:T(8,128)(2,1)S(1)}, f32[2,128,128]{2,1,0:T(8,128)S(1)}) custom-call(s32[2]{0:T(128)S(1)} %pad_add_fusion.where_ref, s32[1,1]{1,0:T(1,128)S(6)} %copy.11.tissue_ref, bf16[384,32,256]{2,1,0:T(8,128)(2,1)S(1)} %bitcast.15, bf16[39,80,128]{2,1,0:T(8,128)(2,1)} %collective-permute-done.mleft_ref.left_ref, ...), custom_call_target="tpu_custom_call" | custom-call | flops 8589934592 | bytes 8388608 | tf_op jit(solution)/shard_map/pallas_call | solution.py:351
  42.1 3.5 %collective-permute-start.4 = (bf16[2304,128]{1,0:T(8,128)(2,1)S(1)}, bf16[2304,128]{1,0:T(8,128)(2,1)S(1)}, u32[]{:S(2)}, u32[]{:S(2)}) collective-permute-start(bf16[2304,128]{1,0:T(8,128)(2,1)S(1)} %get-tuple-element.22), channel_id=1, source_target_pairs={{0,16},{16,32},{32,48},{48,64},{64,80},{80,96},{96,112},{1,17},{17... | collective-permute-start | bytes 1769480 | tf_op jit(solution)/shard_map/ppermute | solution.py:545
  45.6 6.0 %collective-permute-start.5 = (bf16[2304,128]{1,0:T(8,128)(2,1)S(1)}, bf16[2304,128]{1,0:T(8,128)(2,1)S(1)}, u32[]{:S(2)}, u32[]{:S(2)}) collective-permute-start(bf16[2304,128]{1,0:T(8,128)(2,1)S(1)} %get-tuple-element.23), channel_id=1, source_target_pairs={{16,0},{32,16},{48,32},{64,48},{80,64},{96,80},{112,96},{17,1},{33... | collective-permute-start | bytes 1769480 | tf_op jit(solution)/shard_map/ppermute | solution.py:545
  51.6 0.0 collective-permute-done.2.left_ref
  51.6 0.0 collective-permute-done.3.right_ref
  51.7 21.4 %shard_map.87 = (f32[8192,128]{1,0:T(8,128)}, f32[2,128,128]{2,1,0:T(8,128)S(1)}) custom-call(s32[2]{0:T(128)S(1)} %pad_add_fusion.where_ref, s32[1,1]{1,0:T(1,128)S(6)} %copy.11.tissue_ref, bf16[384,32,256]{2,1,0:T(8,128)(2,1)S(1)} %bitcast.18, bf16[39,80,128]{2,1,0:T(8,128)(2,1)} %collective-permute-done.mleft_ref.left_ref, ...), custom_call_target="tpu_custom_call" | custom-call | flops 17179869184 | bytes 12582912 | tf_op jit(solution)/shard_map/pallas_call | solution.py:418
  73.0 0.7 copy-done.2
  73.7 0.0 collective-permute-done.5.below_ref
  73.7 0.8 copy-done.7
  74.5 0.8 copy-done.8
  75.4 2.0 %shard_map.89 = (f32[256,128]{1,0:T(8,128)}, f32[128,384]{1,0:T(8,128)}, f32[8,384]{1,0:T(8,128)}, f32[8,384]{1,0:T(8,128)}) custom-call(s32[2]{0:T(128)} %copy-done.3, f32[2,128,128]{2,1,0:T(8,128)} %copy-done.2, f32[2,128,128]{2,1,0:T(8,128)} %copy-done.1, bf16[2304,128]{1,0:T(8,128)(2,1)} %copy-done.7, bf16[2304,128]{1,0:T(8,128)(2,1)} %copy-done.8), custom_call_target="tpu_custom_call" | custom-call | bytes 1048576 | tf_op jit(solution)/shard_map/pallas_call | solution.py:463
  77.4 1.9 %collective-permute-start.6 = (f32[8,384]{1,0:T(8,128)}, f32[8,384]{1,0:T(8,128)S(1)}, u32[]{:S(2)}, u32[]{:S(2)}) collective-permute-start(f32[8,384]{1,0:T(8,128)} %get-tuple-element.27), channel_id=1, source_target_pairs={{0,1},{1,2},{2,3},{3,4},{4,5},{5,6},{6,7},{7,8},{8,9},{9,10},{10,1... | collective-permute-start | bytes 36872 | tf_op jit(solution)/shard_map/ppermute | solution.py:545
  79.3 5.8 %collective-permute-start.7 = (f32[8,384]{1,0:T(8,128)}, f32[8,384]{1,0:T(8,128)S(1)}, u32[]{:S(2)}, u32[]{:S(2)}) collective-permute-start(f32[8,384]{1,0:T(8,128)} %get-tuple-element.28), channel_id=1, source_target_pairs={{1,0},{2,1},{3,2},{4,3},{5,4},{6,5},{7,6},{8,7},{9,8},{10,9},{11,1... | collective-permute-start | bytes 36872 | tf_op jit(solution)/shard_map/ppermute | solution.py:545
  85.0 4.1 %shard_map.90 = f32[8192,128]{1,0:T(8,128)} custom-call(f32[8192,128]{1,0:T(8,128)} %get-tuple-element.25.rays_ref, bf16[2304,128]{1,0:T(8,128)(2,1)} %copy-done.7, bf16[2304,128]{1,0:T(8,128)(2,1)} %copy-done.8), custom_call_target="tpu_custom_call", output_to_operand_aliasing={{}: (0, {})} | custom-call | bytes 6291456 | tf_op jit(solution)/shard_map/pallas_call | solution.py:506
  89.2 0.0 collective-permute-done.6.west_ref
  89.2 0.6 copy-done.9
  89.8 0.0 copy-done.10
  89.8 2.0 %shard_map.91 = f32[256,128]{1,0:T(8,128)} custom-call(f32[128,384]{1,0:T(8,128)} %get-tuple-element.26.wide_ref, f32[8,384]{1,0:T(8,128)} %copy-done.9, f32[8,384]{1,0:T(8,128)} %copy-done.10), custom_call_target="tpu_custom_call" | custom-call | tf_op jit(solution)/shard_map/pallas_call | solution.py:533
  (22 shorter events, 0.0 us)
Async XLA Ops:
  5.2 21.5 %collective-permute-start = (bf16[39,80,128]{2,1,0:T(8,128)(2,1)}, bf16[39,80,128]{2,1,0:T(8,128)(2,1)}, u32[]{:S(2)}, u32[]{:S(2)}) collective-permute-start(bf16[39,80,128]{2,1,0:T(8,128)(2,1)} %get-tuple-element.16), channel_id=1, source_target_pairs={{0,1},{1,2},{2,3},{3,4},{4,5},{5,6},{6,7},{7,8},{8,9},{9,10},{10,1... | collective-permute-start | bytes 2396168 | tf_op jit(solution)/shard_map/ppermute | solution.py:545
  7.1 19.4 %copy-start.11 = (f32[33]{0:T(128)S(1)}, f32[33]{0:T(128)}, u32[]{:S(2)}) copy-start(f32[33]{0:T(128)} %param.10) | copy-start | bytes 400
  7.1 19.5 %copy-start.4 = (bf16[3,3,32,128]{3,2,1,0:T(8,128)(2,1)S(1)}, bf16[3,3,32,128]{3,2,1,0:T(8,128)(2,1)}, u32[]{:S(2)}) copy-start(bf16[3,3,32,128]{3,2,1,0:T(8,128)(2,1)} %param.7) | copy-start | bytes 221188
  7.1 19.5 %copy-start.5 = (bf16[128,33]{0,1:T(8,128)(2,1)S(1)}, bf16[128,33]{0,1:T(8,128)(2,1)}, u32[]{:S(2)}) copy-start(bf16[128,33]{0,1:T(8,128)(2,1)} %param.9) | copy-start | bytes 25348
  7.1 19.5 %copy-start.6 = (f32[128]{0:T(128)S(1)}, f32[128]{0:T(128)}, u32[]{:S(2)}) copy-start(f32[128]{0:T(128)} %param.8) | copy-start | bytes 1540
  7.1 19.5 %collective-permute-start.1 = (bf16[39,80,128]{2,1,0:T(8,128)(2,1)}, bf16[39,80,128]{2,1,0:T(8,128)(2,1)}, u32[]{:S(2)}, u32[]{:S(2)}) collective-permute-start(bf16[39,80,128]{2,1,0:T(8,128)(2,1)} %get-tuple-element.17), channel_id=1, source_target_pairs={{1,0},{2,1},{3,2},{4,3},{5,4},{6,5},{7,6},{8,7},{9,8},{10,9},{11,1... | collective-permute-start | bytes 2396168 | tf_op jit(solution)/shard_map/ppermute | solution.py:545
  13.0 38.6 %slice-start = ((s8[6291456]{0:T(1024)(128)(4,1)}), s8[2097152]{0:T(1024)(128)(4,1)S(1)}, s32[]{:S(2)}) async-start(s8[6291456]{0:T(1024)(128)(4,1)} %bitcast.16), calls=%async_computation | async-start | bytes 4194304
  18.9 32.8 %collective-permute-start.2 = (bf16[65,80,128]{2,1,0:T(8,128)(2,1)}, bf16[65,80,128]{2,1,0:T(8,128)(2,1)S(1)}, u32[]{:S(2)}, u32[]{:S(2)}) collective-permute-start(bf16[65,80,128]{2,1,0:T(8,128)(2,1)} %get-tuple-element.18), channel_id=1, source_target_pairs={{0,1},{1,2},{2,3},{3,4},{4,5},{5,6},{6,7},{7,8},{8,9},{9,10},{10,1... | collective-permute-start | bytes 3993608 | tf_op jit(solution)/shard_map/ppermute | solution.py:545
  20.8 30.9 %collective-permute-start.3 = (bf16[65,80,128]{2,1,0:T(8,128)(2,1)}, bf16[65,80,128]{2,1,0:T(8,128)(2,1)}, u32[]{:S(2)}, u32[]{:S(2)}) collective-permute-start(bf16[65,80,128]{2,1,0:T(8,128)(2,1)} %get-tuple-element.19), channel_id=1, source_target_pairs={{1,0},{2,1},{3,2},{4,3},{5,4},{6,5},{7,6},{8,7},{9,8},{10,9},{11,1... | collective-permute-start | bytes 3993608 | tf_op jit(solution)/shard_map/ppermute | solution.py:545
  26.6 25.0 %copy-start.3 = (s32[2]{0:T(128)}, s32[2]{0:T(128)S(1)}, u32[]{:S(2)}) copy-start(s32[2]{0:T(128)S(1)} %pad_add_fusion.where_ref) | copy-start | bytes 28
  26.7 2.8 %copy-start = (bf16[384,256,32]{1,2,0:T(8,128)(2,1)S(1)}, bf16[384,256,32]{1,2,0:T(8,128)(2,1)}, u32[]{:S(2)}) copy-start(bf16[384,256,32]{1,2,0:T(8,128)(2,1)} %param.6) | copy-start | bytes 18874372
  29.5 22.2 %slice-start.1 = ((s8[6291456]{0:T(1024)(128)(4,1)}), s8[4194304]{0:T(1024)(128)(4,1)S(1)}, s32[]{:S(2)}) async-start(s8[6291456]{0:T(1024)(128)(4,1)} %bitcast.16), calls=%async_computation.1 | async-start | bytes 8388608
  42.1 30.9 %copy-start.1 = (f32[2,128,128]{2,1,0:T(8,128)}, f32[2,128,128]{2,1,0:T(8,128)S(1)}, u32[]{:S(2)}) copy-start(f32[2,128,128]{2,1,0:T(8,128)S(1)} %get-tuple-element.21.edge_ref) | copy-start | bytes 393220
  42.1 31.6 %collective-permute-start.4 = (bf16[2304,128]{1,0:T(8,128)(2,1)S(1)}, bf16[2304,128]{1,0:T(8,128)(2,1)S(1)}, u32[]{:S(2)}, u32[]{:S(2)}) collective-permute-start(bf16[2304,128]{1,0:T(8,128)(2,1)S(1)} %get-tuple-element.22), channel_id=1, source_target_pairs={{0,16},{16,32},{32,48},{48,64},{64,80},{80,96},{96,112},{1,17},{17... | collective-permute-start | bytes 1769480 | tf_op jit(solution)/shard_map/ppermute | solution.py:545
  45.6 28.1 %collective-permute-start.5 = (bf16[2304,128]{1,0:T(8,128)(2,1)S(1)}, bf16[2304,128]{1,0:T(8,128)(2,1)S(1)}, u32[]{:S(2)}, u32[]{:S(2)}) collective-permute-start(bf16[2304,128]{1,0:T(8,128)(2,1)S(1)} %get-tuple-element.23), channel_id=1, source_target_pairs={{16,0},{32,16},{48,32},{64,48},{80,64},{96,80},{112,96},{17,1},{33... | collective-permute-start | bytes 1769480 | tf_op jit(solution)/shard_map/ppermute | solution.py:545
  73.0 0.7 copy-start.2
  73.7 0.8 copy-start.7
  74.5 0.8 copy-start.8
  77.4 11.8 %collective-permute-start.6 = (f32[8,384]{1,0:T(8,128)}, f32[8,384]{1,0:T(8,128)S(1)}, u32[]{:S(2)}, u32[]{:S(2)}) collective-permute-start(f32[8,384]{1,0:T(8,128)} %get-tuple-element.27), channel_id=1, source_target_pairs={{0,1},{1,2},{2,3},{3,4},{4,5},{5,6},{6,7},{7,8},{8,9},{9,10},{10,1... | collective-permute-start | bytes 36872 | tf_op jit(solution)/shard_map/ppermute | solution.py:545
  79.3 9.9 %collective-permute-start.7 = (f32[8,384]{1,0:T(8,128)}, f32[8,384]{1,0:T(8,128)S(1)}, u32[]{:S(2)}, u32[]{:S(2)}) collective-permute-start(f32[8,384]{1,0:T(8,128)} %get-tuple-element.28), channel_id=1, source_target_pairs={{1,0},{2,1},{3,2},{4,3},{5,4},{6,5},{7,6},{8,7},{9,8},{10,9},{11,1... | collective-permute-start | bytes 36872 | tf_op jit(solution)/shard_map/ppermute | solution.py:545
  89.2 0.6 copy-start.9
  89.2 0.6 copy-start.10

commit v4 on v3

--- a/solution.py
+++ b/solution.py
@@ -21,6 +21,7 @@
 F32, BF16 = jnp.float32, jnp.bfloat16
 SMEM = pl.BlockSpec(memory_space=pltpu.SMEM)
 VMEM = pl.BlockSpec(memory_space=pltpu.VMEM)
+HBM = pl.BlockSpec(memory_space=pltpu.HBM)
 
 
 def lanes_of(shape):
@@ -91,7 +92,7 @@
         in_specs=[VMEM],
         out_specs=[VMEM, VMEM],
         out_shape=[side, side],
-        compiler_params=pltpu.CompilerParams(vmem_limit_bytes=60 << 20),
+        compiler_params=pltpu.CompilerParams(vmem_limit_bytes=20 << 20),
         cost_estimate=pl.CostEstimate(flops=0, bytes_accessed=12 << 20, transcendentals=0),
     )(features)
 
@@ -205,7 +206,7 @@
     return every
 
 
-def walk(count, taps_stage, hidden_stage, head_stage, taps, hidden):
+def walk(count, taps_stage, hidden_stage, head_stage, taps, hidden, after=None):
     taps_stage(0, taps[0])
     taps_stage(1, taps[1])
     hidden_stage(taps[0], hidden[0])
@@ -216,6 +217,8 @@
             taps_stage(i + 1, taps[1 - odd])
             hidden_stage(taps[odd], hidden[odd])
             head_stage(i - 1, hidden[1 - odd])
+        if after is not None:
+            after(n)
         return carry
 
     lax.fori_loop(0, (count - 2) // 2, two, 0)
@@ -260,11 +263,18 @@
 
 
 def margin_kernel(
-    where_ref, tissue_ref, features_ref, left_ref, right_ref, conv_ref, bias_ref, head_ref, hbias_ref,
+    where_ref, tissue_ref, features_hbm, left_ref, right_ref, conv_ref, bias_ref, head_ref, hbias_ref,
     up_ref, down_ref, edge_ref,
+    features_ref, load_sems,
     logit_ref, turn_ref, factor_ref, conv_scr, head_scr, taps0, taps1, hidden0, hidden1, *buffers,
 ):
     tile_row, tile_col = where_ref[0], where_ref[1]
+    loads = [
+        pltpu.make_async_copy(features_hbm.at[rows], features_ref.at[rows], load_sems.at[k])
+        for k, rows in enumerate((pl.ds(0, 80), pl.ds(EXT_H - 80, 80)))
+    ]
+    for load in loads:
+        load.start()
     prepare_weights(conv_ref, head_ref, conv_scr, head_scr)
     for k in range(len(buffers) // 2):
         buffers[2 * k + 1][SIDE:GAP, :] = jnp.zeros((GAP - SIDE, 128), F32)
@@ -276,6 +286,8 @@
     logit_ref[...] = jnp.zeros(logit_ref.shape, F32)
     table = lax.broadcasted_iota(jnp.int32, (EXT_H, 128), 0)
     factor_ref[...] = row_weights(table, tile_row)
+    for load in loads:
+        load.wait()
 
     def taps_stage(g, taps_ref):
         def source(first_block, first_row, block):
@@ -350,10 +362,12 @@
     edge = jax.ShapeDtypeStruct((2, CORE_W, 128), F32)
     return pl.pallas_call(
         margin_kernel,
-        in_specs=[SMEM, SMEM] + [VMEM] * 7,
+        in_specs=[SMEM, SMEM, HBM] + [VMEM] * 6,
         out_specs=[VMEM, VMEM, VMEM],
         out_shape=[shape, shape, edge],
-        scratch_shapes=conv_scratch(2, 6),
+        scratch_shapes=[
+            pltpu.VMEM((EXT_H, CIN, EXT_W), BF16), pltpu.SemaphoreType.DMA((2,)),
+        ] + conv_scratch(2, 6),
         compiler_params=pltpu.CompilerParams(vmem_limit_bytes=24 << 20),
         cost_estimate=pl.CostEstimate(flops=8 << 30, bytes_accessed=8 << 20, transcendentals=0),
     )(where, tissue, features, left, right, *weights)
@@ -362,7 +376,8 @@
 def core_kernel(
     where_ref, tissue_ref, features_ref, mleft_ref, mright_ref, left_ref, right_ref,
     conv_ref, bias_ref, head_ref, hbias_ref,
-    out_ref, prob_ref,
+    out_hbm, prob_ref,
+    out_ref, store_sems,
     logit_ref, turn_ref, factor_ref, conv_scr, head_scr, taps0, taps1, hidden0, hidden1, *buffers,
 ):
     tile_row, tile_col = where_ref[0], where_ref[1]
@@ -402,15 +417,29 @@
                 out_ref[pl.ds(start, 32, stride=8), :] = rays
                 keep_probability(logit_ref, logits, r, row)
 
+    stores = [
+        pltpu.make_async_copy(out_ref.at[rows], out_hbm.at[rows], store_sems.at[k])
+        for k, rows in enumerate((pl.ds(0, 4096), pl.ds(4096, 4096)))
+    ]
+
+    def first_half_out(n):
+        @pl.when(n == 32 // C_GROUPS // 2 - 1)
+        def _():
+            stores[0].start()
+
     walk(
-        64 // C_GROUPS, taps_stage, hidden_stage, head_stage, (taps0, taps1), (hidden0, hidden1)
+        64 // C_GROUPS, taps_stage, hidden_stage, head_stage, (taps0, taps1), (hidden0, hidden1),
+        first_half_out,
     )
+    stores[1].start()
     for block in range(2):
         probability_by_row(
             logit_ref, 4 * block, 4, MARGIN + 128 * block, hbias_ref[0, 0], tile_row,
             own_weight, side_weight, turn_ref,
         )
         prob_ref[block] = turn_ref[...]
+    for store in stores:
+        store.wait()
 
 
 def core_outputs(where, tissue, features, mleft, mright, left, right, weights):
@@ -419,12 +448,14 @@
         core_kernel,
         grid=(1,),
         in_specs=[SMEM, SMEM, VMEM, flag, flag] + [VMEM] * 6,
-        out_specs=[VMEM, VMEM],
+        out_specs=[HBM, VMEM],
         out_shape=[
             jax.ShapeDtypeStruct((CORE_H * 32, 128), F32),
             jax.ShapeDtypeStruct((2, CORE_W, 128), F32),
         ],
-        scratch_shapes=conv_scratch(C_GROUPS, 8),
+        scratch_shapes=[
+            pltpu.VMEM((CORE_H * 32, 128), F32), pltpu.SemaphoreType.DMA((2,)),
+        ] + conv_scratch(C_GROUPS, 8),
         compiler_params=pltpu.CompilerParams(vmem_limit_bytes=32 << 20),
         cost_estimate=pl.CostEstimate(flops=16 << 30, bytes_accessed=12 << 20, transcendentals=0),
     )(where, tissue, features, mleft, mright, left, right, *weights)
@@ -471,6 +502,7 @@
             jax.ShapeDtypeStruct((8, 384), F32),
             jax.ShapeDtypeStruct((8, 384), F32),
         ],
+        compiler_params=pltpu.CompilerParams(vmem_limit_bytes=8 << 20),
         cost_estimate=pl.CostEstimate(flops=0, bytes_accessed=1 << 20, transcendentals=0),
     )(where, prob, edge, above, below)
 
@@ -510,6 +542,7 @@
         out_shape=jax.ShapeDtypeStruct((CORE_H * 32, 128), F32),
         scratch_shapes=[pltpu.VMEM((2, 2048, 128), F32), pltpu.SemaphoreType.DMA((4,))],
         input_output_aliases={0: 0},
+        compiler_params=pltpu.CompilerParams(vmem_limit_bytes=8 << 20),
         cost_estimate=pl.CostEstimate(flops=0, bytes_accessed=6 << 20, transcendentals=0),
     )(rays, above, below)
 
@@ -536,6 +569,7 @@
         out_specs=VMEM,
         out_shape=jax.ShapeDtypeStruct((CORE_H, CORE_W), F32),
         scratch_shapes=[pltpu.VMEM((144, 384), F32)],
+        compiler_params=pltpu.CompilerParams(vmem_limit_bytes=8 << 20),
     )(wide, west, east)
 
 

time: 92.4 us -> 85.8 us (0.929)
  Pallas kernels: 51.9 us -> 45.7 us
    pallas_call x1, Pallas kernels: 5.8 us -> 2.87 us  [turn_core(): pl.pallas_call(turn_core_kernel, in_specs=[VMEM], out_specs=[VMEM, VMEM],...]
    pallas_call x1, Pallas kernels: 4.13 us -> 2.88 us  [add_margins(): pl.pallas_call(add_margins_kernel, in_specs=[some, VMEM, VMEM], out_specs...]
    pallas_call x1, Pallas kernels: 2.05 us -> 1.11 us  [peak(): pl.pallas_call(peak_kernel, in_specs=[VMEM] * 3, out_specs=VMEM, out_shap...]
    unnamed x28 -> x16, local copies, waits for them, and re-layouts: 5.74 us -> 5.58 us
  transfers between devices with their start and end apart: 8 -> 8, of which waited for: 0 -> 0; matrix products, arithmetic and copies ran while one was open for 0% -> 0% of each run, Pallas kernels for 48% -> 46%
where the time goes in v4:
time: 85.8 us; the launch traced here: 85.4 us
  Pallas kernels  45.7 us (53%)
  starting transfers between devices  32.4 us (38%)
  local copies, waits for them, and re-layouts  5.59 us (7%)
  between operations  1.51 us (2%)
    ppermute x8, starting transfers between devices, shift(): return lax.ppermute(array, axis, pairs)  32.4 us
    pallas_call x1, Pallas kernels, core_outputs(): pl.pallas_call(core_kernel, grid=(1,), in_specs=[SMEM, SMEM, VMEM, flag,...  20.6 us
    pallas_call x1, Pallas kernels, margin_outputs(): pl.pallas_call(margin_kernel, in_specs=[SMEM, SMEM, HBM] + [VMEM] * 6, ou...  13 us
    unnamed x16, local copies, waits for them, and re-layouts  5.58 us
    pallas_call x1, Pallas kernels, turn_margin(): pl.pallas_call(turn_margin_kernel, grid=(1,), in_specs=[SMEM, pl.BlockSpe...  3.9 us
    pallas_call x1, Pallas kernels, add_margins(): pl.pallas_call(add_margins_kernel, in_specs=[some, VMEM, VMEM], out_specs...  2.88 us
    pallas_call x1, Pallas kernels, turn_core(): pl.pallas_call(turn_core_kernel, in_specs=[VMEM], out_specs=[VMEM, VMEM],...  2.87 us
  transfers between devices with their start and end apart: 8, of which 0 were waited for; matrix products, arithmetic and copies ran while one was open for 0% of the time, Pallas kernels for 46%

profile of v4, /device:TPU:6, one launch (start us, length us, event | category | flops | bytes accessed | tf_op | source)
XLA Modules:
  0.0 85.4 jit_solution(15196877386653340847)
XLA Ops:
  1.3 3.9 %shard_map.85 = (bf16[39,80,128]{2,1,0:T(8,128)(2,1)}, bf16[39,80,128]{2,1,0:T(8,128)(2,1)}) custom-call(s32[1,1]{1,0:T(1,128)S(6)} %copy.11.tissue_ref, bf16[384,32,256]{2,1,0:T(8,128)(2,1)} %bitcast.12, bf16[384,32,256]{2,1,0:T(8,128)(2,1)} %bitcast.13), custom_call_target="tpu_custom_call" | custom-call | bytes 8388608 | tf_op jit(solution)/shard_map/pallas_call | solution.py:64
  5.2 1.9 %collective-permute-start = (bf16[39,80,128]{2,1,0:T(8,128)(2,1)}, bf16[39,80,128]{2,1,0:T(8,128)(2,1)}, u32[]{:S(2)}, u32[]{:S(2)}) collective-permute-start(bf16[39,80,128]{2,1,0:T(8,128)(2,1)} %get-tuple-element.16), channel_id=1, source_target_pairs={{0,1},{1,2},{2,3},{3,4},{4,5},{5,6},{6,7},{7,8},{8,9},{9,10},{10,1... | collective-permute-start | bytes 2396168 | tf_op jit(solution)/shard_map/ppermute | solution.py:579
  7.1 5.8 %collective-permute-start.1 = (bf16[39,80,128]{2,1,0:T(8,128)(2,1)}, bf16[39,80,128]{2,1,0:T(8,128)(2,1)}, u32[]{:S(2)}, u32[]{:S(2)}) collective-permute-start(bf16[39,80,128]{2,1,0:T(8,128)(2,1)} %get-tuple-element.17), channel_id=1, source_target_pairs={{1,0},{2,1},{3,2},{4,3},{5,4},{6,5},{7,6},{8,7},{9,8},{10,9},{11,1... | collective-permute-start | bytes 2396168 | tf_op jit(solution)/shard_map/ppermute | solution.py:579
  12.9 0.0 copy-start
  12.9 2.8 %copy-done = bf16[384,256,32]{1,2,0:T(8,128)(2,1)S(1)} copy-done((bf16[384,256,32]{1,2,0:T(8,128)(2,1)S(1)}, bf16[384,256,32]{1,2,0:T(8,128)(2,1)}, u32[]{:S(2)}) %copy-start) | copy-done | bytes 6291480
  15.7 0.0 slice-start
  15.7 2.9 %shard_map.86 = (bf16[65,80,128]{2,1,0:T(8,128)(2,1)}, bf16[65,80,128]{2,1,0:T(8,128)(2,1)}) custom-call(bf16[384,32,256]{2,1,0:T(8,128)(2,1)S(1)} %bitcast.14), custom_call_target="tpu_custom_call" | custom-call | bytes 12582912 | tf_op jit(solution)/shard_map/pallas_call | solution.py:90
  18.5 1.9 %collective-permute-start.2 = (bf16[65,80,128]{2,1,0:T(8,128)(2,1)}, bf16[65,80,128]{2,1,0:T(8,128)(2,1)S(1)}, u32[]{:S(2)}, u32[]{:S(2)}) collective-permute-start(bf16[65,80,128]{2,1,0:T(8,128)(2,1)} %get-tuple-element.18), channel_id=1, source_target_pairs={{0,1},{1,2},{2,3},{3,4},{4,5},{5,6},{6,7},{7,8},{8,9},{9,10},{10,1... | collective-permute-start | bytes 3993608 | tf_op jit(solution)/shard_map/ppermute | solution.py:579
  20.5 5.8 %collective-permute-start.3 = (bf16[65,80,128]{2,1,0:T(8,128)(2,1)}, bf16[65,80,128]{2,1,0:T(8,128)(2,1)}, u32[]{:S(2)}, u32[]{:S(2)}) collective-permute-start(bf16[65,80,128]{2,1,0:T(8,128)(2,1)} %get-tuple-element.19), channel_id=1, source_target_pairs={{1,0},{2,1},{3,2},{4,3},{5,4},{6,5},{7,6},{8,7},{9,8},{10,9},{11,1... | collective-permute-start | bytes 3993608 | tf_op jit(solution)/shard_map/ppermute | solution.py:579
  26.2 0.0 copy-done.5
  26.2 0.1 pad_add_fusion.where_ref
  26.3 0.0 collective-permute-done.mleft_ref.left_ref
  26.3 0.0 collective-permute-done.1.mright_ref.right_ref
  26.3 0.0 copy-done.2
  26.3 0.0 copy-done.3
  26.4 0.0 copy-start.1
  26.4 2.8 %copy-done.1 = bf16[384,256,32]{1,2,0:T(8,128)(2,1)S(1)} copy-done((bf16[384,256,32]{1,2,0:T(8,128)(2,1)S(1)}, bf16[384,256,32]{1,2,0:T(8,128)(2,1)}, u32[]{:S(2)}) %copy-start.1) | copy-done | bytes 6291480
  29.1 13.0 %shard_map.88 = (bf16[2304,128]{1,0:T(8,128)(2,1)S(1)}, bf16[2304,128]{1,0:T(8,128)(2,1)S(1)}, f32[2,128,128]{2,1,0:T(8,128)S(1)}) custom-call(s32[2]{0:T(128)S(1)} %pad_add_fusion.where_ref, s32[1,1]{1,0:T(1,128)S(6)} %copy.11.tissue_ref, bf16[384,32,256]{2,1,0:T(8,128)(2,1)S(1)} %bitcast.15, bf16[39,80,128]{2,1,0:T(8,128)(2,1)} %collective-permute-done.mleft_ref.left_ref, ...), custom_call_target="tpu_custom_call" | custom-call | flops 8589934592 | bytes 8388608 | tf_op jit(solution)/shard_map/pallas_call | solution.py:363
  42.1 3.5 %collective-permute-start.4 = (bf16[2304,128]{1,0:T(8,128)(2,1)S(1)}, bf16[2304,128]{1,0:T(8,128)(2,1)S(1)}, u32[]{:S(2)}, u32[]{:S(2)}) collective-permute-start(bf16[2304,128]{1,0:T(8,128)(2,1)S(1)} %get-tuple-element.22), channel_id=1, source_target_pairs={{0,16},{16,32},{32,48},{48,64},{64,80},{80,96},{96,112},{1,17},{17... | collective-permute-start | bytes 1769480 | tf_op jit(solution)/shard_map/ppermute | solution.py:579
  45.6 6.0 %collective-permute-start.5 = (bf16[2304,128]{1,0:T(8,128)(2,1)S(1)}, bf16[2304,128]{1,0:T(8,128)(2,1)S(1)}, u32[]{:S(2)}, u32[]{:S(2)}) collective-permute-start(bf16[2304,128]{1,0:T(8,128)(2,1)S(1)} %get-tuple-element.23), channel_id=1, source_target_pairs={{16,0},{32,16},{48,32},{64,48},{80,64},{96,80},{112,96},{17,1},{33... | collective-permute-start | bytes 1769480 | tf_op jit(solution)/shard_map/ppermute | solution.py:579
  51.6 0.0 collective-permute-done.2.left_ref
  51.6 0.0 collective-permute-done.3.right_ref
  51.7 20.6 %shard_map.87 = (f32[8192,128]{1,0:T(8,128)}, f32[2,128,128]{2,1,0:T(8,128)S(1)}) custom-call(s32[2]{0:T(128)S(1)} %pad_add_fusion.where_ref, s32[1,1]{1,0:T(1,128)S(6)} %copy.11.tissue_ref, bf16[384,32,256]{2,1,0:T(8,128)(2,1)S(1)} %bitcast.18, bf16[39,80,128]{2,1,0:T(8,128)(2,1)} %collective-permute-done.mleft_ref.left_ref, ...), custom_call_target="tpu_custom_call" | custom-call | flops 17179869184 | bytes 12582912 | tf_op jit(solution)/shard_map/pallas_call | solution.py:447
  72.3 0.0 collective-permute-done.4.above_ref
  72.3 0.0 collective-permute-done.5.below_ref
  72.3 1.4 %shard_map.89 = (f32[256,128]{1,0:T(8,128)}, f32[128,384]{1,0:T(8,128)S(1)}, f32[8,384]{1,0:T(8,128)S(1)}, f32[8,384]{1,0:T(8,128)S(1)}) custom-call(s32[2]{0:T(128)S(1)} %pad_add_fusion.where_ref, f32[2,128,128]{2,1,0:T(8,128)S(1)} %get-tuple-element.20.prob_ref, f32[2,128,128]{2,1,0:T(8,128)S(1)} %get-tuple-element.21.edge_ref, ...), custom_call_target="tpu_custom_call" | custom-call | bytes 1048576 | tf_op jit(solution)/shard_map/pallas_call | solution.py:494
  73.7 1.9 %collective-permute-start.6 = (f32[8,384]{1,0:T(8,128)S(1)}, f32[8,384]{1,0:T(8,128)S(1)}, u32[]{:S(2)}, u32[]{:S(2)}) collective-permute-start(f32[8,384]{1,0:T(8,128)S(1)} %get-tuple-element.27), channel_id=1, source_target_pairs={{0,1},{1,2},{2,3},{3,4},{4,5},{5,6},{6,7},{7,8},{8,9},{9,10},{10,1... | collective-permute-start | bytes 36872 | tf_op jit(solution)/shard_map/ppermute | solution.py:579
  75.6 5.8 %collective-permute-start.7 = (f32[8,384]{1,0:T(8,128)S(1)}, f32[8,384]{1,0:T(8,128)S(1)}, u32[]{:S(2)}, u32[]{:S(2)}) collective-permute-start(f32[8,384]{1,0:T(8,128)S(1)} %get-tuple-element.28), channel_id=1, source_target_pairs={{1,0},{2,1},{3,2},{4,3},{5,4},{6,5},{7,6},{8,7},{9,8},{10,9},{11,1... | collective-permute-start | bytes 36872 | tf_op jit(solution)/shard_map/ppermute | solution.py:579
  81.3 2.9 %shard_map.90 = f32[8192,128]{1,0:T(8,128)} custom-call(f32[8192,128]{1,0:T(8,128)} %get-tuple-element.25.rays_ref, bf16[2304,128]{1,0:T(8,128)(2,1)S(1)} %collective-permute-done.4.above_ref, bf16[2304,128]{1,0:T(8,128)(2,1)S(1)} %collective-permute-done.5.below_ref), custom_call_target="tpu_custom_call", output_to_operand_aliasing={{}: (0, {})} | custom-call | bytes 6291456 | tf_op jit(solution)/shard_map/pallas_call | solution.py:538
  84.2 0.0 collective-permute-done.6.west_ref
  84.2 0.0 collective-permute-done.7.east_ref
  84.3 1.1 %shard_map.91 = f32[256,128]{1,0:T(8,128)} custom-call(f32[128,384]{1,0:T(8,128)S(1)} %get-tuple-element.26.wide_ref, f32[8,384]{1,0:T(8,128)S(1)} %collective-permute-done.6.west_ref, f32[8,384]{1,0:T(8,128)S(1)} %collective-permute-done.7.east_ref), custom_call_target="tpu_custom_call" | custom-call | tf_op jit(solution)/shard_map/pallas_call | solution.py:566
  (10 shorter events, 0.0 us)
Async XLA Ops:
  5.2 21.1 %collective-permute-start = (bf16[39,80,128]{2,1,0:T(8,128)(2,1)}, bf16[39,80,128]{2,1,0:T(8,128)(2,1)}, u32[]{:S(2)}, u32[]{:S(2)}) collective-permute-start(bf16[39,80,128]{2,1,0:T(8,128)(2,1)} %get-tuple-element.16), channel_id=1, source_target_pairs={{0,1},{1,2},{2,3},{3,4},{4,5},{5,6},{6,7},{7,8},{8,9},{9,10},{10,1... | collective-permute-start | bytes 2396168 | tf_op jit(solution)/shard_map/ppermute | solution.py:579
  7.1 19.2 %collective-permute-start.1 = (bf16[39,80,128]{2,1,0:T(8,128)(2,1)}, bf16[39,80,128]{2,1,0:T(8,128)(2,1)}, u32[]{:S(2)}, u32[]{:S(2)}) collective-permute-start(bf16[39,80,128]{2,1,0:T(8,128)(2,1)} %get-tuple-element.17), channel_id=1, source_target_pairs={{1,0},{2,1},{3,2},{4,3},{5,4},{6,5},{7,6},{8,7},{9,8},{10,9},{11,1... | collective-permute-start | bytes 2396168 | tf_op jit(solution)/shard_map/ppermute | solution.py:579
  12.9 2.8 %copy-start = (bf16[384,256,32]{1,2,0:T(8,128)(2,1)S(1)}, bf16[384,256,32]{1,2,0:T(8,128)(2,1)}, u32[]{:S(2)}) copy-start(bf16[384,256,32]{1,2,0:T(8,128)(2,1)} %param.6) | copy-start | bytes 18874372
  15.6 10.6 %copy-start.5 = (f32[33]{0:T(128)S(1)}, f32[33]{0:T(128)}, u32[]{:S(2)}) copy-start(f32[33]{0:T(128)} %param.10) | copy-start | bytes 400
  15.6 10.7 %copy-start.2 = (bf16[3,3,32,128]{3,2,1,0:T(8,128)(2,1)S(1)}, bf16[3,3,32,128]{3,2,1,0:T(8,128)(2,1)}, u32[]{:S(2)}) copy-start(bf16[3,3,32,128]{3,2,1,0:T(8,128)(2,1)} %param.7) | copy-start | bytes 221188
  15.6 10.7 %copy-start.3 = (bf16[128,33]{0,1:T(8,128)(2,1)S(1)}, bf16[128,33]{0,1:T(8,128)(2,1)}, u32[]{:S(2)}) copy-start(bf16[128,33]{0,1:T(8,128)(2,1)} %param.9) | copy-start | bytes 25348
  15.6 10.7 %copy-start.4 = (f32[128]{0:T(128)S(1)}, f32[128]{0:T(128)}, u32[]{:S(2)}) copy-start(f32[128]{0:T(128)} %param.8) | copy-start | bytes 1540
  15.7 36.0 %slice-start = ((s8[6291456]{0:T(1024)(128)(4,1)}), s8[2097152]{0:T(1024)(128)(4,1)S(1)}, s32[]{:S(2)}) async-start(s8[6291456]{0:T(1024)(128)(4,1)} %bitcast.16), calls=%async_computation | async-start | bytes 4194304
  18.5 33.1 %collective-permute-start.2 = (bf16[65,80,128]{2,1,0:T(8,128)(2,1)}, bf16[65,80,128]{2,1,0:T(8,128)(2,1)S(1)}, u32[]{:S(2)}, u32[]{:S(2)}) collective-permute-start(bf16[65,80,128]{2,1,0:T(8,128)(2,1)} %get-tuple-element.18), channel_id=1, source_target_pairs={{0,1},{1,2},{2,3},{3,4},{4,5},{5,6},{6,7},{7,8},{8,9},{9,10},{10,1... | collective-permute-start | bytes 3993608 | tf_op jit(solution)/shard_map/ppermute | solution.py:579
  20.5 31.2 %collective-permute-start.3 = (bf16[65,80,128]{2,1,0:T(8,128)(2,1)}, bf16[65,80,128]{2,1,0:T(8,128)(2,1)}, u32[]{:S(2)}, u32[]{:S(2)}) collective-permute-start(bf16[65,80,128]{2,1,0:T(8,128)(2,1)} %get-tuple-element.19), channel_id=1, source_target_pairs={{1,0},{2,1},{3,2},{4,3},{5,4},{6,5},{7,6},{8,7},{9,8},{10,9},{11,1... | collective-permute-start | bytes 3993608 | tf_op jit(solution)/shard_map/ppermute | solution.py:579
  26.4 2.8 %copy-start.1 = (bf16[384,256,32]{1,2,0:T(8,128)(2,1)S(1)}, bf16[384,256,32]{1,2,0:T(8,128)(2,1)}, u32[]{:S(2)}) copy-start(bf16[384,256,32]{1,2,0:T(8,128)(2,1)} %param.6) | copy-start | bytes 18874372
  29.1 22.5 %slice-start.1 = ((s8[6291456]{0:T(1024)(128)(4,1)}), s8[4194304]{0:T(1024)(128)(4,1)S(1)}, s32[]{:S(2)}) async-start(s8[6291456]{0:T(1024)(128)(4,1)} %bitcast.16), calls=%async_computation.1 | async-start | bytes 8388608
  42.1 30.1 %collective-permute-start.4 = (bf16[2304,128]{1,0:T(8,128)(2,1)S(1)}, bf16[2304,128]{1,0:T(8,128)(2,1)S(1)}, u32[]{:S(2)}, u32[]{:S(2)}) collective-permute-start(bf16[2304,128]{1,0:T(8,128)(2,1)S(1)} %get-tuple-element.22), channel_id=1, source_target_pairs={{0,16},{16,32},{32,48},{48,64},{64,80},{80,96},{96,112},{1,17},{17... | collective-permute-start | bytes 1769480 | tf_op jit(solution)/shard_map/ppermute | solution.py:579
  45.6 26.6 %collective-permute-start.5 = (bf16[2304,128]{1,0:T(8,128)(2,1)S(1)}, bf16[2304,128]{1,0:T(8,128)(2,1)S(1)}, u32[]{:S(2)}, u32[]{:S(2)}) collective-permute-start(bf16[2304,128]{1,0:T(8,128)(2,1)S(1)} %get-tuple-element.23), channel_id=1, source_target_pairs={{16,0},{32,16},{48,32},{64,48},{80,64},{96,80},{112,96},{17,1},{33... | collective-permute-start | bytes 1769480 | tf_op jit(solution)/shard_map/ppermute | solution.py:579
  73.7 10.6 %collective-permute-start.6 = (f32[8,384]{1,0:T(8,128)S(1)}, f32[8,384]{1,0:T(8,128)S(1)}, u32[]{:S(2)}, u32[]{:S(2)}) collective-permute-start(f32[8,384]{1,0:T(8,128)S(1)} %get-tuple-element.27), channel_id=1, source_target_pairs={{0,1},{1,2},{2,3},{3,4},{4,5},{5,6},{6,7},{7,8},{8,9},{9,10},{10,1... | collective-permute-start | bytes 36872 | tf_op jit(solution)/shard_map/ppermute | solution.py:579
  75.6 8.7 %collective-permute-start.7 = (f32[8,384]{1,0:T(8,128)S(1)}, f32[8,384]{1,0:T(8,128)S(1)}, u32[]{:S(2)}, u32[]{:S(2)}) collective-permute-start(f32[8,384]{1,0:T(8,128)S(1)} %get-tuple-element.28), channel_id=1, source_target_pairs={{1,0},{2,1},{3,2},{4,3},{5,4},{6,5},{7,6},{8,7},{9,8},{10,9},{11,1... | collective-permute-start | bytes 36872 | tf_op jit(solution)/shard_map/ppermute | solution.py:579

commit v5 on v4

--- a/solution.py
+++ b/solution.py
@@ -71,7 +71,7 @@
         ],
         out_specs=[VMEM, VMEM],
         out_shape=[side, side],
-        compiler_params=pltpu.CompilerParams(vmem_limit_bytes=60 << 20),
+        compiler_params=pltpu.CompilerParams(vmem_limit_bytes=20 << 20),
         cost_estimate=pl.CostEstimate(flops=0, bytes_accessed=8 << 20, transcendentals=0),
     )(tissue, features, features)
 

time: 85.8 us -> 84.1 us (0.980)
  Pallas kernels: 45.7 us -> 43.8 us
    pallas_call x1, Pallas kernels: 3.9 us -> 2.01 us  [turn_margin(): pl.pallas_call(turn_margin_kernel, grid=(1,), in_specs=[SMEM, pl.BlockSpe...]
  transfers between devices with their start and end apart: 8 -> 8, of which waited for: 0 -> 0; matrix products, arithmetic and copies ran while one was open for 0% -> 0% of each run, Pallas kernels for 46% -> 47%
where the time goes in v5:
time: 84.1 us; the launch traced here: 83.6 us
  Pallas kernels  43.8 us (52%)
  starting transfers between devices  32.6 us (39%)
  local copies, waits for them, and re-layouts  5.6 us (7%)
  between operations  1.53 us (2%)
    ppermute x8, starting transfers between devices, shift(): return lax.ppermute(array, axis, pairs)  32.6 us
    pallas_call x1, Pallas kernels, core_outputs(): pl.pallas_call(core_kernel, grid=(1,), in_specs=[SMEM, SMEM, VMEM, flag,...  20.6 us
    pallas_call x1, Pallas kernels, margin_outputs(): pl.pallas_call(margin_kernel, in_specs=[SMEM, SMEM, HBM] + [VMEM] * 6, ou...  13 us
    unnamed x16, local copies, waits for them, and re-layouts  5.6 us
    pallas_call x1, Pallas kernels, add_margins(): pl.pallas_call(add_margins_kernel, in_specs=[some, VMEM, VMEM], out_specs...  2.88 us
    pallas_call x1, Pallas kernels, turn_core(): pl.pallas_call(turn_core_kernel, in_specs=[VMEM], out_specs=[VMEM, VMEM],...  2.87 us
    pallas_call x1, Pallas kernels, turn_margin(): pl.pallas_call(turn_margin_kernel, grid=(1,), in_specs=[SMEM, pl.BlockSpe...  2.01 us
  transfers between devices with their start and end apart: 8, of which 0 were waited for; matrix products, arithmetic and copies ran while one was open for 0% of the time, Pallas kernels for 47%

profile of v5, /device:TPU:6, one launch (start us, length us, event | category | flops | bytes accessed | tf_op | source)
XLA Modules:
  0.0 83.6 jit_solution(4613821672701603059)
XLA Ops:
  1.3 0.0 copy-start
  1.3 2.8 %copy-done = bf16[384,256,32]{1,2,0:T(8,128)(2,1)S(1)} copy-done((bf16[384,256,32]{1,2,0:T(8,128)(2,1)S(1)}, bf16[384,256,32]{1,2,0:T(8,128)(2,1)}, u32[]{:S(2)}) %copy-start) | copy-done | bytes 6291480
  4.1 2.0 %shard_map.85 = (bf16[39,80,128]{2,1,0:T(8,128)(2,1)}, bf16[39,80,128]{2,1,0:T(8,128)(2,1)}) custom-call(s32[1,1]{1,0:T(1,128)S(6)} %copy.11.tissue_ref, bf16[384,32,256]{2,1,0:T(8,128)(2,1)S(1)} %bitcast.12, bf16[384,32,256]{2,1,0:T(8,128)(2,1)S(1)} %bitcast.13), custom_call_target="tpu_custom_call" | custom-call | bytes 8388608 | tf_op jit(solution)/shard_map/pallas_call | solution.py:64
  6.1 1.9 %collective-permute-start = (bf16[39,80,128]{2,1,0:T(8,128)(2,1)}, bf16[39,80,128]{2,1,0:T(8,128)(2,1)}, u32[]{:S(2)}, u32[]{:S(2)}) collective-permute-start(bf16[39,80,128]{2,1,0:T(8,128)(2,1)} %get-tuple-element.16), channel_id=1, source_target_pairs={{0,1},{1,2},{2,3},{3,4},{4,5},{5,6},{6,7},{7,8},{8,9},{9,10},{10,1... | collective-permute-start | bytes 2396168 | tf_op jit(solution)/shard_map/ppermute | solution.py:579
  8.0 0.0 copy-start.5
  8.0 0.0 copy-start.2
  8.0 0.0 copy-start.3
  8.0 0.0 copy-start.4
  8.0 5.9 %collective-permute-start.1 = (bf16[39,80,128]{2,1,0:T(8,128)(2,1)}, bf16[39,80,128]{2,1,0:T(8,128)(2,1)}, u32[]{:S(2)}, u32[]{:S(2)}) collective-permute-start(bf16[39,80,128]{2,1,0:T(8,128)(2,1)} %get-tuple-element.17), channel_id=1, source_target_pairs={{1,0},{2,1},{3,2},{4,3},{5,4},{6,5},{7,6},{8,7},{9,8},{10,9},{11,1... | collective-permute-start | bytes 2396168 | tf_op jit(solution)/shard_map/ppermute | solution.py:579
  13.9 0.0 slice-start
  13.9 2.9 %shard_map.86 = (bf16[65,80,128]{2,1,0:T(8,128)(2,1)}, bf16[65,80,128]{2,1,0:T(8,128)(2,1)}) custom-call(bf16[384,32,256]{2,1,0:T(8,128)(2,1)S(1)} %bitcast.14), custom_call_target="tpu_custom_call" | custom-call | bytes 12582912 | tf_op jit(solution)/shard_map/pallas_call | solution.py:90
  16.8 1.9 %collective-permute-start.2 = (bf16[65,80,128]{2,1,0:T(8,128)(2,1)}, bf16[65,80,128]{2,1,0:T(8,128)(2,1)S(1)}, u32[]{:S(2)}, u32[]{:S(2)}) collective-permute-start(bf16[65,80,128]{2,1,0:T(8,128)(2,1)} %get-tuple-element.18), channel_id=1, source_target_pairs={{0,1},{1,2},{2,3},{3,4},{4,5},{5,6},{6,7},{7,8},{8,9},{9,10},{10,1... | collective-permute-start | bytes 3993608 | tf_op jit(solution)/shard_map/ppermute | solution.py:579
  18.7 5.8 %collective-permute-start.3 = (bf16[65,80,128]{2,1,0:T(8,128)(2,1)}, bf16[65,80,128]{2,1,0:T(8,128)(2,1)}, u32[]{:S(2)}, u32[]{:S(2)}) collective-permute-start(bf16[65,80,128]{2,1,0:T(8,128)(2,1)} %get-tuple-element.19), channel_id=1, source_target_pairs={{1,0},{2,1},{3,2},{4,3},{5,4},{6,5},{7,6},{8,7},{9,8},{10,9},{11,1... | collective-permute-start | bytes 3993608 | tf_op jit(solution)/shard_map/ppermute | solution.py:579
  24.5 0.1 pad_add_fusion.where_ref
  24.6 0.0 collective-permute-done.mleft_ref.left_ref
  24.6 0.0 collective-permute-done.1.mright_ref.right_ref
  24.6 0.0 copy-start.1
  24.6 2.8 %copy-done.1 = bf16[384,256,32]{1,2,0:T(8,128)(2,1)S(1)} copy-done((bf16[384,256,32]{1,2,0:T(8,128)(2,1)S(1)}, bf16[384,256,32]{1,2,0:T(8,128)(2,1)}, u32[]{:S(2)}) %copy-start.1) | copy-done | bytes 6291480
  27.4 13.0 %shard_map.88 = (bf16[2304,128]{1,0:T(8,128)(2,1)S(1)}, bf16[2304,128]{1,0:T(8,128)(2,1)S(1)}, f32[2,128,128]{2,1,0:T(8,128)S(1)}) custom-call(s32[2]{0:T(128)S(1)} %pad_add_fusion.where_ref, s32[1,1]{1,0:T(1,128)S(6)} %copy.11.tissue_ref, bf16[384,32,256]{2,1,0:T(8,128)(2,1)S(1)} %bitcast.15, bf16[39,80,128]{2,1,0:T(8,128)(2,1)} %collective-permute-done.mleft_ref.left_ref, ...), custom_call_target="tpu_custom_call" | custom-call | flops 8589934592 | bytes 8388608 | tf_op jit(solution)/shard_map/pallas_call | solution.py:363
  40.4 3.5 %collective-permute-start.4 = (bf16[2304,128]{1,0:T(8,128)(2,1)S(1)}, bf16[2304,128]{1,0:T(8,128)(2,1)S(1)}, u32[]{:S(2)}, u32[]{:S(2)}) collective-permute-start(bf16[2304,128]{1,0:T(8,128)(2,1)S(1)} %get-tuple-element.22), channel_id=1, source_target_pairs={{0,16},{16,32},{32,48},{48,64},{64,80},{80,96},{96,112},{1,17},{17... | collective-permute-start | bytes 1769480 | tf_op jit(solution)/shard_map/ppermute | solution.py:579
  43.9 6.0 %collective-permute-start.5 = (bf16[2304,128]{1,0:T(8,128)(2,1)S(1)}, bf16[2304,128]{1,0:T(8,128)(2,1)S(1)}, u32[]{:S(2)}, u32[]{:S(2)}) collective-permute-start(bf16[2304,128]{1,0:T(8,128)(2,1)S(1)} %get-tuple-element.23), channel_id=1, source_target_pairs={{16,0},{32,16},{48,32},{64,48},{80,64},{96,80},{112,96},{17,1},{33... | collective-permute-start | bytes 1769480 | tf_op jit(solution)/shard_map/ppermute | solution.py:579
  49.9 0.0 collective-permute-done.2.left_ref
  49.9 0.0 collective-permute-done.3.right_ref
  49.9 20.6 %shard_map.87 = (f32[8192,128]{1,0:T(8,128)}, f32[2,128,128]{2,1,0:T(8,128)S(1)}) custom-call(s32[2]{0:T(128)S(1)} %pad_add_fusion.where_ref, s32[1,1]{1,0:T(1,128)S(6)} %copy.11.tissue_ref, bf16[384,32,256]{2,1,0:T(8,128)(2,1)S(1)} %bitcast.18, bf16[39,80,128]{2,1,0:T(8,128)(2,1)} %collective-permute-done.mleft_ref.left_ref, ...), custom_call_target="tpu_custom_call" | custom-call | flops 17179869184 | bytes 12582912 | tf_op jit(solution)/shard_map/pallas_call | solution.py:447
  70.5 0.0 collective-permute-done.5.below_ref
  70.6 1.4 %shard_map.89 = (f32[256,128]{1,0:T(8,128)}, f32[128,384]{1,0:T(8,128)S(1)}, f32[8,384]{1,0:T(8,128)S(1)}, f32[8,384]{1,0:T(8,128)S(1)}) custom-call(s32[2]{0:T(128)S(1)} %pad_add_fusion.where_ref, f32[2,128,128]{2,1,0:T(8,128)S(1)} %get-tuple-element.20.prob_ref, f32[2,128,128]{2,1,0:T(8,128)S(1)} %get-tuple-element.21.edge_ref, ...), custom_call_target="tpu_custom_call" | custom-call | bytes 1048576 | tf_op jit(solution)/shard_map/pallas_call | solution.py:494
  72.0 1.9 %collective-permute-start.6 = (f32[8,384]{1,0:T(8,128)S(1)}, f32[8,384]{1,0:T(8,128)S(1)}, u32[]{:S(2)}, u32[]{:S(2)}) collective-permute-start(f32[8,384]{1,0:T(8,128)S(1)} %get-tuple-element.27), channel_id=1, source_target_pairs={{0,1},{1,2},{2,3},{3,4},{4,5},{5,6},{6,7},{7,8},{8,9},{9,10},{10,1... | collective-permute-start | bytes 36872 | tf_op jit(solution)/shard_map/ppermute | solution.py:579
  73.9 5.8 %collective-permute-start.7 = (f32[8,384]{1,0:T(8,128)S(1)}, f32[8,384]{1,0:T(8,128)S(1)}, u32[]{:S(2)}, u32[]{:S(2)}) collective-permute-start(f32[8,384]{1,0:T(8,128)S(1)} %get-tuple-element.28), channel_id=1, source_target_pairs={{1,0},{2,1},{3,2},{4,3},{5,4},{6,5},{7,6},{8,7},{9,8},{10,9},{11,1... | collective-permute-start | bytes 36872 | tf_op jit(solution)/shard_map/ppermute | solution.py:579
  79.6 2.9 %shard_map.90 = f32[8192,128]{1,0:T(8,128)} custom-call(f32[8192,128]{1,0:T(8,128)} %get-tuple-element.25.rays_ref, bf16[2304,128]{1,0:T(8,128)(2,1)S(1)} %collective-permute-done.4.above_ref, bf16[2304,128]{1,0:T(8,128)(2,1)S(1)} %collective-permute-done.5.below_ref), custom_call_target="tpu_custom_call", output_to_operand_aliasing={{}: (0, {})} | custom-call | bytes 6291456 | tf_op jit(solution)/shard_map/pallas_call | solution.py:538
  82.5 0.0 collective-permute-done.6.west_ref
  82.5 0.0 collective-permute-done.7.east_ref
  82.5 1.1 %shard_map.91 = f32[256,128]{1,0:T(8,128)} custom-call(f32[128,384]{1,0:T(8,128)S(1)} %get-tuple-element.26.wide_ref, f32[8,384]{1,0:T(8,128)S(1)} %collective-permute-done.6.west_ref, f32[8,384]{1,0:T(8,128)S(1)} %collective-permute-done.7.east_ref), custom_call_target="tpu_custom_call" | custom-call | tf_op jit(solution)/shard_map/pallas_call | solution.py:566
  (10 shorter events, 0.0 us)
Async XLA Ops:
  1.3 2.8 %copy-start = (bf16[384,256,32]{1,2,0:T(8,128)(2,1)S(1)}, bf16[384,256,32]{1,2,0:T(8,128)(2,1)}, u32[]{:S(2)}) copy-start(bf16[384,256,32]{1,2,0:T(8,128)(2,1)} %param.6) | copy-start | bytes 18874372
  6.1 18.5 %collective-permute-start = (bf16[39,80,128]{2,1,0:T(8,128)(2,1)}, bf16[39,80,128]{2,1,0:T(8,128)(2,1)}, u32[]{:S(2)}, u32[]{:S(2)}) collective-permute-start(bf16[39,80,128]{2,1,0:T(8,128)(2,1)} %get-tuple-element.16), channel_id=1, source_target_pairs={{0,1},{1,2},{2,3},{3,4},{4,5},{5,6},{6,7},{7,8},{8,9},{9,10},{10,1... | collective-permute-start | bytes 2396168 | tf_op jit(solution)/shard_map/ppermute | solution.py:579
  8.0 16.5 %copy-start.5 = (f32[33]{0:T(128)S(1)}, f32[33]{0:T(128)}, u32[]{:S(2)}) copy-start(f32[33]{0:T(128)} %param.10) | copy-start | bytes 400
  8.0 16.6 %copy-start.2 = (bf16[3,3,32,128]{3,2,1,0:T(8,128)(2,1)S(1)}, bf16[3,3,32,128]{3,2,1,0:T(8,128)(2,1)}, u32[]{:S(2)}) copy-start(bf16[3,3,32,128]{3,2,1,0:T(8,128)(2,1)} %param.7) | copy-start | bytes 221188
  8.0 16.6 %copy-start.3 = (bf16[128,33]{0,1:T(8,128)(2,1)S(1)}, bf16[128,33]{0,1:T(8,128)(2,1)}, u32[]{:S(2)}) copy-start(bf16[128,33]{0,1:T(8,128)(2,1)} %param.9) | copy-start | bytes 25348
  8.0 16.6 %copy-start.4 = (f32[128]{0:T(128)S(1)}, f32[128]{0:T(128)}, u32[]{:S(2)}) copy-start(f32[128]{0:T(128)} %param.8) | copy-start | bytes 1540
  8.0 16.6 %collective-permute-start.1 = (bf16[39,80,128]{2,1,0:T(8,128)(2,1)}, bf16[39,80,128]{2,1,0:T(8,128)(2,1)}, u32[]{:S(2)}, u32[]{:S(2)}) collective-permute-start(bf16[39,80,128]{2,1,0:T(8,128)(2,1)} %get-tuple-element.17), channel_id=1, source_target_pairs={{1,0},{2,1},{3,2},{4,3},{5,4},{6,5},{7,6},{8,7},{9,8},{10,9},{11,1... | collective-permute-start | bytes 2396168 | tf_op jit(solution)/shard_map/ppermute | solution.py:579
  13.9 36.0 %slice-start = ((s8[6291456]{0:T(1024)(128)(4,1)}), s8[2097152]{0:T(1024)(128)(4,1)S(1)}, s32[]{:S(2)}) async-start(s8[6291456]{0:T(1024)(128)(4,1)} %bitcast.16), calls=%async_computation | async-start | bytes 4194304
  16.8 33.1 %collective-permute-start.2 = (bf16[65,80,128]{2,1,0:T(8,128)(2,1)}, bf16[65,80,128]{2,1,0:T(8,128)(2,1)S(1)}, u32[]{:S(2)}, u32[]{:S(2)}) collective-permute-start(bf16[65,80,128]{2,1,0:T(8,128)(2,1)} %get-tuple-element.18), channel_id=1, source_target_pairs={{0,1},{1,2},{2,3},{3,4},{4,5},{5,6},{6,7},{7,8},{8,9},{9,10},{10,1... | collective-permute-start | bytes 3993608 | tf_op jit(solution)/shard_map/ppermute | solution.py:579
  18.7 31.2 %collective-permute-start.3 = (bf16[65,80,128]{2,1,0:T(8,128)(2,1)}, bf16[65,80,128]{2,1,0:T(8,128)(2,1)}, u32[]{:S(2)}, u32[]{:S(2)}) collective-permute-start(bf16[65,80,128]{2,1,0:T(8,128)(2,1)} %get-tuple-element.19), channel_id=1, source_target_pairs={{1,0},{2,1},{3,2},{4,3},{5,4},{6,5},{7,6},{8,7},{9,8},{10,9},{11,1... | collective-permute-start | bytes 3993608 | tf_op jit(solution)/shard_map/ppermute | solution.py:579
  24.6 2.8 %copy-start.1 = (bf16[384,256,32]{1,2,0:T(8,128)(2,1)S(1)}, bf16[384,256,32]{1,2,0:T(8,128)(2,1)}, u32[]{:S(2)}) copy-start(bf16[384,256,32]{1,2,0:T(8,128)(2,1)} %param.6) | copy-start | bytes 18874372
  27.4 22.5 %slice-start.1 = ((s8[6291456]{0:T(1024)(128)(4,1)}), s8[4194304]{0:T(1024)(128)(4,1)S(1)}, s32[]{:S(2)}) async-start(s8[6291456]{0:T(1024)(128)(4,1)} %bitcast.16), calls=%async_computation.1 | async-start | bytes 8388608
  40.4 30.1 %collective-permute-start.4 = (bf16[2304,128]{1,0:T(8,128)(2,1)S(1)}, bf16[2304,128]{1,0:T(8,128)(2,1)S(1)}, u32[]{:S(2)}, u32[]{:S(2)}) collective-permute-start(bf16[2304,128]{1,0:T(8,128)(2,1)S(1)} %get-tuple-element.22), channel_id=1, source_target_pairs={{0,16},{16,32},{32,48},{48,64},{64,80},{80,96},{96,112},{1,17},{17... | collective-permute-start | bytes 1769480 | tf_op jit(solution)/shard_map/ppermute | solution.py:579
  43.9 26.6 %collective-permute-start.5 = (bf16[2304,128]{1,0:T(8,128)(2,1)S(1)}, bf16[2304,128]{1,0:T(8,128)(2,1)S(1)}, u32[]{:S(2)}, u32[]{:S(2)}) collective-permute-start(bf16[2304,128]{1,0:T(8,128)(2,1)S(1)} %get-tuple-element.23), channel_id=1, source_target_pairs={{16,0},{32,16},{48,32},{64,48},{80,64},{96,80},{112,96},{17,1},{33... | collective-permute-start | bytes 1769480 | tf_op jit(solution)/shard_map/ppermute | solution.py:579
  72.0 10.6 %collective-permute-start.6 = (f32[8,384]{1,0:T(8,128)S(1)}, f32[8,384]{1,0:T(8,128)S(1)}, u32[]{:S(2)}, u32[]{:S(2)}) collective-permute-start(f32[8,384]{1,0:T(8,128)S(1)} %get-tuple-element.27), channel_id=1, source_target_pairs={{0,1},{1,2},{2,3},{3,4},{4,5},{5,6},{6,7},{7,8},{8,9},{9,10},{10,1... | collective-permute-start | bytes 36872 | tf_op jit(solution)/shard_map/ppermute | solution.py:579
  73.9 8.7 %collective-permute-start.7 = (f32[8,384]{1,0:T(8,128)S(1)}, f32[8,384]{1,0:T(8,128)S(1)}, u32[]{:S(2)}, u32[]{:S(2)}) collective-permute-start(f32[8,384]{1,0:T(8,128)S(1)} %get-tuple-element.28), channel_id=1, source_target_pairs={{1,0},{2,1},{3,2},{4,3},{5,4},{6,5},{7,6},{8,7},{9,8},{10,9},{11,1... | collective-permute-start | bytes 36872 | tf_op jit(solution)/shard_map/ppermute | solution.py:579
